TPU v7x, 32 devices: a whole 2x2x4 slice. The times are simulated.
32 devices in a mesh: dp: 8 (over z, x), blk: 4 (over y, core).
Axes of the slice: x: 2, y: 2, z: 4, core: 2. Of those that a mesh axis runs over, the one named last changes fastest.
Arguments:
- hidden_input: bfloat16 [24, 512, 512], P('dp', 'blk'), may hold values from -6 to 6
- lengths: int32 [24], P('dp'), may hold values from 64 to 512, as said below
- key_mask: int32 [24, 512], P('dp', 'blk'), may hold values 0 or 1
- query_weight: bfloat16 [512, 512], replicated, may hold values from -0.25 to 0.25
- query_offset: bfloat16 [512], replicated, may hold values from -3 to 3
- key_weight: bfloat16 [512, 512], replicated, may hold values from -0.25 to 0.25
- value_weight: bfloat16 [512, 512], replicated, may hold values from -0.25 to 0.25
- value_offset: bfloat16 [512], replicated, may hold values from -0.29882812 to 0.29882812
- output_weight: bfloat16 [512, 512], replicated, may hold values from -2 to 2
- output_offset: bfloat16 [512], replicated, may hold values from -3 to 3
- mixer_gain: bfloat16 [512], replicated, may hold values from 0.5 to 1.5
- mixer_shift: bfloat16 [512], replicated, may hold values from -3 to 3
- up_weight: bfloat16 [512, 2048], replicated, may hold values from -0.25 to 0.25
- up_offset: bfloat16 [2048], replicated, may hold values from -3 to 3
- down_weight: bfloat16 [2048, 512], replicated, may hold values from -0.125 to 0.125
- down_offset: bfloat16 [512], replicated, may hold values from -3 to 3
- final_gain: bfloat16 [512], replicated, may hold values from 0.5 to 1.5
- final_shift: bfloat16 [512], replicated, may hold values from -3 to 3
- cotangent: bfloat16 [24, 512, 512], P('dp', 'blk'), may hold values from -6 to 6
Outputs:
- hidden_output: bfloat16 [24, 512, 512], P('dp', 'blk')
- input_gradient: bfloat16 [24, 512, 512], P('dp', 'blk')
- query_weight_gradient: float32 [512, 512], replicated
- query_offset_gradient: float32 [512], replicated
- key_weight_gradient: float32 [512, 512], replicated
- value_weight_gradient: float32 [512, 512], replicated
- value_offset_gradient: float32 [512], replicated
- output_weight_gradient: float32 [512, 512], replicated
- output_offset_gradient: float32 [512], replicated
- mixer_gain_gradient: float32 [512], replicated
- mixer_shift_gradient: float32 [512], replicated
- up_weight_gradient: float32 [512, 2048], replicated
- up_offset_gradient: float32 [2048], replicated
- down_weight_gradient: float32 [2048, 512], replicated
- down_offset_gradient: float32 [512], replicated
- final_gain_gradient: float32 [512], replicated
- final_shift_gradient: float32 [512], replicated
Inputs may be any that keep to these rules, and one draw needn't show every extreme that they name: `lengths`: in each aligned group of 3 consecutive sequences at least one, drawn from the seed, has length 512.
All inputs are finite; a program needn't handle non-finite values. No bound on the sum of `key_mask` on one device may be relied on, other than what follows from the above.
Results may differ from a plain program's by a relative error of at most 0.019.
Values may be sent and summed in bfloat16 or wider, within the bound.
A program may use at most 128 MiB of HBM per device.

v0:
```python
import jax
import jax.numpy as jnp
from jax import lax
from jax.sharding import PartitionSpec as P

HEADS = 8
HEAD = 64


EPSILON = 1e-06


def project(inputs, weight):
    return jnp.einsum("sqd,df->sqf", inputs, weight, preferred_element_type=jnp.float32)


def project_back(upstream, weight):
    return jnp.einsum("sqf,df->sqd", upstream, weight, preferred_element_type=jnp.float32)


def weight_term(inputs, upstream):
    return jnp.einsum("sqd,sqf->df", inputs, upstream, preferred_element_type=jnp.float32)


def totals(values):
    return jnp.sum(values.astype(jnp.float32), axis=(0, 1))


def normalize(values, gain, shift):
    center = values - jnp.mean(values, axis=-1, keepdims=True)
    inverse = lax.rsqrt(jnp.mean(center * center, axis=-1, keepdims=True) + EPSILON)
    scaled = center * inverse
    return (scaled * gain + shift, scaled, inverse)


def norm_back(upstream, scaled, inverse, gain):
    inner = upstream * gain
    return inverse * (
        inner
        - jnp.mean(inner, axis=-1, keepdims=True)
        - scaled * jnp.mean(inner * scaled, axis=-1, keepdims=True)
    )


def on_device(
    hidden_input,
    lengths,
    key_mask,
    query_weight,
    query_offset,
    key_weight,
    value_weight,
    value_offset,
    output_weight,
    output_offset,
    mixer_gain,
    mixer_shift,
    up_weight,
    up_offset,
    down_weight,
    down_offset,
    final_gain,
    final_shift,
    cotangent,
):
    seqs, rows, width = hidden_input.shape
    factor_scale = HEAD ** (-0.5)
    positions = lax.axis_index("blk") * rows + jnp.arange(rows, dtype=jnp.int32)
    usable = ((key_mask == 1) & (positions[None, :] < lengths[:, None])).astype(jnp.int32)
    inputs_wide = hidden_input.astype(jnp.float32)
    queries = (project(hidden_input, query_weight) + query_offset.astype(jnp.float32)).astype(
        jnp.bfloat16
    )
    keys = project(hidden_input, key_weight).astype(jnp.bfloat16)
    values = (project(hidden_input, value_weight) + value_offset.astype(jnp.float32)).astype(
        jnp.bfloat16
    )
    query_heads = queries.reshape(seqs, rows, HEADS, HEAD)

    def score_block(key_piece, usable_piece):
        count = key_piece.shape[1]
        key_heads = key_piece.reshape(seqs, count, HEADS, HEAD)
        scores = (
            jnp.einsum(
                "sqhd,skhd->sqhk", query_heads, key_heads, preferred_element_type=jnp.float32
            )
            * factor_scale
        )
        places = jnp.arange(count, dtype=jnp.int32)
        allowed = (usable_piece[:, None, None, :] == 1) | (
            places[None, None, None, :] == positions[None, :, None, None]
        )
        return jnp.where(allowed, scores, -1000000000.0)

    running = jnp.full((seqs, rows, HEADS), -1e30, jnp.float32)
    key_piece = lax.all_gather(keys, "blk", axis=1, tiled=True)
    value_piece = lax.all_gather(values, "blk", axis=1, tiled=True)
    usable_piece = lax.all_gather(usable, "blk", axis=1, tiled=True)
    scores_part = score_block(key_piece, usable_piece)
    newmax = jnp.maximum(running, jnp.max(scores_part, axis=-1))
    weights = jnp.exp(scores_part - newmax[..., None])
    mass = jnp.sum(weights, axis=-1)
    value_heads = value_piece.reshape(seqs, value_piece.shape[1], HEADS, HEAD)
    accum = jnp.einsum(
        "sqhk,skhd->sqhd",
        weights.astype(jnp.bfloat16),
        value_heads,
        preferred_element_type=jnp.float32,
    )
    running, mass, accum = (newmax, mass, accum)
    logsum = running + jnp.log(mass)
    attended = accum / mass[..., None]
    mixed = attended.reshape(seqs, rows, width).astype(jnp.bfloat16)
    branch = project(mixed, output_weight) + output_offset.astype(jnp.float32)
    mixer_wide = mixer_gain.astype(jnp.float32)
    normed, mixer_scaled, mixer_inverse = normalize(
        inputs_wide + branch, mixer_wide, mixer_shift.astype(jnp.float32)
    )
    normed_low = normed.astype(jnp.bfloat16)
    inner = project(normed_low, up_weight) + up_offset.astype(jnp.float32)
    activated, gelu_back = jax.vjp(lambda given: jax.nn.gelu(given, approximate=False), inner)
    activated_low = activated.astype(jnp.bfloat16)
    result = project(activated_low, down_weight) + down_offset.astype(jnp.float32)
    final_wide = final_gain.astype(jnp.float32)
    output_wide, final_scaled, final_inverse = normalize(
        normed + result, final_wide, final_shift.astype(jnp.float32)
    )
    hidden_output = output_wide.astype(jnp.bfloat16)
    upstream = cotangent.astype(jnp.float32)
    final_shift_part = jnp.sum(upstream, axis=(0, 1))
    final_gain_part = jnp.sum(upstream * final_scaled, axis=(0, 1))
    second_grad = norm_back(upstream, final_scaled, final_inverse, final_wide)
    result_grad = second_grad.astype(jnp.bfloat16)
    down_weight_part = weight_term(activated_low, result_grad)
    down_offset_part = totals(result_grad)
    inner_grad = gelu_back(project_back(result_grad, down_weight))[0].astype(jnp.bfloat16)
    up_weight_part = weight_term(normed_low, inner_grad)
    up_offset_part = totals(inner_grad)
    normed_grad = second_grad + project_back(inner_grad, up_weight)
    mixer_shift_part = jnp.sum(normed_grad, axis=(0, 1))
    mixer_gain_part = jnp.sum(normed_grad * mixer_scaled, axis=(0, 1))
    first_grad = norm_back(normed_grad, mixer_scaled, mixer_inverse, mixer_wide)
    branch_grad = first_grad.astype(jnp.bfloat16)
    output_weight_part = weight_term(mixed, branch_grad)
    output_offset_part = totals(branch_grad)
    mixed_grad = project_back(branch_grad, output_weight).astype(jnp.bfloat16)
    mixed_heads = mixed_grad.reshape(seqs, rows, HEADS, HEAD)
    key_all, value_all, usable_all = (
        lax.all_gather(keys, "blk", axis=1, tiled=True),
        lax.all_gather(values, "blk", axis=1, tiled=True),
        lax.all_gather(usable, "blk", axis=1, tiled=True),
    )
    scores = score_block(key_all, usable_all)
    probs = jnp.exp(scores - logsum[..., None])
    probs_low = probs.astype(jnp.bfloat16)
    length_all = key_all.shape[1]
    key_heads_all = key_all.reshape(seqs, length_all, HEADS, HEAD)
    value_heads_all = value_all.reshape(seqs, length_all, HEADS, HEAD)
    prob_grad = jnp.einsum(
        "sqhd,skhd->sqhk", mixed_heads, value_heads_all, preferred_element_type=jnp.float32
    )
    centre = jnp.sum(probs * prob_grad, axis=-1)
    score_grad = (probs * (prob_grad - centre[..., None])).astype(jnp.bfloat16)
    query_grad = (
        (
            jnp.einsum(
                "sqhk,skhd->sqhd", score_grad, key_heads_all, preferred_element_type=jnp.float32
            )
            * factor_scale
        )
        .reshape(seqs, rows, width)
        .astype(jnp.bfloat16)
    )
    key_term = (
        jnp.einsum("sqhk,sqhd->skhd", score_grad, query_heads, preferred_element_type=jnp.float32)
        * factor_scale
    )
    value_term = jnp.einsum(
        "sqhk,sqhd->skhd", probs_low, mixed_heads, preferred_element_type=jnp.float32
    )
    joined = jnp.concatenate(
        [key_term.reshape(seqs, length_all, width), value_term.reshape(seqs, length_all, width)],
        axis=-1,
    )
    returned = lax.psum_scatter(
        joined.astype(jnp.bfloat16), "blk", scatter_dimension=1, tiled=True
    ).astype(jnp.float32)
    key_grad = returned[:, :, :width].astype(jnp.bfloat16)
    value_grad = returned[:, :, width:].astype(jnp.bfloat16)
    query_weight_part = weight_term(hidden_input, query_grad)
    query_offset_part = totals(query_grad)
    key_weight_part = weight_term(hidden_input, key_grad)
    value_weight_part = weight_term(hidden_input, value_grad)
    value_offset_part = totals(value_grad)
    input_wide = (
        first_grad
        + project_back(query_grad, query_weight)
        + project_back(key_grad, key_weight)
        + project_back(value_grad, value_weight)
    )
    input_gradient = input_wide.astype(jnp.bfloat16)
    (
        query_weight_sum,
        query_offset_sum,
        key_weight_sum,
        value_weight_sum,
        value_offset_sum,
        output_weight_sum,
        output_offset_sum,
        mixer_gain_sum,
        mixer_shift_sum,
        up_weight_sum,
        up_offset_sum,
        down_weight_sum,
        down_offset_sum,
        final_gain_sum,
        final_shift_sum,
    ) = lax.psum(
        (
            query_weight_part,
            query_offset_part,
            key_weight_part,
            value_weight_part,
            value_offset_part,
            output_weight_part,
            output_offset_part,
            mixer_gain_part,
            mixer_shift_part,
            up_weight_part,
            up_offset_part,
            down_weight_part,
            down_offset_part,
            final_gain_part,
            final_shift_part,
        ),
        ("dp", "blk"),
    )
    return (
        hidden_output,
        input_gradient,
        query_weight_sum,
        query_offset_sum,
        key_weight_sum,
        value_weight_sum,
        value_offset_sum,
        output_weight_sum,
        output_offset_sum,
        mixer_gain_sum,
        mixer_shift_sum,
        up_weight_sum,
        up_offset_sum,
        down_weight_sum,
        down_offset_sum,
        final_gain_sum,
        final_shift_sum,
    )


def solution(mesh):
    in_specs = (
        P("dp", "blk", None),
        P("dp"),
        P("dp", "blk"),
        P(),
        P(),
        P(),
        P(),
        P(),
        P(),
        P(),
        P(),
        P(),
        P(),
        P(),
        P(),
        P(),
        P(),
        P(),
        P("dp", "blk", None),
    )
    out_specs = (
        P("dp", "blk", None),
        P("dp", "blk", None),
        P(),
        P(),
        P(),
        P(),
        P(),
        P(),
        P(),
        P(),
        P(),
        P(),
        P(),
        P(),
        P(),
        P(),
        P(),
    )
    return jax.shard_map(
        on_device, mesh=mesh, in_specs=in_specs, out_specs=out_specs, check_vma=False
    )
```

profile of v0, /device:TPU:5, one launch (start us, length us, event | category | flops | bytes accessed | tf_op | source)
XLA Modules:
  0.0 412.7 jit_solution(7878987979435068747)
XLA Ops:
  7.4 2.4 convolution_convert_fusion.1
  10.6 2.3 fusion.40
  13.0 1.1 fusion.41
  14.1 1.2 copy.61
  15.5 5.6 %all_gather.13 = s32[3,512]{1,0:T(4,128)S(1)} all-gather(s32[3,128]{1,0:T(4,128)S(1)} %and_convert_fusion.2), channel_id=1, replica_groups=mesh['dp'=8,'blk'=4] {'blk'}, dimensions={1}, use_global_device_ids=true | all-gather | bytes 7680 | tf_op jit(solution)/shard_map/all_gather | solution.py:98
  21.5 9.0 %all-gather.5.cloned.1.call-done = bf16[3,512,512]{2,1,0:T(8,128)(2,1)} async-done(((bf16[3,128,512]{2,1,0:T(8,128)(2,1)}), bf16[3,512,512]{2,1,0:T(8,128)(2,1)}) %all-gather.5.cloned.1.call-update) | async-done | bytes 1572880 | tf_op jit(solution)/shard_map/all_gather | solution.py:96
  30.4 2.6 copy.60
  33.0 2.8 fusion.79
  35.9 0.9 fusion.3
  36.8 1.7 copy-done.2
  38.6 13.7 %all-gather.3.cloned.1.call-done = bf16[3,512,512]{2,1,0:T(8,128)(2,1)} async-done(((bf16[3,128,512]{2,1,0:T(8,128)(2,1)}), bf16[3,512,512]{2,1,0:T(8,128)(2,1)}) %all-gather.3.cloned.1.call-update) | async-done | bytes 1572880 | tf_op jit(solution)/shard_map/all_gather | solution.py:97
  52.3 2.6 copy.59
  54.9 4.6 %fusion.47 = bf16[3,128,8,64]{1,3,2,0:T(8,128)(2,1)S(1)} fusion(bf16[3,512,8,64]{1,3,2,0:T(8,128)(2,1)} %bitcast.125, f32[3,128,8,512]{1,3,2,0:T(8,128)} %copy-done.2, f32[3,128,8]{1,2,0:T(8,128)S(1)} %broadcast_maximum_fusion, f32[3,128,8]{1,2,0:T(8,128)S(1)} %fusion.3), kind=kOutput, calls=%fused_computation.75 | convolution fusion | flops 204865536 | bytes 8282112 | tf_op jit(solution)/shard_map/sqhk,skhd->sqhd/dot_general | solution.py:104
  60.2 1.8 fusion.58
  62.1 7.3 %multiply_convert_fusion.1 = (bf16[3,128,2048]{2,1,0:T(8,128)(2,1)S(1)}, f32[3,128,2048]{2,1,0:T(8,128)S(1)}) fusion(f32[3,128,2048]{2,1,0:T(8,128)S(1)} %get-tuple-element.87, u8[128,2048]{1,0:T(8,128)(4,1)S(1)} %get-tuple-element.52, u8[128,2048]{1,0:T(8,128)(4,1)S(1)} %get-tuple-element.51), kind=kLoop, calls=%fused_computation.27 | loop fusion | flops 55050240 | bytes 8388608 | tf_op jit(solution)/shard_map/convert_element_type | solution.py:122
  69.4 1.1 fusion.81
  71.2 1.1 convert_reduce_fusion.2
  72.3 1.9 convert_reduce_fusion
  74.3 1.4 multiply_reduce_fusion
  76.8 1.1 convolution_convert_fusion
  77.9 1.2 copy.64
  79.1 7.0 %fusion = (f32[3,128,8]{1,2,0:T(8,128)S(1)}, f32[3,8,512,128]{3,2,1,0:T(8,128)}) fusion(f32[3,128,8,512]{1,3,2,0:T(8,128)} %copy-done.2, f32[3,128,8]{1,2,0:T(8,128)S(1)} %log_add_fusion, bf16[3,512,8,64]{1,3,2,0:T(8,128)(2,1)S(1)} %bitcast.126, bf16[3,128,8,64]{1,3,2,0:T(8,128)(2,1)S(1)} %bitcast.135), kind=kOutput, calls=%fused_computation.2 | convolution fusion | flops 206042112 | bytes 14573568 | tf_op jit(solution)/shard_map/sqhd,skhd->sqhk/dot_general | solution.py:159
  86.1 4.0 fusion.24
  90.1 1.6 copy.70
  91.7 6.1 %fusion.2 = bf16[3,128,8,512]{1,3,2,0:T(8,128)(2,1)S(1)} fusion(f32[3,8,512,128]{3,2,1,0:T(8,128)} %get-tuple-element.92, f32[3,128,8,512]{1,3,2,0:T(8,128)} %copy-done.2, f32[3,128,8]{1,2,0:T(8,128)S(1)} %get-tuple-element.91, f32[3,128,8]{1,2,0:T(8,128)S(1)} %log_add_fusion), kind=kLoop, calls=%fused_computation.4 | loop fusion | flops 6291456 | bytes 15753216 | tf_op jit(solution)/shard_map/convert_element_type | solution.py:163
  97.8 1.7 copy-done.3
  99.5 2.4 multiply_convert_fusion
  101.9 2.6 copy.69
  104.5 3.6 pad_maximum_fusion
  108.3 0.7 copy-done.15
  109.0 2.4 convolution_bitcast_fusion.2
  111.4 2.8 convert_reduce_fusion.5
  114.3 1.4 convolution_bitcast_fusion.5
  115.7 3.3 convolution_bitcast_fusion
  119.0 3.4 convolution_bitcast_fusion.1
  122.4 23.5 %reduce-scatter.2.cloned.1.call-done = bf16[3,128,1024]{2,1,0:T(8,128)(2,1)} async-done(((bf16[3,512,1024]{2,1,0:T(8,128)(2,1)}), bf16[3,128,1024]{2,1,0:T(8,128)(2,1)}) %reduce-scatter.2.cloned.1.call-update) | async-done | bytes 786448 | tf_op jit(solution)/shard_map/reduce_scatter | solution.py:185
  145.9 2.4 convolution_bitcast_fusion.4
  148.3 2.4 convolution_bitcast_fusion.3
  150.9 1.9 convolution_add_fusion.3
  152.9 42.8 %all-reduce = (f32[512]{0:T(512)}, f32[512]{0:T(512)}, f32[512]{0:T(512)}, f32[512]{0:T(512)}, f32[512]{0:T(512)}, /*index=5*/f32[2048]{0:T(1024)}, f32[512]{0:T(512)}, f32[512]{0:T(512)}, f32[512]{0:T(512)}) all-reduce(f32[512]{0:T(512)S(1)} %reduce_sum.184, ...), channel_id=1, replica_groups=mesh['dp'=8,'blk'=4] {'dp','blk'}, use_global_device_ids=true, to_apply=%region_14.15 | all-reduce | flops 6144 | bytes 49152 | tf_op jit(solution)/shard_map/psum | solution.py:218
  196.1 2.2 fusion.42
  198.3 193.4 %all-reduce.4.cloned.1.call-done = (f32[512,512]{0,1:T(8,128)}, f32[512,512]{0,1:T(8,128)}, f32[512,512]{0,1:T(8,128)}, f32[512,512]{1,0:T(8,128)}, f32[512,2048]{1,0:T(8,128)}, /*index=5*/f32[2048,512]{1,0:T(8,128)}) async-done(((f32[512,512]{0,1:T(8,128)}, f32[512,512]{0,1:T(8,128)}, f32[512,512]{0,1:T(8,128)}, f32[512,512]{1,0:T(8,128)}, f32[512,2048]{1,0:T(8,128)}, /*index=5*/f32[2048,512]{1,0:T(8,128)}), ...) | async-done | bytes 12582928 | tf_op jit(solution)/shard_map/psum | solution.py:218
  391.8 2.7 copy.75
  394.5 2.5 copy.76
  397.0 1.3 copy.77
  398.3 1.0 copy.94
  399.3 4.8 %copy.95 = f32[512,2048]{1,0:T(8,128)} copy(f32[512,2048]{1,0:T(8,128)} %get-tuple-element.110) | data formatting | bytes 8388608
  404.1 2.0 copy.96
  (114 shorter events, 4.8 us)
Async XLA Ops:
  7.2 53.0 %copy-start = (bf16[512,2048]{1,0:T(8,128)(2,1)S(1)}, bf16[512,2048]{1,0:T(8,128)(2,1)}, u32[]{:S(2)}) copy-start(bf16[512,2048]{1,0:T(8,128)(2,1)} %param.31) | copy-start | bytes 6291460
  7.2 5.7 %copy-start.6 = (bf16[3,128,512]{2,1,0:T(8,128)(2,1)S(1)}, bf16[3,128,512]{2,1,0:T(8,128)(2,1)}, u32[]{:S(2)}) copy-start(bf16[3,128,512]{2,1,0:T(8,128)(2,1)} %param.19) | copy-start | bytes 1179652
  7.2 5.7 %copy-start.30 = (bf16[512]{0:T(512)(128)(2,1)S(1)}, bf16[512]{0:T(512)(128)(2,1)}, u32[]{:S(2)}) copy-start(bf16[512]{0:T(512)(128)(2,1)} %param.23) | copy-start | bytes 3076
  7.2 5.7 %copy-start.27 = (bf16[512,512]{1,0:T(8,128)(2,1)S(1)}, bf16[512,512]{1,0:T(8,128)(2,1)}, u32[]{:S(2)}) copy-start(bf16[512,512]{1,0:T(8,128)(2,1)} %param.22) | copy-start | bytes 1572868
  7.2 6.8 %copy-start.31 = (bf16[512]{0:T(512)(128)(2,1)S(1)}, bf16[512]{0:T(512)(128)(2,1)}, u32[]{:S(2)}) copy-start(bf16[512]{0:T(512)(128)(2,1)} %param.34) | copy-start | bytes 3076
  7.3 6.8 %copy-start.28 = (bf16[2048]{0:T(1024)(128)(2,1)S(1)}, bf16[2048]{0:T(1024)(128)(2,1)}, u32[]{:S(2)}) copy-start(bf16[2048]{0:T(1024)(128)(2,1)} %param.32) | copy-start | bytes 12292
  7.3 6.8 %copy-start.32 = (bf16[512]{0:T(512)(128)(2,1)S(1)}, bf16[512]{0:T(512)(128)(2,1)}, u32[]{:S(2)}) copy-start(bf16[512]{0:T(512)(128)(2,1)} %param.28) | copy-start | bytes 3076
  7.3 8.1 %copy-start.33 = (bf16[512]{0:T(512)(128)(2,1)S(1)}, bf16[512]{0:T(512)(128)(2,1)}, u32[]{:S(2)}) copy-start(bf16[512]{0:T(512)(128)(2,1)} %param.30) | copy-start | bytes 3076
  7.3 8.1 %copy-start.34 = (bf16[512]{0:T(512)(128)(2,1)S(1)}, bf16[512]{0:T(512)(128)(2,1)}, u32[]{:S(2)}) copy-start(bf16[512]{0:T(512)(128)(2,1)} %param.29) | copy-start | bytes 3076
  7.3 8.1 %copy-start.35 = (bf16[512]{0:T(512)(128)(2,1)S(1)}, bf16[512]{0:T(512)(128)(2,1)}, u32[]{:S(2)}) copy-start(bf16[512]{0:T(512)(128)(2,1)} %param.35) | copy-start | bytes 3076
  7.3 8.1 %copy-start.36 = (bf16[512]{0:T(512)(128)(2,1)S(1)}, bf16[512]{0:T(512)(128)(2,1)}, u32[]{:S(2)}) copy-start(bf16[512]{0:T(512)(128)(2,1)} %param.36) | copy-start | bytes 3076
  7.3 8.1 %copy-start.29 = (s32[3,128]{1,0:T(4,128)S(1)}, s32[3,128]{1,0:T(4,128)}, u32[]{:S(2)}) copy-start(s32[3,128]{1,0:T(4,128)} %param.21) | copy-start | bytes 4612
  7.3 8.1 %copy-start.37 = (s32[3]{0:T(128)S(1)}, s32[3]{0:T(128)}, u32[]{:S(2)}) copy-start(s32[3]{0:T(128)} %param.20) | copy-start | bytes 40
  7.3 23.1 %all-gather.5.cloned.1.call-start = ((), (), s32[]{:S(2)}) async-start(), calls=%async_computation.2 | async-start | bytes 1966080 | tf_op jit(solution)/shard_map/all_gather | solution.py:96
  9.8 42.4 %all-gather.3.cloned.1.call-start = ((), (), s32[]{:S(2)}) async-start(), calls=%async_computation.1 | async-start | bytes 1966080 | tf_op jit(solution)/shard_map/all_gather | solution.py:97
  12.9 133.1 %reduce-scatter.2.cloned.1.call-start = ((), (), s32[]{:S(2)}) async-start(), calls=%async_computation.3 | async-start | bytes 3932160 | tf_op jit(solution)/shard_map/reduce_scatter | solution.py:185
  15.3 20.5 %copy-start.12 = (bf16[3,128,512]{1,2,0:T(8,128)(2,1)}, bf16[3,128,512]{1,2,0:T(8,128)(2,1)S(1)}, u32[]{:S(2)}) copy-start(bf16[3,128,512]{1,2,0:T(8,128)(2,1)S(1)} %copy.61) | copy-start | bytes 1179652
  35.9 2.7 copy-start.2
  54.9 4.6 %copy-start.19 = (bf16[512,512]{1,0:T(8,128)(2,1)S(1)}, bf16[512,512]{1,0:T(8,128)(2,1)}, u32[]{:S(2)}) copy-start(bf16[512,512]{1,0:T(8,128)(2,1)} %param.27) | copy-start | bytes 1572868
  59.5 2.6 copy-start.14
  62.1 7.3 %copy-start.38 = (bf16[2048,512]{1,0:T(8,128)(2,1)S(1)}, bf16[2048,512]{1,0:T(8,128)(2,1)}, u32[]{:S(2)}) copy-start(bf16[2048,512]{1,0:T(8,128)(2,1)} %param.33) | copy-start | bytes 6291460
  69.4 1.1 copy-start.7
  69.4 1.4 copy-start.22
  72.3 1.9 copy-start.23
  74.2 1.4 copy-start.20
  75.7 0.9 copy-start.17
  75.7 3.5 copy-start.5
  76.0 0.7 copy-start.16
  91.7 7.8 %copy-start.13 = (bf16[3,128,512]{1,2,0:T(8,128)(2,1)S(1)}, bf16[3,128,512]{1,2,0:T(8,128)(2,1)}, u32[]{:S(2)}) copy-start(bf16[3,128,512]{1,2,0:T(8,128)(2,1)} %copy-done.12) | copy-start | bytes 1179652
  97.8 1.7 copy-start.3
  99.5 5.0 %copy-start.9 = (bf16[3,512,512]{2,1,0:T(8,128)(2,1)S(1)}, bf16[3,512,512]{2,1,0:T(8,128)(2,1)}, u32[]{:S(2)}) copy-start(bf16[3,512,512]{2,1,0:T(8,128)(2,1)} %copy.70) | copy-start | bytes 4718596
  108.0 1.0 copy-start.15
  108.0 3.4 copy-start.4
  108.1 283.7 %all-reduce.4.cloned.1.call-start = ((), (), s32[]{:S(2)}) async-start(), calls=%async_computation.4 | async-start | bytes 25165824 | tf_op jit(solution)/shard_map/psum | solution.py:218
  111.4 4.2 %copy-start.8 = (bf16[3,128,2048]{2,1,0:T(8,128)(2,1)S(1)}, bf16[3,128,2048]{2,1,0:T(8,128)(2,1)}, u32[]{:S(2)}) copy-start(bf16[3,128,2048]{2,1,0:T(8,128)(2,1)} %copy-done.7) | copy-start | bytes 4718596
  111.4 4.2 %copy-start.24 = (bf16[3,128,512]{2,1,0:T(8,128)(2,1)S(1)}, bf16[3,128,512]{2,1,0:T(8,128)(2,1)}, u32[]{:S(2)}) copy-start(bf16[3,128,512]{2,1,0:T(8,128)(2,1)} %copy-done.23) | copy-start | bytes 1179652
  115.7 3.3 copy-start.21
  150.8 2.0 copy-start.10
  150.8 44.9 %copy-start.18 = (bf16[512,512]{1,0:T(8,128)(2,1)S(1)}, bf16[512,512]{1,0:T(8,128)(2,1)}, u32[]{:S(2)}) copy-start(bf16[512,512]{1,0:T(8,128)(2,1)} %param.24) | copy-start | bytes 1572868
  391.8 5.2 %copy-start.26 = (f32[512,512]{0,1:T(8,128)S(1)}, f32[512,512]{0,1:T(8,128)}, u32[]{:S(2)}) copy-start(f32[512,512]{0,1:T(8,128)} %get-tuple-element.72) | copy-start | bytes 3145732
  391.8 6.5 %copy-start.25 = (f32[512,512]{1,0:T(8,128)S(1)}, f32[512,512]{1,0:T(8,128)}, u32[]{:S(2)}) copy-start(f32[512,512]{1,0:T(8,128)} %get-tuple-element.106) | copy-start | bytes 3145732
  399.3 4.9 %copy-start.11 = (f32[2048,512]{1,0:T(8,128)S(1)}, f32[2048,512]{1,0:T(8,128)}, u32[]{:S(2)}) copy-start(f32[2048,512]{1,0:T(8,128)} %get-tuple-element.112) | copy-start | bytes 12582916
  399.3 6.9 %copy-start.1 = (bf16[512,2048]{1,0:T(8,128)(2,1)S(1)}, bf16[512,2048]{1,0:T(8,128)(2,1)}, u32[]{:S(2)}) copy-start(bf16[512,2048]{1,0:T(8,128)(2,1)} %param.31) | copy-start | bytes 6291460
Sparse Core Ops, SparseCore 0:
  10.3 20.0 all-gather.4
  32.6 19.6 all-gather.2
  108.2 37.6 reduce-scatter.1
  154.5 237.2 all-reduce.3
where the time goes:
time: 416 us; the launch traced here: 413 us
  waiting for transfers between devices  240 us (58%)
  matrix products  57.2 us (14%)
  blocking collectives  48.4 us (12%)
  local copies, waits for them, and re-layouts  31.1 us (7%)
  other arithmetic  21.5 us (5%)
  between operations  14.4 us (3%)
    psum x1, waiting for transfers between devices, on_device(): lax.psum((query_weight_part, query_offset_part, key_weight_part, value_we...  193 us
    psum x1, blocking collectives, on_device(): lax.psum((query_weight_part, query_offset_part, key_weight_part, value_we...  42.8 us
    reduce_scatter x1, waiting for transfers between devices, on_device(): lax.psum_scatter(joined.astype(jnp.bfloat16), 'blk', scatter_dimension=1,...  23.5 us
    unnamed x84, local copies, waits for them, and re-layouts  19.3 us
    dot_general x6, matrix products, weight_term(): jnp.einsum('sqd,sqf->df', inputs, upstream, preferred_element_type=jnp.fl...  15.4 us
    all_gather x1, waiting for transfers between devices, on_device(): value_piece = lax.all_gather(values, 'blk', axis=1, tiled=True)  13.7 us
    dot_general x6, matrix products, project(): jnp.einsum('sqd,df->sqf', inputs, weight, preferred_element_type=jnp.floa...  9.24 us
    dot_general x6, matrix products, project_back(): jnp.einsum('sqf,df->sqd', upstream, weight, preferred_element_type=jnp.fl...  8.96 us
  transfers between devices with their start and end apart: 4, of which 4 were waited for; matrix products, arithmetic and copies ran while one was open for 7% of the time, Pallas kernels for 0%

commit v1 on v0

--- a/solution.py
+++ b/solution.py
@@ -1,7 +1,14 @@
+import functools
+
 import jax
 import jax.numpy as jnp
 from jax import lax
+from jax.experimental import pallas as pl
+from jax.experimental.pallas import tpu as pltpu
 from jax.sharding import PartitionSpec as P
+
+MESH = pl.DeviceIdType.MESH
+ROWS = 16
 
 HEADS = 8
 HEAD = 64
@@ -42,7 +49,220 @@
     )
 
 
+def bits_of(sizes):
+    found = {}
+    for axis, size in sizes.items():
+        steps = []
+        step = 1
+        while step < size:
+            steps.append((axis, step))
+            step *= 2
+        found[axis] = steps
+    return found
+
+
+def orders_of(sizes):
+    bits = bits_of(sizes)
+    blk, dp = bits["blk"], bits["dp"]
+    return (
+        blk[:1] + dp[:1] + blk[1:] + dp[1:],
+        blk + dp,
+        blk[:1] + dp[1:] + dp[:1] + blk[1:],
+    )
+
+
+def partner_of(bit):
+    axis, step = bit
+    index = lax.axis_index(axis)
+    side = lax.rem(lax.div(index, step), 2)
+    return side, {axis: index + step - 2 * step * side}
+
+
+def greet(bits):
+    barrier = pltpu.get_barrier_semaphore()
+    for bit in bits:
+        pl.semaphore_signal(barrier, inc=1, device_id=partner_of(bit)[1], device_id_type=MESH)
+    pl.semaphore_wait(barrier, len(bits))
+
+
+def rows_at(ref, start, count):
+    if not isinstance(start, int):
+        start = pl.multiple_of(start, ROWS)
+    return ref.at[pl.ds(start, count)]
+
+
+def plan_of(rows, order):
+    plan = []
+    size = rows
+    for bit in order:
+        split = (size // 2) % ROWS == 0
+        size = size // 2 if split else size
+        plan.append((bit, split, size))
+    return plan
+
+
+def landing_rows(rows, order):
+    return sum(size for _, _, size in plan_of(rows, order))
+
+
+def add_rows(first, first_at, second, second_at, out, out_at, count):
+    chunk = 64 if count % 64 == 0 else (32 if count % 32 == 0 else 16)
+
+    def body(step, carry):
+        shift = step * chunk
+        at = lambda start: pl.ds(pl.multiple_of(start + shift, ROWS), chunk)
+        total = first[at(first_at)].astype(jnp.float32) + second[at(second_at)].astype(jnp.float32)
+        out[at(out_at)] = total.astype(out.dtype)
+        return carry
+
+    lax.fori_loop(0, count // chunk, body, 0)
+
+
+def reduce_rows(work, land, out, sends, receives, base, rows, land_at, sem_at, order):
+    plan = plan_of(rows, order)
+    start, size = base, rows
+    pending, trail = [], []
+    for level, (bit, split, count) in enumerate(plan):
+        side, peer = partner_of(bit)
+        keep = start + side * count if split else start
+        give = start + (1 - side) * count if split else start
+        copy = pltpu.make_async_remote_copy(
+            src_ref=rows_at(work, give, count),
+            dst_ref=rows_at(land, land_at, count),
+            send_sem=sends.at[sem_at],
+            recv_sem=receives.at[sem_at],
+            device_id=peer,
+            device_id_type=MESH,
+        )
+        copy.start()
+        yield
+        copy.wait_recv()
+        if split:
+            pending.append(copy)
+        else:
+            copy.wait_send()
+        target = out if level == len(plan) - 1 else work
+        add_rows(work, keep, land, land_at, target, keep, count)
+        land_at += count
+        sem_at += 1
+        if split:
+            trail.append((peer, start, keep, count))
+        start = keep
+    for peer, parent, mine, count in reversed(trail):
+        copy = pltpu.make_async_remote_copy(
+            src_ref=rows_at(out, mine, count),
+            dst_ref=rows_at(out, mine, count),
+            send_sem=sends.at[sem_at],
+            recv_sem=receives.at[sem_at],
+            device_id=peer,
+            device_id_type=MESH,
+        )
+        copy.start()
+        yield
+        copy.wait_recv()
+        pending.append(copy)
+        sem_at += 1
+    for copy in pending:
+        copy.wait_send()
+
+
+def reduce_whole(steps, land, sends, receives, sem_at, order):
+    for level, bit in enumerate(order):
+        copy = pltpu.make_async_remote_copy(
+            src_ref=steps.at[level],
+            dst_ref=land.at[level],
+            send_sem=sends.at[sem_at + level],
+            recv_sem=receives.at[sem_at + level],
+            device_id=partner_of(bit)[1],
+            device_id_type=MESH,
+        )
+        copy.start()
+        yield
+        copy.wait()
+        steps[level + 1] = steps[level] + land[level]
+
+
+def interleave(running):
+    running = list(running)
+    while running:
+        kept = []
+        for item in running:
+            if next(item, True) is None:
+                kept.append(item)
+        running = kept
+
+
+GROUP_ROWS = 1024
+
+
+def sum_kernel(orders, grad_in, vec_in, grad_out, vec_out, work, land, out, steps, vec_land, sends, receives, local):
+    greet(sorted(set(orders[0])))
+    count = grad_in.shape[0] // GROUP_ROWS
+    loads = []
+    for group in range(count):
+        span = pl.ds(group * GROUP_ROWS, GROUP_ROWS)
+        load = pltpu.make_async_copy(grad_in.at[span], work.at[span], local.at[group])
+        load.start()
+        loads.append(load)
+    running = []
+    land_at = sem_at = 0
+    steps[0] = vec_in[...]
+    running.append(reduce_whole(steps, vec_land, sends, receives, 0, orders[1]))
+    sem_at += len(orders[1])
+    for group in range(count):
+        order = orders[group % 3]
+        running.append(
+            reduce_rows(work, land, out, sends, receives, group * GROUP_ROWS, GROUP_ROWS, land_at, sem_at, order)
+        )
+        land_at += landing_rows(GROUP_ROWS, order)
+        sem_at += 2 * len(order)
+    for load in loads:
+        load.wait()
+    interleave(running)
+    vec_out[...] = steps[len(orders[0])]
+    stores = []
+    for group in range(count):
+        span = pl.ds(group * GROUP_ROWS, GROUP_ROWS)
+        store = pltpu.make_async_copy(out.at[span], grad_out.at[span], local.at[group])
+        store.start()
+        stores.append(store)
+    for store in stores:
+        store.wait()
+
+
+def sum_all(grads, vecs, sizes):
+    orders = orders_of(sizes)
+    levels = len(orders[0])
+    rows, width = grads.shape
+    count = rows // GROUP_ROWS
+    land_total = sum(landing_rows(GROUP_ROWS, orders[group % 3]) for group in range(count))
+    sems = levels + 2 * levels * count
+    return pl.pallas_call(
+        functools.partial(sum_kernel, orders),
+        out_shape=(
+            jax.ShapeDtypeStruct(grads.shape, grads.dtype),
+            jax.ShapeDtypeStruct(vecs.shape, vecs.dtype),
+        ),
+        in_specs=[pl.BlockSpec(memory_space=pl.ANY), pl.BlockSpec(memory_space=pltpu.VMEM)],
+        out_specs=(pl.BlockSpec(memory_space=pl.ANY), pl.BlockSpec(memory_space=pltpu.VMEM)),
+        scratch_shapes=[
+            pltpu.VMEM((rows, width), jnp.bfloat16),
+            pltpu.VMEM((land_total, width), jnp.bfloat16),
+            pltpu.VMEM((rows, width), jnp.bfloat16),
+            pltpu.VMEM((levels + 1,) + vecs.shape, jnp.float32),
+            pltpu.VMEM((levels,) + vecs.shape, jnp.float32),
+            pltpu.SemaphoreType.DMA((sems,)),
+            pltpu.SemaphoreType.DMA((sems,)),
+            pltpu.SemaphoreType.DMA((count,)),
+        ],
+        compiler_params=pltpu.CompilerParams(
+            collective_id=0, has_side_effects=True, vmem_limit_bytes=48 * 1024 * 1024
+        ),
+    )(grads, vecs)
+
+
 def on_device(
+    sizes,
     hidden_input,
     lengths,
     key_mask,
@@ -199,42 +419,47 @@
         + project_back(value_grad, value_weight)
     )
     input_gradient = input_wide.astype(jnp.bfloat16)
+    low = lambda value: value.astype(jnp.bfloat16)
+    cut = lambda value: [low(value[:, at : at + width]) for at in range(0, value.shape[1], width)]
+    hidden = up_weight_part.shape[1]
+    grads = jnp.concatenate(
+        [low(down_weight_part)]
+        + cut(up_weight_part)
+        + [low(output_weight_part), low(query_weight_part), low(key_weight_part), low(value_weight_part)],
+        axis=0,
+    )
+    vecs = jnp.concatenate(
+        [
+            query_offset_part,
+            value_offset_part,
+            output_offset_part,
+            mixer_gain_part,
+            mixer_shift_part,
+            down_offset_part,
+            final_gain_part,
+            final_shift_part,
+            up_offset_part,
+            jnp.zeros((4 * width,), jnp.float32),
+        ]
+    ).reshape(-1, width)
+    grad_sums, vec_sums = sum_all(grads, vecs, sizes)
+    wide = lambda at, count: grad_sums[at : at + count].astype(jnp.float32)
+    down_weight_sum = wide(0, hidden)
+    up_weight_sum = jnp.concatenate([wide(hidden + at, width) for at in range(0, hidden, width)], axis=1)
+    output_weight_sum, query_weight_sum, key_weight_sum, value_weight_sum = (
+        wide(2 * hidden + at * width, width) for at in range(4)
+    )
     (
-        query_weight_sum,
         query_offset_sum,
-        key_weight_sum,
-        value_weight_sum,
         value_offset_sum,
-        output_weight_sum,
         output_offset_sum,
         mixer_gain_sum,
         mixer_shift_sum,
-        up_weight_sum,
-        up_offset_sum,
-        down_weight_sum,
         down_offset_sum,
         final_gain_sum,
         final_shift_sum,
-    ) = lax.psum(
-        (
-            query_weight_part,
-            query_offset_part,
-            key_weight_part,
-            value_weight_part,
-            value_offset_part,
-            output_weight_part,
-            output_offset_part,
-            mixer_gain_part,
-            mixer_shift_part,
-            up_weight_part,
-            up_offset_part,
-            down_weight_part,
-            down_offset_part,
-            final_gain_part,
-            final_shift_part,
-        ),
-        ("dp", "blk"),
-    )
+    ) = (vec_sums[at] for at in range(8))
+    up_offset_sum = vec_sums[8:12].reshape(-1)
     return (
         hidden_output,
         input_gradient,
@@ -298,5 +523,5 @@
         P(),
     )
     return jax.shard_map(
-        on_device, mesh=mesh, in_specs=in_specs, out_specs=out_specs, check_vma=False
-    )
+        functools.partial(on_device, dict(mesh.shape)), mesh=mesh, in_specs=in_specs, out_specs=out_specs, check_vma=False
+    )

time: 416 us -> 252 us (0.61)
  waiting for transfers between devices: 240 us -> 43.3 us
  Pallas kernels: 0 us -> 77.6 us
  blocking collectives: 48.4 us -> 5.62 us
  other arithmetic: 21.5 us -> 33.8 us
  local copies, waits for them, and re-layouts: 31.1 us -> 22.1 us
  matrix products: 57.2 us -> 52.9 us
    psum x1 -> x0, waiting for transfers between devices: 193 us -> none  [on_device(): lax.psum((query_weight_part, query_offset_part, key_weight_part, value_we...]
    pallas_call x0 -> x1, Pallas kernels: none -> 77.6 us  [sum_all(): pl.pallas_call(functools.partial(sum_kernel, orders), out_shape=(jax.Shap...]
    psum x1 -> x0, blocking collectives: 42.8 us -> none  [on_device(): lax.psum((query_weight_part, query_offset_part, key_weight_part, value_we...]
    unnamed x84 -> x95, local copies, waits for them, and re-layouts: 19.3 us -> 9.67 us
    slice x0 -> x1, other arithmetic: none -> 4.5 us  [on_device(): wide = lambda at, count: grad_sums[at:at + count].astype(jnp.float32)]
    convert_element_type x0 -> x1, other arithmetic: none -> 4.2 us  [on_device(): wide = lambda at, count: grad_sums[at:at + count].astype(jnp.float32)]
  transfers between devices with their start and end apart: 4 -> 3, of which waited for: 4 -> 3; matrix products, arithmetic and copies ran while one was open for 7% -> 11% of each run, Pallas kernels for 0% -> 0%
where the time goes in v1:
time: 252 us; the launch traced here: 250 us
  Pallas kernels  77.6 us (31%)
  matrix products  52.9 us (21%)
  waiting for transfers between devices  43.3 us (17%)
  other arithmetic  33.8 us (13%)
  local copies, waits for them, and re-layouts  22.1 us (9%)
  between operations  14.5 us (6%)
  blocking collectives  5.62 us (2%)
    pallas_call x1, Pallas kernels, sum_all(): pl.pallas_call(functools.partial(sum_kernel, orders), out_shape=(jax.Shap...  77.6 us
    reduce_scatter x1, waiting for transfers between devices, on_device(): lax.psum_scatter(joined.astype(jnp.bfloat16), 'blk', scatter_dimension=1,...  20.6 us
    all_gather x1, waiting for transfers between devices, on_device(): value_piece = lax.all_gather(values, 'blk', axis=1, tiled=True)  13.7 us
    dot_general x6, matrix products, weight_term(): jnp.einsum('sqd,sqf->df', inputs, upstream, preferred_element_type=jnp.fl...  12.7 us
    unnamed x95, local copies, waits for them, and re-layouts  9.67 us
    dot_general x6, matrix products, project(): jnp.einsum('sqd,df->sqf', inputs, weight, preferred_element_type=jnp.floa...  9.25 us
    all_gather x1, waiting for transfers between devices, on_device(): key_piece = lax.all_gather(keys, 'blk', axis=1, tiled=True)  8.96 us
    dot_general x6, matrix products, project_back(): jnp.einsum('sqf,df->sqd', upstream, weight, preferred_element_type=jnp.fl...  7.43 us
  transfers between devices with their start and end apart: 3, of which 3 were waited for; matrix products, arithmetic and copies ran while one was open for 11% of the time, Pallas kernels for 0%

profile of v1, /device:TPU:5, one launch (start us, length us, event | category | flops | bytes accessed | tf_op | source)
XLA Modules:
  0.0 250.0 jit_solution(14174282336107472637)
XLA Ops:
  7.4 2.4 convolution_convert_fusion.1
  10.6 2.3 fusion.46
  13.0 1.1 fusion.47
  14.1 1.2 copy.60
  15.5 5.6 %all_gather.13 = s32[3,512]{1,0:T(4,128)S(1)} all-gather(s32[3,128]{1,0:T(4,128)S(1)} %and_convert_fusion.2), channel_id=1, replica_groups=mesh['dp'=8,'blk'=4] {'blk'}, dimensions={1}, use_global_device_ids=true | all-gather | bytes 7680 | tf_op jit(solution)/shard_map/all_gather | solution.py:318
  21.5 9.0 %all-gather.5.cloned.1.call-done = bf16[3,512,512]{2,1,0:T(8,128)(2,1)} async-done(((bf16[3,128,512]{2,1,0:T(8,128)(2,1)}), bf16[3,512,512]{2,1,0:T(8,128)(2,1)}) %all-gather.5.cloned.1.call-update) | async-done | bytes 1572880 | tf_op jit(solution)/shard_map/all_gather | solution.py:316
  30.4 2.6 %copy.59 = bf16[3,512,512]{1,2,0:T(8,128)(2,1)} copy(bf16[3,512,512]{2,1,0:T(8,128)(2,1)} %all-gather.5.cloned.1.call-done) | data formatting | bytes 3145728 | tf_op jit(solution)/shard_map/all_gather | solution.py:316
  33.1 2.8 %fusion.93 = (f32[3,128,8]{1,2,0:T(8,128)S(1)}, f32[3,128,8,512]{1,3,2,0:T(8,128)S(1)}) fusion(bf16[3,512,8,64]{1,3,2,0:T(8,128)(2,1)} %bitcast.164, bf16[3,128,8,64]{1,3,2,0:T(8,128)(2,1)S(1)} %bitcast.172, pred[3,128,512]{1,2,0:T(8,128)(4,1)S(1)} %broadcast_or_fusion), kind=kOutput, calls=%fused_computation.164 | convolution fusion | flops 206042112 | bytes 8466432 | tf_op jit(solution)/shard_map/sqhd,skhd->sqhk/dot_general | solution.py:304
  35.9 0.9 fusion.3
  36.9 1.7 copy-done.2
  38.6 13.7 %all-gather.3.cloned.1.call-done = bf16[3,512,512]{2,1,0:T(8,128)(2,1)} async-done(((bf16[3,128,512]{2,1,0:T(8,128)(2,1)}), bf16[3,512,512]{2,1,0:T(8,128)(2,1)}) %all-gather.3.cloned.1.call-update) | async-done | bytes 1572880 | tf_op jit(solution)/shard_map/all_gather | solution.py:317
  52.3 2.6 %copy.58 = bf16[3,512,512]{1,2,0:T(8,128)(2,1)} copy(bf16[3,512,512]{2,1,0:T(8,128)(2,1)} %all-gather.3.cloned.1.call-done) | data formatting | bytes 3145728 | tf_op jit(solution)/shard_map/all_gather | solution.py:317
  54.9 4.6 %fusion.59 = bf16[3,128,8,64]{1,3,2,0:T(8,128)(2,1)S(1)} fusion(bf16[3,512,8,64]{1,3,2,0:T(8,128)(2,1)} %bitcast.166, f32[3,128,8,512]{1,3,2,0:T(8,128)} %copy-done.2, f32[3,128,8]{1,2,0:T(8,128)S(1)} %broadcast_maximum_fusion, f32[3,128,8]{1,2,0:T(8,128)S(1)} %fusion.3), kind=kOutput, calls=%fused_computation.89 | convolution fusion | flops 204865536 | bytes 8282112 | tf_op jit(solution)/shard_map/sqhk,skhd->sqhd/dot_general | solution.py:324
  60.3 1.8 fusion.70
  62.1 7.3 %multiply_convert_fusion.1 = (bf16[3,128,2048]{2,1,0:T(8,128)(2,1)S(1)}, f32[3,128,2048]{2,1,0:T(8,128)S(1)}) fusion(f32[3,128,2048]{2,1,0:T(8,128)S(1)} %get-tuple-element.58, u8[128,2048]{1,0:T(8,128)(4,1)S(1)} %get-tuple-element.22, u8[128,2048]{1,0:T(8,128)(4,1)S(1)} %get-tuple-element.21), kind=kLoop, calls=%fused_computation.27 | loop fusion | flops 55050240 | bytes 8388608 | tf_op jit(solution)/shard_map/convert_element_type | solution.py:342
  69.4 1.1 fusion.95
  71.3 1.1 convert_reduce_fusion.2
  72.4 1.9 convert_reduce_fusion
  74.3 1.4 multiply_reduce_fusion
  76.8 1.1 convolution_convert_fusion
  77.9 1.2 copy.63
  79.2 7.0 %fusion = (f32[3,128,8]{1,2,0:T(8,128)S(1)}, f32[3,8,512,128]{3,2,1,0:T(8,128)}) fusion(f32[3,128,8,512]{1,3,2,0:T(8,128)} %copy-done.2, f32[3,128,8]{1,2,0:T(8,128)S(1)} %log_add_fusion, bf16[3,512,8,64]{1,3,2,0:T(8,128)(2,1)S(1)} %bitcast.167, bf16[3,128,8,64]{1,3,2,0:T(8,128)(2,1)S(1)} %bitcast.174), kind=kOutput, calls=%fused_computation.2 | convolution fusion | flops 206042112 | bytes 14573568 | tf_op jit(solution)/shard_map/sqhd,skhd->sqhk/dot_general | solution.py:379
  86.2 4.0 %fusion.25 = bf16[3,8,64,512]{3,2,1,0:T(8,128)(2,1)S(1)} fusion(bf16[3,128,8,64]{1,3,2,0:T(8,128)(2,1)S(1)} %bitcast.175, f32[3,128,8,512]{1,3,2,0:T(8,128)} %copy-done.2, f32[3,128,8]{1,2,0:T(8,128)S(1)} %log_add_fusion), kind=kOutput, calls=%fused_computation.51 | convolution fusion | flops 205258752 | bytes 8269824 | tf_op jit(solution)/shard_map/sqhk,sqhd->skhd/dot_general | solution.py:398
  90.2 1.6 copy.69
  91.7 6.1 %fusion.2 = bf16[3,128,8,512]{1,3,2,0:T(8,128)(2,1)S(1)} fusion(f32[3,8,512,128]{3,2,1,0:T(8,128)} %get-tuple-element.63, f32[3,128,8,512]{1,3,2,0:T(8,128)} %copy-done.2, f32[3,128,8]{1,2,0:T(8,128)S(1)} %get-tuple-element.62, f32[3,128,8]{1,2,0:T(8,128)S(1)} %log_add_fusion), kind=kLoop, calls=%fused_computation.4 | loop fusion | flops 6291456 | bytes 15753216 | tf_op jit(solution)/shard_map/convert_element_type | solution.py:383
  97.8 1.7 copy-done.3
  99.5 2.4 multiply_convert_fusion
  101.8 2.6 %copy.68 = bf16[3,512,512]{2,1,0:T(8,128)(2,1)} copy(bf16[3,512,512]{1,2,0:T(8,128)(2,1)} %bitcast.169) | data formatting | bytes 3145728 | tf_op jit(solution)/shard_map/reshape | solution.py:402
  104.4 3.6 %pad_maximum_fusion = bf16[3,512,1024]{2,1,0:T(8,128)(2,1)} fusion(bf16[3,512,512]{2,1,0:T(8,128)(2,1)S(1)} %copy-done.6, bf16[3,512,512]{2,1,0:T(8,128)(2,1)} %copy.68), kind=kLoop, calls=%fused_computation.22 | loop fusion | flops 6291456 | bytes 6291456 | tf_op jit(solution)/shard_map/concatenate | solution.py:401
  108.0 1.4 copy-done.4
  109.4 2.7 %convert_reduce_fusion.5 = (f32[8,64]{1,0:T(8,128)S(1)}, bf16[3,8,64,128]{3,2,1,0:T(8,128)(2,1)S(1)}) fusion(bf16[3,512,8,64]{1,3,2,0:T(8,128)(2,1)S(1)} %bitcast.165, bf16[3,128,8,512]{1,3,2,0:T(8,128)(2,1)} %copy-done.3), kind=kOutput, calls=%fused_computation.101 | convolution fusion | flops 202112512 | bytes 5113856 | tf_op jit(solution)/shard_map/sqhk,skhd->sqhd/dot_general | solution.py:386
  112.2 4.2 %fusion.18 = bf16[6144,512]{1,0:T(8,128)(2,1)} fusion(bf16[3,128,2048]{2,1,0:T(8,128)(2,1)} %copy-done.18, bf16[3,128,512]{2,1,0:T(8,128)(2,1)S(1)} %copy-done.26), kind=kOutput, calls=%fused_computation.42 | convolution fusion | flops 806354944 | bytes 4063232 | tf_op jit(solution)/shard_map/sqd,sqf->df/dot_general | solution.py:29
  116.4 1.4 bitcast_convert_fusion
  117.9 0.8 slice_dynamic-update-slice_fusion.3
  118.7 0.9 slice_dynamic-update-slice_fusion.2
  120.4 0.9 slice_dynamic-update-slice_fusion
  121.2 1.2 fusion.30
  122.5 1.3 fusion.55
  123.8 1.5 convolution_add_fusion.3
  125.3 20.6 %reduce-scatter.2.cloned.1.call-done = bf16[3,128,1024]{2,1,0:T(8,128)(2,1)} async-done(((bf16[3,512,1024]{2,1,0:T(8,128)(2,1)}), bf16[3,128,1024]{2,1,0:T(8,128)(2,1)}) %reduce-scatter.2.cloned.1.call-update) | async-done | bytes 786448 | tf_op jit(solution)/shard_map/reduce_scatter | solution.py:405
  145.9 1.1 convert_reduce_fusion.4
  147.1 2.3 fusion.53
  149.4 2.3 fusion.51.grad_in
  151.6 77.6 %shard_map.314 = (bf16[6144,512]{1,0:T(8,128)(2,1)}, f32[16,512]{1,0:T(8,128)S(1)}) custom-call(bf16[6144,512]{1,0:T(8,128)(2,1)} %fusion.51.grad_in, f32[16,512]{1,0:T(8,128)S(1)} %reshape.174.vec_in), custom_call_target="tpu_custom_call" | custom-call | tf_op jit(solution)/shard_map/pallas_call | solution.py:240
  229.9 4.5 %fusion.91 = (bf16[512,512]{1,0:T(8,128)(2,1)S(1)}, bf16[512,512]{1,0:T(8,128)(2,1)S(1)}, bf16[512,512]{1,0:T(8,128)(2,1)S(1)}, bf16[512,512]{1,0:T(8,128)(2,1)S...) fusion(bf16[6144,512]{1,0:T(8,128)(2,1)} %get-tuple-element.19), kind=kLoop, calls=%fused_computation.162 | loop fusion | flops 1048576 | bytes 10485760 | tf_op jit(solution)/shard_map/slice | solution.py:446
  234.4 4.2 %slice_convert_fusion = f32[2048,512]{1,0:T(8,128)} fusion(bf16[6144,512]{1,0:T(8,128)(2,1)} %get-tuple-element.19), kind=kLoop, calls=%fused_computation.50 | loop fusion | flops 1048576 | bytes 6291456 | tf_op jit(solution)/shard_map/convert_element_type | solution.py:446
  239.2 2.7 %maximum_convert_fusion = f32[512,2048]{1,0:T(8,128)} fusion(bf16[512,512]{1,0:T(8,128)(2,1)S(1)} %get-tuple-element.38, bf16[512,512]{1,0:T(8,128)(2,1)S(1)} %get-tuple-element.39, bf16[512,512]{1,0:T(8,128)(2,1)S(1)} %get-tuple-element.40, bf16[512,512]{1,0:T(8,128)(2,1)S(1)} %get-tuple-element.37), kind=kLoop, calls=%fused_computation.43 | loop fusion | flops 8388608 | bytes 6291456 | tf_op jit(solution)/shard_map/concatenate | solution.py:448
  242.3 1.2 fusion.48
  (129 shorter events, 6.6 us)
Async XLA Ops:
  7.2 53.1 %copy-start = (bf16[512,2048]{1,0:T(8,128)(2,1)S(1)}, bf16[512,2048]{1,0:T(8,128)(2,1)}, u32[]{:S(2)}) copy-start(bf16[512,2048]{1,0:T(8,128)(2,1)} %param.31) | copy-start | bytes 6291460
  7.2 5.7 %copy-start.7 = (bf16[3,128,512]{2,1,0:T(8,128)(2,1)S(1)}, bf16[3,128,512]{2,1,0:T(8,128)(2,1)}, u32[]{:S(2)}) copy-start(bf16[3,128,512]{2,1,0:T(8,128)(2,1)} %param.19) | copy-start | bytes 1179652
  7.2 5.7 %copy-start.29 = (bf16[512]{0:T(512)(128)(2,1)S(1)}, bf16[512]{0:T(512)(128)(2,1)}, u32[]{:S(2)}) copy-start(bf16[512]{0:T(512)(128)(2,1)} %param.23) | copy-start | bytes 3076
  7.2 5.7 %copy-start.22 = (bf16[512,512]{1,0:T(8,128)(2,1)S(1)}, bf16[512,512]{1,0:T(8,128)(2,1)}, u32[]{:S(2)}) copy-start(bf16[512,512]{1,0:T(8,128)(2,1)} %param.22) | copy-start | bytes 1572868
  7.2 6.8 %copy-start.30 = (bf16[512]{0:T(512)(128)(2,1)S(1)}, bf16[512]{0:T(512)(128)(2,1)}, u32[]{:S(2)}) copy-start(bf16[512]{0:T(512)(128)(2,1)} %param.34) | copy-start | bytes 3076
  7.3 6.8 %copy-start.27 = (bf16[2048]{0:T(1024)(128)(2,1)S(1)}, bf16[2048]{0:T(1024)(128)(2,1)}, u32[]{:S(2)}) copy-start(bf16[2048]{0:T(1024)(128)(2,1)} %param.32) | copy-start | bytes 12292
  7.3 6.8 %copy-start.31 = (bf16[512]{0:T(512)(128)(2,1)S(1)}, bf16[512]{0:T(512)(128)(2,1)}, u32[]{:S(2)}) copy-start(bf16[512]{0:T(512)(128)(2,1)} %param.28) | copy-start | bytes 3076
  7.3 8.1 %copy-start.32 = (bf16[512]{0:T(512)(128)(2,1)S(1)}, bf16[512]{0:T(512)(128)(2,1)}, u32[]{:S(2)}) copy-start(bf16[512]{0:T(512)(128)(2,1)} %param.30) | copy-start | bytes 3076
  7.3 8.1 %copy-start.33 = (bf16[512]{0:T(512)(128)(2,1)S(1)}, bf16[512]{0:T(512)(128)(2,1)}, u32[]{:S(2)}) copy-start(bf16[512]{0:T(512)(128)(2,1)} %param.29) | copy-start | bytes 3076
  7.3 8.1 %copy-start.34 = (bf16[512]{0:T(512)(128)(2,1)S(1)}, bf16[512]{0:T(512)(128)(2,1)}, u32[]{:S(2)}) copy-start(bf16[512]{0:T(512)(128)(2,1)} %param.35) | copy-start | bytes 3076
  7.3 8.1 %copy-start.35 = (bf16[512]{0:T(512)(128)(2,1)S(1)}, bf16[512]{0:T(512)(128)(2,1)}, u32[]{:S(2)}) copy-start(bf16[512]{0:T(512)(128)(2,1)} %param.36) | copy-start | bytes 3076
  7.3 8.1 %copy-start.28 = (s32[3,128]{1,0:T(4,128)S(1)}, s32[3,128]{1,0:T(4,128)}, u32[]{:S(2)}) copy-start(s32[3,128]{1,0:T(4,128)} %param.21) | copy-start | bytes 4612
  7.3 8.1 %copy-start.36 = (s32[3]{0:T(128)S(1)}, s32[3]{0:T(128)}, u32[]{:S(2)}) copy-start(s32[3]{0:T(128)} %param.20) | copy-start | bytes 40
  7.3 23.1 %all-gather.5.cloned.1.call-start = ((), (), s32[]{:S(2)}) async-start(), calls=%async_computation.2 | async-start | bytes 1966080 | tf_op jit(solution)/shard_map/all_gather | solution.py:316
  9.8 42.4 %all-gather.3.cloned.1.call-start = ((), (), s32[]{:S(2)}) async-start(), calls=%async_computation.1 | async-start | bytes 1966080 | tf_op jit(solution)/shard_map/all_gather | solution.py:317
  12.9 133.0 %reduce-scatter.2.cloned.1.call-start = ((), (), s32[]{:S(2)}) async-start(), calls=%async_computation.3 | async-start | bytes 3932160 | tf_op jit(solution)/shard_map/reduce_scatter | solution.py:405
  35.9 2.7 %copy-start.2 = (f32[3,128,8,512]{1,3,2,0:T(8,128)}, f32[3,128,8,512]{1,3,2,0:T(8,128)S(1)}, u32[]{:S(2)}) copy-start(f32[3,128,8,512]{1,3,2,0:T(8,128)S(1)} %get-tuple-element.55) | copy-start | bytes 18874372
  54.9 4.6 %copy-start.8 = (bf16[3,128,512]{2,1,0:T(8,128)(2,1)S(1)}, bf16[3,128,512]{2,1,0:T(8,128)(2,1)}, u32[]{:S(2)}) copy-start(bf16[3,128,512]{2,1,0:T(8,128)(2,1)} %param.19) | copy-start | bytes 1179652
  54.9 4.7 %copy-start.14 = (bf16[512,512]{1,0:T(8,128)(2,1)S(1)}, bf16[512,512]{1,0:T(8,128)(2,1)}, u32[]{:S(2)}) copy-start(bf16[512,512]{1,0:T(8,128)(2,1)} %param.27) | copy-start | bytes 1572868
  59.5 2.6 %copy-start.16 = (bf16[3,128,8,64]{1,3,2,0:T(8,128)(2,1)}, bf16[3,128,8,64]{1,3,2,0:T(8,128)(2,1)S(1)}, u32[]{:S(2)}) copy-start(bf16[3,128,8,64]{1,3,2,0:T(8,128)(2,1)S(1)} %fusion.59) | copy-start | bytes 1179652
  62.1 7.3 %copy-start.37 = (bf16[2048,512]{1,0:T(8,128)(2,1)S(1)}, bf16[2048,512]{1,0:T(8,128)(2,1)}, u32[]{:S(2)}) copy-start(bf16[2048,512]{1,0:T(8,128)(2,1)} %param.33) | copy-start | bytes 6291460
  69.4 1.1 copy-start.18
  69.4 1.4 copy-start.19
  72.4 1.9 copy-start.25
  74.3 1.4 copy-start.38
  75.7 0.9 copy-start.11
  75.7 3.5 %copy-start.5 = (bf16[3,512,512]{1,2,0:T(8,128)(2,1)S(1)}, bf16[3,512,512]{1,2,0:T(8,128)(2,1)}, u32[]{:S(2)}) copy-start(bf16[3,512,512]{1,2,0:T(8,128)(2,1)} %copy.58) | copy-start | bytes 4718596
  76.0 0.7 copy-start.20
  97.8 1.7 copy-start.3
  99.5 5.0 %copy-start.6 = (bf16[3,512,512]{2,1,0:T(8,128)(2,1)S(1)}, bf16[3,512,512]{2,1,0:T(8,128)(2,1)}, u32[]{:S(2)}) copy-start(bf16[3,512,512]{2,1,0:T(8,128)(2,1)} %copy.69) | copy-start | bytes 4718596
  108.0 1.4 copy-start.4
  109.4 2.8 %copy-start.26 = (bf16[3,128,512]{2,1,0:T(8,128)(2,1)S(1)}, bf16[3,128,512]{2,1,0:T(8,128)(2,1)}, u32[]{:S(2)}) copy-start(bf16[3,128,512]{2,1,0:T(8,128)(2,1)} %copy-done.25) | copy-start | bytes 1179652
  112.2 4.2 %copy-start.39 = (bf16[3,128,2048]{2,1,0:T(8,128)(2,1)S(1)}, bf16[3,128,2048]{2,1,0:T(8,128)(2,1)}, u32[]{:S(2)}) copy-start(bf16[3,128,2048]{2,1,0:T(8,128)(2,1)} %copy-done.38) | copy-start | bytes 4718596
  117.8 3.4 %copy-start.17 = (bf16[3,128,8,64]{1,3,2,0:T(8,128)(2,1)S(1)}, bf16[3,128,8,64]{1,3,2,0:T(8,128)(2,1)}, u32[]{:S(2)}) copy-start(bf16[3,128,8,64]{1,3,2,0:T(8,128)(2,1)} %copy-done.16) | copy-start | bytes 1179652
  117.8 3.4 %copy-start.21 = (bf16[3,128,512]{2,1,0:T(8,128)(2,1)S(1)}, bf16[3,128,512]{2,1,0:T(8,128)(2,1)}, u32[]{:S(2)}) copy-start(bf16[3,128,512]{2,1,0:T(8,128)(2,1)} %copy-done.20) | copy-start | bytes 1179652
  117.8 4.6 %copy-start.9 = (bf16[3,128,512]{2,1,0:T(8,128)(2,1)S(1)}, bf16[3,128,512]{2,1,0:T(8,128)(2,1)}, u32[]{:S(2)}) copy-start(bf16[3,128,512]{2,1,0:T(8,128)(2,1)} %param.19) | copy-start | bytes 1179652
  118.7 5.1 %copy-start.12 = (f32[3,128,512]{2,1,0:T(8,128)S(1)}, f32[3,128,512]{2,1,0:T(8,128)}, u32[]{:S(2)}) copy-start(f32[3,128,512]{2,1,0:T(8,128)} %copy-done.11) | copy-start | bytes 2359300
  118.7 5.1 %copy-start.23 = (bf16[512,512]{1,0:T(8,128)(2,1)S(1)}, bf16[512,512]{1,0:T(8,128)(2,1)}, u32[]{:S(2)}) copy-start(bf16[512,512]{1,0:T(8,128)(2,1)} %param.22) | copy-start | bytes 1572868
  239.2 2.7 %copy-start.10 = (f32[3,128,512]{2,1,0:T(8,128)S(1)}, f32[3,128,512]{2,1,0:T(8,128)}, u32[]{:S(2)}) copy-start(f32[3,128,512]{2,1,0:T(8,128)} %convolution_add_fusion.3) | copy-start | bytes 2359300
  239.2 2.7 %copy-start.13 = (bf16[512,512]{1,0:T(8,128)(2,1)S(1)}, bf16[512,512]{1,0:T(8,128)(2,1)}, u32[]{:S(2)}) copy-start(bf16[512,512]{1,0:T(8,128)(2,1)} %param.24) | copy-start | bytes 1572868
  239.2 2.7 %copy-start.15 = (bf16[3,128,1024]{2,1,0:T(8,128)(2,1)S(1)}, bf16[3,128,1024]{2,1,0:T(8,128)(2,1)}, u32[]{:S(2)}) copy-start(bf16[3,128,1024]{2,1,0:T(8,128)(2,1)} %reduce-scatter.2.cloned.1.call-done) | copy-start | bytes 2359300
  239.2 3.1 %copy-start.24 = (bf16[512,512]{1,0:T(8,128)(2,1)S(1)}, bf16[512,512]{1,0:T(8,128)(2,1)}, u32[]{:S(2)}) copy-start(bf16[512,512]{1,0:T(8,128)(2,1)} %param.25) | copy-start | bytes 1572868
  239.2 4.3 %copy-start.1 = (bf16[512,2048]{1,0:T(8,128)(2,1)S(1)}, bf16[512,2048]{1,0:T(8,128)(2,1)}, u32[]{:S(2)}) copy-start(bf16[512,2048]{1,0:T(8,128)(2,1)} %param.31) | copy-start | bytes 6291460
Sparse Core Ops, SparseCore 0:
  10.3 20.0 all-gather.4
  32.6 19.6 all-gather.2
  108.1 37.6 reduce-scatter.1

commit v2 on v0

v2 whole, which is shorter than its diff:
```python
import functools

import jax
import jax.numpy as jnp
from jax import lax
from jax.experimental import pallas as pl
from jax.experimental.pallas import tpu as pltpu
from jax.sharding import PartitionSpec as P

HEAD = 64
EPSILON = 1e-06
MESH = pl.DeviceIdType.MESH
ROWS = 16
LOW = jnp.bfloat16
WIDE = jnp.float32
VECTORS = 16


def bits_of(sizes):
    found = {}
    for axis, size in sizes.items():
        found[axis] = []
        step = 1
        while step < size:
            found[axis].append((axis, step))
            step *= 2
    return found


def orders_of(sizes):
    bits = bits_of(sizes)
    blk, dp = bits["blk"], bits["dp"]
    return (
        blk[:1] + dp[:1] + blk[1:] + dp[1:],
        blk + dp,
        blk[:1] + dp[1:] + dp[:1] + blk[1:],
    )


def partner_of(bit):
    axis, step = bit
    index = lax.axis_index(axis)
    side = lax.rem(lax.div(index, step), 2)
    return side, {axis: index + step - 2 * step * side}


def flip(index, step):
    return index + step - 2 * step * lax.rem(lax.div(index, step), 2)


def aligned(start, unit):
    return start if isinstance(start, int) else pl.multiple_of(start, unit)


def span(start, count, unit=ROWS):
    return pl.ds(aligned(start, unit), count)


def send(src, dst, sems, at, peer):
    sends, receives = sems
    copy = pltpu.make_async_remote_copy(
        src_ref=src,
        dst_ref=dst,
        send_sem=sends.at[at],
        recv_sem=receives.at[at],
        device_id=peer,
        device_id_type=MESH,
    )
    copy.start()
    return copy


def plan_of(rows, order):
    plan = []
    size = rows
    for bit in order:
        split = (size // 2) % ROWS == 0
        size = size // 2 if split else size
        plan.append((bit, split, size))
    return plan


def landing_rows(rows, order):
    return sum(size for _, _, size in plan_of(rows, order))


def add_rows(first, first_at, second, second_at, out, out_at, count):
    chunk = 64 if count % 64 == 0 else (32 if count % 32 == 0 else 16)

    def body(step, carry):
        shift = step * chunk
        total = first[span(first_at + shift, chunk)].astype(WIDE) + second[span(second_at + shift, chunk)].astype(WIDE)
        out[span(out_at + shift, chunk)] = total.astype(out.dtype)
        return carry

    lax.fori_loop(0, count // chunk, body, 0)


def reduce_rows(work, land, out, sems, base, rows, land_at, sem_at, order, pending):
    plan = plan_of(rows, order)
    start = base
    trail = []
    for level, (bit, split, count) in enumerate(plan):
        side, peer = partner_of(bit)
        keep = start + side * count if split else start
        give = start + (1 - side) * count if split else start
        copy = send(work.at[span(give, count)], land.at[span(land_at, count)], sems, sem_at, peer)
        yield
        copy.wait_recv()
        if split:
            pending.append(copy)
            trail.append((peer, keep, count))
        else:
            copy.wait_send()
        target = out if level == len(plan) - 1 else work
        add_rows(work, keep, land, land_at, target, keep, count)
        land_at += count
        sem_at += 1
        start = keep
    for peer, mine, count in reversed(trail):
        part = out.at[span(mine, count)]
        copy = send(part, part, sems, sem_at, peer)
        yield
        copy.wait_recv()
        pending.append(copy)
        sem_at += 1


def reduce_whole(steps, land, sems, sem_at, order):
    for level, bit in enumerate(order):
        copy = send(steps.at[level], land.at[level], sems, sem_at + level, partner_of(bit)[1])
        yield
        copy.wait()
        steps[level + 1] = steps[level] + land[level]


def share_blocks(slots, sems, sem_at, me, pending):
    near, far = flip(me, 1), flip(me, 2)
    across = send(slots.at[me], slots.at[me], sems, sem_at, {"blk": far})
    beside = send(slots.at[me], slots.at[me], sems, sem_at + 1, {"blk": near})
    yield
    across.wait_recv()
    onward = send(slots.at[far], slots.at[far], sems, sem_at + 2, {"blk": near})
    yield
    beside.wait_recv()
    onward.wait_recv()
    pending.extend([across, beside, onward])


def advance(running):
    running[:] = [item for item in running if next(item, True) is None]


def by_rows(total, chunk, body, carry=0):
    def step(index, held):
        return body(pl.multiple_of(index * chunk, chunk), held)

    return lax.fori_loop(0, total // chunk, step, carry)


def dot(left, right):
    return jnp.dot(left, right, preferred_element_type=WIDE)


def dot_right_t(left, right):
    return lax.dot_general(left, right, (((1,), (1,)), ((), ())), preferred_element_type=WIDE)


def dot_left_t(left, right):
    return lax.dot_general(left, right, (((0,), (0,)), ((), ())), preferred_element_type=WIDE)


def fold(values):
    rows, width = values.shape
    return jnp.sum(values.reshape(rows // 8, 8, width), axis=0)


def mean_of(values):
    return jnp.mean(values, axis=-1, keepdims=True)


def norm_back(upstream, scaled, inverse, gain):
    inner = upstream * gain
    return inverse * (inner - mean_of(inner) - scaled * mean_of(inner * scaled))


def layout_of(sizes, seqs, rows, width, hidden):
    tokens = seqs * rows
    blocks = sizes["blk"]
    length = rows * blocks
    own = width // blocks
    heads = own // HEAD
    orders = orders_of(sizes)
    levels = len(orders[0])
    units = 2 * (hidden // width) + 1
    groups = group_table(sizes, width, hidden)
    land_total = sum(landing_rows(count, order) for _, count, order in groups)
    dp_order = bits_of(sizes)["dp"]
    shapes = {
        "x_all": ((seqs, length, width), LOW),
        "x_own": ((seqs, rows, width), LOW),
        "cot": ((seqs, rows, width), LOW),
        "w_qkv": ((width, 3 * own), LOW),
        "w_o": ((width, width), LOW),
        "w_up": ((width, hidden), LOW),
        "w_down": ((hidden, width), LOW),
        "flags": ((blocks, 8, rows), WIDE),
        "qkv": ((seqs, length, 3 * own), LOW),
        "probs": ((seqs * heads, length, length), LOW),
        "o_wide": ((seqs, length, own), WIDE),
        "o_send": ((seqs, length, own), LOW),
        "o_all": ((seqs, rows, width), LOW),
        "total": ((tokens, width), WIDE),
        "scaled": ((tokens, width), WIDE),
        "inverse": ((tokens, 128), WIDE),
        "normed": ((tokens, width), WIDE),
        "normed_low": ((tokens, width), LOW),
        "active": ((tokens, hidden), LOW),
        "slope": ((tokens, hidden), WIDE),
        "hid": ((seqs, rows, width), LOW),
        "grad_b": ((tokens, width), WIDE),
        "grad_y": ((tokens, width), LOW),
        "grad_z": ((tokens, hidden), LOW),
        "grad_t": ((tokens, width), LOW),
        "do_send": ((seqs, rows, width), LOW),
        "do_all": ((seqs, length, own), LOW),
        "grad_s": ((heads, length, length), LOW),
        "d_qkv": ((seqs, length, 3 * own), LOW),
        "dx_part": ((seqs, length, width), LOW),
        "dx_near": ((seqs, 2, rows, width), LOW),
        "dx_chip": ((seqs, rows, width), LOW),
        "dx_far": ((seqs, rows, width), LOW),
        "dx": ((seqs, rows, width), LOW),
        "work": ((units * width, width), LOW),
        "land": ((land_total, width), LOW),
        "out": ((units * width, width), LOW),
        "qkv_work": ((width, 3 * own), LOW),
        "qkv_land": ((landing_rows(width, dp_order), 3 * own), LOW),
        "qkv_out": ((blocks, width, 3 * own), LOW),
        "steps": ((levels + 1, VECTORS, width), WIDE),
        "vec_land": ((levels, VECTORS, width), WIDE),
    }
    return shapes


def group_table(sizes, width, hidden):
    orders = orders_of(sizes)
    half = hidden // 2
    return (
        (0, half, orders[0]),
        (half, half, orders[1]),
        (2 * half, half, orders[2]),
        (3 * half, half + width, orders[0]),
    )


OUT_NAMES = ("hid_out", "dx_out", "sums_out", "qkv_sums_out", "vec_out")
IN_NAMES = ("x", "lengths", "mask", "wq", "wk", "wv", "wo", "wu", "wd", "vec", "cotangent")


def layer_kernel(sizes, scratch_names, *refs):
    names = IN_NAMES + OUT_NAMES + tuple(scratch_names) + ("sends", "receives", "local")
    r = dict(zip(names, refs, strict=True))
    sems = (r["sends"], r["receives"])
    local = r["local"]
    x_all, qkv, vec, steps = r["x_all"], r["qkv"], r["vec"], r["steps"]
    seqs, rows, width = r["x_own"].shape
    tokens = seqs * rows
    length = x_all.shape[1]
    blocks = sizes["blk"]
    own = width // blocks
    heads = own // HEAD
    hidden = r["w_up"].shape[1]
    tiles = hidden // width
    scale = HEAD ** (-0.5)
    bits = bits_of(sizes)
    me = lax.axis_index("blk")
    near, far = flip(me, 1), flip(me, 2)
    cross = flip(far, 1)
    peers = (near, far, cross)
    place = lambda index: span(index * rows, rows, rows)
    lanes = lambda index: span(index * own, own, own)

    used = {"sem": 0, "local": 0}
    pending, stores = [], []

    def slot(count=1):
        at = used["sem"]
        used["sem"] += count
        return at

    def fetch(src, dst):
        copy = pltpu.make_async_copy(src, dst, local.at[used["local"]])
        used["local"] += 1
        copy.start()
        return copy

    loads_x = [
        fetch(r["x"], x_all.at[:, place(me), :]),
        fetch(r["x"], r["x_own"]),
    ]
    loads_w = [
        fetch(r[name].at[:, lanes(me)], r["w_qkv"].at[:, pl.ds(at * own, own)])
        for at, name in enumerate(("wq", "wk", "wv"))
    ]
    load_o = fetch(r["wo"], r["w_o"])
    load_up = fetch(r["wu"], r["w_up"])
    load_down = fetch(r["wd"], r["w_down"])
    load_cot = fetch(r["cotangent"], r["cot"])

    positions = me * rows + lax.broadcasted_iota(jnp.int32, (1, rows), 1)
    flag_rows = []
    for seq in range(seqs):
        good = (r["mask"][seq : seq + 1, :] == 1) & (positions < r["lengths"][seq])
        flag_rows.append(jnp.where(good, 0.0, -1000000000.0).astype(WIDE))
    flag_rows.append(jnp.zeros((8 - seqs, rows), WIDE))
    r["flags"][me] = jnp.concatenate(flag_rows, axis=0)

    barrier = pltpu.get_barrier_semaphore()
    greeted = [{"blk": peer} for peer in peers] + [partner_of(bit)[1] for bit in bits["dp"]]
    for peer in greeted:
        pl.semaphore_signal(barrier, inc=1, device_id=peer, device_id_type=MESH)
    pl.semaphore_wait(barrier, len(greeted))

    at_far, at_near, at_on, at_flag = slot(seqs), slot(seqs), slot(seqs), slot(len(peers))
    flag_copies = [
        send(r["flags"].at[me], r["flags"].at[me], sems, at_flag + index, {"blk": peer})
        for index, peer in enumerate(peers)
    ]
    x_far, x_near, x_on = [], [], []
    for seq in range(seqs):
        target = x_all.at[seq, place(me), :]
        x_far.append(send(r["x"].at[seq], target, sems, at_far + seq, {"blk": far}))
        x_near.append(send(r["x"].at[seq], target, sems, at_near + seq, {"blk": near}))
    pending += flag_copies + x_far + x_near

    def forward_x(seq):
        x_far[seq].wait_recv()
        block = x_all.at[seq, place(far), :]
        x_on.append(send(block, block, sems, at_on + seq, {"blk": near}))

    lane = lax.broadcasted_iota(jnp.int32, (1, own), 1)
    of_head = [(lane >= head * HEAD) & (lane < (head + 1) * HEAD) for head in range(heads)]
    only = lambda values, head: jnp.where(of_head[head], values.astype(WIDE), 0.0)
    bias_q = vec[0:1, lanes(me)]
    bias_v = vec[1:2, lanes(me)]
    bias_qkv = jnp.concatenate([bias_q, jnp.zeros_like(bias_q), bias_v], axis=1)
    o_all, o_send = r["o_all"], r["o_send"]
    at_o = slot(seqs * len(peers))
    o_copies = []

    def project(seq):
        def body(at, carry):
            made = dot(x_all[seq, pl.ds(at, 256), :], r["w_qkv"][...]) + bias_qkv
            qkv[seq, pl.ds(at, 256), :] = made.astype(LOW)
            return carry

        by_rows(length, 256, body)

    def attend(seq):
        keys = qkv[seq, :, own : 2 * own]
        values = qkv[seq, :, 2 * own :]
        key_bias = jnp.concatenate([r["flags"][block, seq : seq + 1, :] for block in range(blocks)], axis=1)
        column = lax.broadcasted_iota(jnp.int32, (128, length), 1)
        row = lax.broadcasted_iota(jnp.int32, (128, length), 0)

        def body(at, carry):
            query = qkv[seq, pl.ds(at, 128), 0:own].astype(WIDE) * scale
            bias = jnp.where(column == row + at, 0.0, key_bias)
            joined = None
            for head in range(heads):
                scores = dot_right_t(only(query, head).astype(LOW), keys) + bias
                raised = jnp.exp(scores - jnp.max(scores, axis=-1, keepdims=True))
                probs = (raised / jnp.sum(raised, axis=-1, keepdims=True)).astype(LOW)
                r["probs"][seq * heads + head, pl.ds(at, 128), :] = probs
                result = dot(probs, values)
                joined = result if joined is None else jnp.where(of_head[head], result, joined)
            r["o_wide"][seq, pl.ds(at, 128), :] = joined
            o_send[seq, pl.ds(at, 128), :] = joined.astype(LOW)
            return carry

        by_rows(length, 128, body)
        for index, peer in enumerate(peers):
            o_copies.append(
                send(
                    o_send.at[seq, place(peer), :],
                    o_all.at[seq, :, lanes(me)],
                    sems,
                    at_o + seq * len(peers) + index,
                    {"blk": peer},
                )
            )
        o_all[seq, :, lanes(me)] = o_send[seq, place(me), :]

    for copy in loads_w:
        copy.wait()
    for copy in loads_x:
        copy.wait()
    for copy in flag_copies:
        copy.wait_recv()
    forward_x(0)
    for seq in range(seqs):
        x_near[seq].wait_recv()
        x_on[seq].wait_recv()
        project(seq)
        if seq + 1 < seqs:
            forward_x(seq + 1)
        attend(seq)
    pending += x_on + o_copies

    total, scaled, inverse = r["total"], r["scaled"], r["inverse"]
    normed, normed_low = r["normed"], r["normed_low"]
    wide_row = lambda at: vec[at : at + 1, :]
    load_o.wait()
    for copy in o_copies:
        copy.wait_recv()
    flat = lambda ref, at, count: ref[lax.div(at, rows), span(lax.rem(at, rows), count), :]

    total[...] = dot(o_all[...].reshape(tokens, width), r["w_o"][...])

    def first_norm(at, carry):
        part = pl.ds(at, 32)
        values = flat(r["x_own"], at, 32).astype(WIDE) + total[part, :] + wide_row(2)
        center = values - mean_of(values)
        inv = lax.rsqrt(mean_of(center * center) + EPSILON)
        made = center * inv
        scaled[part, :] = made
        inverse[part, :] = jnp.broadcast_to(inv, (32, 128))
        result = made * wide_row(3) + wide_row(4)
        normed[part, :] = result
        normed_low[part, :] = result.astype(LOW)
        return carry

    by_rows(tokens, 32, first_norm)

    load_up.wait()
    active, slope = r["active"], r["slope"]

    def up(tile, carry):
        columns = span(tile * width, width, width)
        total[...] = dot(normed_low[...], r["w_up"][:, columns])
        offset = vec[pl.ds(8 + tile, 1), :]

        def bend(at, held):
            part = pl.ds(at, 32)
            z = total[part, :] + offset
            below = 0.5 * (1.0 + lax.erf(z * 0.7071067811865476))
            active[part, columns] = (z * below).astype(LOW)
            slope[part, columns] = below + z * (0.3989422804014327 * jnp.exp(-0.5 * z * z))
            return held

        by_rows(tokens, 32, bend)
        return carry

    lax.fori_loop(0, tiles, up, 0)
    load_down.wait()
    load_cot.wait()
    total[...] = dot(active[...], r["w_down"][...])

    grad_b, grad_y = r["grad_b"], r["grad_y"]
    zero = jnp.zeros((8, width), WIDE)

    def second_norm(at, sums):
        shift_sum, gain_sum, down_sum = sums
        part = pl.ds(at, 32)
        values = normed[part, :] + total[part, :] + wide_row(5)
        center = values - mean_of(values)
        inv = lax.rsqrt(mean_of(center * center) + EPSILON)
        made = center * inv
        r["hid"][lax.div(at, rows), span(lax.rem(at, rows), 32), :] = (made * wide_row(6) + wide_row(7)).astype(LOW)
        upstream = flat(r["cot"], at, 32).astype(WIDE)
        back = norm_back(upstream, made, inv, wide_row(6))
        grad_b[part, :] = back
        rounded = back.astype(LOW)
        grad_y[part, :] = rounded
        return shift_sum + fold(upstream), gain_sum + fold(upstream * made), down_sum + fold(rounded.astype(WIDE))

    shift_sum, gain_sum, down_sum = by_rows(tokens, 32, second_norm, (zero, zero, zero))
    stores.append(fetch(r["hid"], r["hid_out"]))
    total_row = lambda values: jnp.sum(values, axis=0, keepdims=True)
    steps[0] = jnp.zeros((VECTORS, width), WIDE)
    steps[0, 7:8, :] = total_row(shift_sum)
    steps[0, 6:7, :] = total_row(gain_sum)
    steps[0, 5:6, :] = total_row(down_sum)

    work = r["work"]
    groups = group_table(sizes, width, hidden)
    running = []
    land_at = 0

    def launch(index):
        nonlocal land_at
        base, count, order = groups[index]
        running.append(
            reduce_rows(work, r["land"], r["out"], sems, base, count, land_at, slot(2 * len(order)), order, pending)
        )
        land_at += landing_rows(count, order)
        next(running[-1])

    for tile in range(tiles):
        work[tile * width : (tile + 1) * width, :] = dot_left_t(
            active[:, tile * width : (tile + 1) * width], grad_y[...]
        ).astype(LOW)
        if tile == tiles // 2 - 1:
            launch(0)
    launch(1)

    grad_z = r["grad_z"]

    def back_up(tile, carry):
        columns = span(tile * width, width, width)
        total[...] = dot_right_t(grad_y[...], r["w_down"][columns, :])

        def bend(at, held):
            part = pl.ds(at, 32)
            made = (total[part, :] * slope[part, columns]).astype(LOW)
            grad_z[part, columns] = made
            return held + fold(made.astype(WIDE))

        sums = by_rows(tokens, 32, bend, zero)
        steps[0, pl.ds(8 + tile, 1), :] = total_row(sums)
        return carry

    lax.fori_loop(0, tiles, back_up, 0)
    advance(running)
    total[...] = dot_right_t(grad_z[...], r["w_up"][...])

    grad_t = r["grad_t"]

    def first_back(at, sums):
        shift_part, gain_part, out_part = sums
        part = pl.ds(at, 32)
        upstream = grad_b[part, :] + total[part, :]
        made = scaled[part, :]
        back = norm_back(upstream, made, inverse[part, 0:1], wide_row(3))
        grad_b[part, :] = back
        rounded = back.astype(LOW)
        grad_t[part, :] = rounded
        return shift_part + fold(upstream), gain_part + fold(upstream * made), out_part + fold(rounded.astype(WIDE))

    shift_part, gain_part, out_part = by_rows(tokens, 32, first_back, (zero, zero, zero))
    steps[0, 4:5, :] = total_row(shift_part)
    steps[0, 3:4, :] = total_row(gain_part)
    steps[0, 2:3, :] = total_row(out_part)

    do_send, do_all = r["do_send"], r["do_all"]
    at_do = slot(seqs * len(peers))
    do_copies = []
    made = dot_right_t(grad_t[...], r["w_o"][...]).astype(LOW)
    do_send[...] = made.reshape(seqs, rows, width)
    for seq in range(seqs):
        do_copies.append(
            [
                send(
                    do_send.at[seq, :, lanes(peer)],
                    do_all.at[seq, place(me), :],
                    sems,
                    at_do + seq * len(peers) + index,
                    {"blk": peer},
                )
                for index, peer in enumerate(peers)
            ]
        )
        do_all[seq, place(me), :] = do_send[seq, :, lanes(me)]
        pending += do_copies[-1]

    advance(running)
    for tile in range(tiles):
        at = hidden + tile * width
        work[at : at + width, :] = dot_left_t(normed_low[...], grad_z[:, tile * width : (tile + 1) * width]).astype(LOW)
        if tile == tiles // 2 - 1:
            launch(2)
    work[2 * hidden : 2 * hidden + width, :] = dot_left_t(
        o_all[...].reshape(tokens, width), grad_t[...]
    ).astype(LOW)
    launch(3)
    advance(running)

    d_qkv, grad_s, dx_part = r["d_qkv"], r["grad_s"], r["dx_part"]
    at_dx_near, at_dx_far = slot(2 * seqs), slot(seqs)
    dx_near, dx_far = [], []

    def attend_back(seq):
        keys = qkv[seq, :, own : 2 * own]
        values = qkv[seq, :, 2 * own :]

        def body(at, carry):
            upstream = do_all[seq, pl.ds(at, 128), :].astype(WIDE)
            inner = upstream * r["o_wide"][seq, pl.ds(at, 128), :]
            for head in range(heads):
                delta = jnp.sum(jnp.where(of_head[head], inner, 0.0), axis=-1, keepdims=True)
                prob_grad = dot_right_t(only(upstream, head).astype(LOW), values)
                probs = r["probs"][seq * heads + head, pl.ds(at, 128), :].astype(WIDE)
                grad_s[head, pl.ds(at, 128), :] = (probs * (prob_grad - delta)).astype(LOW)
            return carry

        by_rows(length, 128, body)
        queries_wide = qkv[seq, :, 0:own].astype(WIDE) * scale
        keys_wide = keys.astype(WIDE) * scale
        upstream = do_all[seq]
        query_grad = key_grad = value_grad = None
        for head in range(heads):
            terms = (
                dot(grad_s[head], only(keys_wide, head).astype(LOW)),
                dot_left_t(grad_s[head], only(queries_wide, head).astype(LOW)),
                dot_left_t(r["probs"][seq * heads + head], only(upstream, head).astype(LOW)),
            )
            if query_grad is None:
                query_grad, key_grad, value_grad = terms
            else:
                query_grad, key_grad, value_grad = query_grad + terms[0], key_grad + terms[1], value_grad + terms[2]
        d_qkv[seq, :, 0:own] = query_grad.astype(LOW)
        d_qkv[seq, :, own : 2 * own] = key_grad.astype(LOW)
        d_qkv[seq, :, 2 * own :] = value_grad.astype(LOW)

        def partial(at, carry):
            dx_part[seq, pl.ds(at, 128), :] = dot_right_t(d_qkv[seq, pl.ds(at, 128), :], r["w_qkv"][...]).astype(LOW)
            return carry

        by_rows(length, 128, partial)
        dx_near.append(
            [
                send(dx_part.at[seq, place(near), :], r["dx_near"].at[seq, 0], sems, at_dx_near + 2 * seq, {"blk": near}),
                send(dx_part.at[seq, place(cross), :], r["dx_near"].at[seq, 1], sems, at_dx_near + 2 * seq + 1, {"blk": near}),
            ]
        )
        pending.extend(dx_near[-1])

    def hand_on(seq):
        dx_near[seq][1].wait_recv()

        def body(at, carry):
            part = pl.ds(at, 32)
            summed = dx_part[seq, span(far * rows + at, 32), :].astype(WIDE) + r["dx_near"][seq, 1, part, :].astype(WIDE)
            r["dx_chip"][seq, part, :] = summed.astype(LOW)
            return carry

        by_rows(rows, 32, body)
        dx_far.append(send(r["dx_chip"].at[seq], r["dx_far"].at[seq], sems, at_dx_far + seq, {"blk": far}))
        pending.append(dx_far[-1])

    for seq in range(seqs):
        for copy in do_copies[seq]:
            copy.wait_recv()
        attend_back(seq)
        if seq > 0:
            hand_on(seq - 1)
        advance(running)
    hand_on(seqs - 1)

    flat_d = d_qkv[...].reshape(seqs * length, 3 * own)
    made = dot_left_t(x_all[...].reshape(seqs * length, width), flat_d)
    r["qkv_work"][...] = made.astype(LOW)

    def offsets(at, sums):
        part = flat_rows(d_qkv, at, 128, length)
        return sums + fold(part.astype(WIDE))

    flat_rows = lambda ref, at, count, each: ref[lax.div(at, each), span(lax.rem(at, each), count), :]
    sums = total_row(by_rows(seqs * length, 128, offsets, jnp.zeros((8, 3 * own), WIDE)))
    steps[0, 0:1, lanes(me)] = sums[:, 0:own]
    steps[0, 1:2, lanes(me)] = sums[:, 2 * own :]

    def sum_qkv():
        dp_order = bits["dp"]
        base = slot(2 * len(dp_order))
        blocks_at = slot(3)
        yield from reduce_rows(
            r["qkv_work"], r["qkv_land"], r["qkv_out"].at[me], sems, 0, width, 0, base, dp_order, pending
        )
        yield from share_blocks(r["qkv_out"], sems, blocks_at, me, pending)

    running.append(sum_qkv())
    running.append(reduce_whole(steps, r["vec_land"], sems, slot(len(groups[0][2])), groups[1][2]))
    advance(running)

    for seq in range(seqs):
        dx_near[seq][0].wait_recv()
        dx_far[seq].wait_recv()

        def finish(at, carry):
            part = pl.ds(at, 32)
            summed = grad_b[span(seq * rows + at, 32), :] + dx_part[seq, span(me * rows + at, 32), :].astype(WIDE)
            summed = summed + r["dx_near"][seq, 0, part, :].astype(WIDE) + r["dx_far"][seq, part, :].astype(WIDE)
            r["dx"][seq, part, :] = summed.astype(LOW)
            return carry

        by_rows(rows, 32, finish)
        advance(running)
    stores.append(fetch(r["dx"], r["dx_out"]))

    while running:
        advance(running)
    r["vec_out"][...] = steps[len(groups[0][2])]
    stores.append(fetch(r["out"], r["sums_out"]))
    stores.append(fetch(r["qkv_out"], r["qkv_sums_out"]))
    for copy in pending:
        copy.wait_send()
    for copy in stores:
        copy.wait()


def on_device(
    sizes,
    hidden_input,
    lengths,
    key_mask,
    query_weight,
    query_offset,
    key_weight,
    value_weight,
    value_offset,
    output_weight,
    output_offset,
    mixer_gain,
    mixer_shift,
    up_weight,
    up_offset,
    down_weight,
    down_offset,
    final_gain,
    final_shift,
    cotangent,
):
    seqs, rows, width = hidden_input.shape
    hidden = up_weight.shape[1]
    blocks = sizes["blk"]
    own = width // blocks
    tiles = hidden // width
    vectors = (query_offset, value_offset, output_offset, mixer_gain, mixer_shift, down_offset, final_gain, final_shift)
    spare = jnp.zeros(((VECTORS - len(vectors) - tiles) * width,), LOW)
    vec = jnp.concatenate(vectors + (up_offset, spare)).astype(WIDE).reshape(VECTORS, width)
    scratch = layout_of(sizes, seqs, rows, width, hidden)
    anywhere = pl.BlockSpec(memory_space=pl.ANY)
    inside = pl.BlockSpec(memory_space=pltpu.VMEM)
    scalars = pl.BlockSpec(memory_space=pltpu.SMEM)
    units = scratch["work"][0]
    hid, dx, sums, qkv_sums, vec_sums = pl.pallas_call(
        functools.partial(layer_kernel, sizes, tuple(scratch)),
        out_shape=(
            jax.ShapeDtypeStruct(hidden_input.shape, LOW),
            jax.ShapeDtypeStruct(hidden_input.shape, LOW),
            jax.ShapeDtypeStruct(units, LOW),
            jax.ShapeDtypeStruct((blocks, width, 3 * own), LOW),
            jax.ShapeDtypeStruct((VECTORS, width), WIDE),
        ),
        in_specs=[anywhere, scalars, inside] + [anywhere] * 6 + [inside, anywhere],
        out_specs=(anywhere, anywhere, anywhere, anywhere, inside),
        scratch_shapes=[pltpu.VMEM(shape, kind) for shape, kind in scratch.values()]
        + [
            pltpu.SemaphoreType.DMA((256,)),
            pltpu.SemaphoreType.DMA((256,)),
            pltpu.SemaphoreType.DMA((32,)),
        ],
        compiler_params=pltpu.CompilerParams(
            collective_id=0, has_side_effects=True, vmem_limit_bytes=60 * 1024 * 1024
        ),
    )(
        hidden_input,
        lengths,
        key_mask,
        query_weight,
        key_weight,
        value_weight,
        output_weight,
        up_weight,
        down_weight,
        vec,
        cotangent,
    )
    wide = lambda at, count: sums[at : at + count].astype(WIDE)
    down_sum = wide(0, hidden)
    up_sum = jnp.concatenate([wide(hidden + at, width) for at in range(0, hidden, width)], axis=1)
    output_sum = wide(2 * hidden, width)
    query_sum, key_sum, value_sum = (
        jnp.concatenate([qkv_sums[block, :, at * own : (at + 1) * own] for block in range(blocks)], axis=1).astype(WIDE)
        for at in range(3)
    )
    return (
        hid,
        dx,
        query_sum,
        vec_sums[0],
        key_sum,
        value_sum,
        vec_sums[1],
        output_sum,
        vec_sums[2],
        vec_sums[3],
        vec_sums[4],
        up_sum,
        vec_sums[8 : 8 + tiles].reshape(-1),
        down_sum,
        vec_sums[5],
        vec_sums[6],
        vec_sums[7],
    )


def solution(mesh):
    split = P("dp", "blk", None)
    in_specs = (split, P("dp"), P("dp", "blk")) + (P(),) * 15 + (split,)
    out_specs = (split, split) + (P(),) * 15
    return jax.shard_map(
        functools.partial(on_device, dict(mesh.shape)),
        mesh=mesh,
        in_specs=in_specs,
        out_specs=out_specs,
        check_vma=False,
    )
```

time: 416 us -> 166 us (0.40)
  waiting for transfers between devices: 240 us -> 0 us
  Pallas kernels: 0 us -> 142 us
  matrix products: 57.2 us -> 0 us
  blocking collectives: 48.4 us -> 0 us
  local copies, waits for them, and re-layouts: 31.1 us -> 14.4 us
  between operations: 14.4 us -> 0.7 us
  other arithmetic: 21.5 us -> 8.27 us
    psum x1 -> x0, waiting for transfers between devices: 193 us -> none  [on_device(): lax.psum((query_weight_part, query_offset_part, key_weight_part, value_we...]
    pallas_call x0 -> x1, Pallas kernels: none -> 142 us  [on_device(): pl.pallas_call(functools.partial(layer_kernel, sizes, tuple(scratch)), ou...]
    dot_general x24 -> x0, matrix products: 57.2 us -> none  [the longest x6 15.4 us: weight_term(): jnp.einsum('sqd,sqf->df', inputs, upstream, preferred_element_type=jnp.fl...]
    psum x1 -> x0, blocking collectives: 42.8 us -> none  [on_device(): lax.psum((query_weight_part, query_offset_part, key_weight_part, value_we...]
    reduce_scatter x1 -> x0, waiting for transfers between devices: 23.5 us -> none  [on_device(): lax.psum_scatter(joined.astype(jnp.bfloat16), 'blk', scatter_dimension=1,...]
    all_gather x2 -> x0, waiting for transfers between devices: 22.7 us -> none  [the longest x1 13.7 us: on_device(): value_piece = lax.all_gather(values, 'blk', axis=1, tiled=True)]
    convert_element_type x12 -> x2, other arithmetic: 14.2 us -> 4.05 us  [the longest x1 2.6 us: on_device(): wide = lambda at, count: sums[at:at + count].astype(WIDE)]
    unnamed x84 -> x19, local copies, waits for them, and re-layouts: 19.3 us -> 10.5 us
  transfers between devices with their start and end apart: 4 -> 0, of which waited for: 4 -> 0; matrix products, arithmetic and copies ran while one was open for 7% -> 0% of each run, Pallas kernels for 0% -> 0%
where the time goes in v2:
time: 166 us; the launch traced here: 165 us
  Pallas kernels  142 us (86%)
  local copies, waits for them, and re-layouts  14.4 us (9%)
  other arithmetic  8.27 us (5%)
    pallas_call x1, Pallas kernels, on_device(): pl.pallas_call(functools.partial(layer_kernel, sizes, tuple(scratch)), ou...  142 us
    unnamed x19, local copies, waits for them, and re-layouts  10.5 us

profile of v2, /device:TPU:5, one launch (start us, length us, event | category | flops | bytes accessed | tf_op | source)
XLA Modules:
  0.0 165.4 jit_solution(17190860951160370483)
XLA Ops:
  0.7 0.9 dynamic-update-slice
  1.5 0.9 dynamic-update-slice.1
  2.4 0.9 dynamic-update-slice.2
  3.3 0.9 dynamic-update-slice.3
  4.1 0.9 dynamic-update-slice.4
  5.0 0.9 dynamic-update-slice.5
  5.8 0.9 dynamic-update-slice.6
  6.7 0.9 dynamic-update-slice.7
  7.5 0.7 constant_dynamic-update-slice_fusion.1
  8.2 0.6 reshape.42.refs_9_
  8.9 142.1 %shard_map.314 = (bf16[3,128,512]{2,1,0:T(8,128)(2,1)}, bf16[3,128,512]{2,1,0:T(8,128)(2,1)}, bf16[4608,512]{1,0:T(8,128)(2,1)}, bf16[4,512,384]{2,1,0:T(8,128)(2,1)}, f32[16,512]{1,0:T(8,128)}) custom-call(bf16[3,128,512]{2,1,0:T(8,128)(2,1)} %refs_0_.1, s32[3]{0:T(128)} %refs_1_.1, s32[3,128]{1,0:T(4,128)} %refs_2_.1, bf16[512,512]{1,0:T(8,128)(2,1)} %refs_3_.1, ...), custom_call_target="tpu_custom_call" | custom-call | tf_op jit(solution)/shard_map/pallas_call | solution.py:738
  151.0 0.0 copy-start
  151.0 0.9 slice_bitcast_fusion.12
  151.8 1.6 fusion.1
  153.5 0.6 copy.36
  154.1 1.5 slice_bitcast_fusion.3
  155.6 1.5 maximum_convert_fusion.1
  157.1 0.0 copy-done
  157.1 1.7 %fusion = (bf16[512,512]{1,0:T(8,128)(2,1)S(1)}, bf16[512,512]{1,0:T(8,128)(2,1)S(1)}, bf16[512,512]{1,0:T(8,128)(2,1)S(1)}, bf16[512,512]{1,0:T(8,128)(2,1)S(1)}, f32[512,512]{1,0:T(8,128)}, /*index=5*/f32[512,512]{1,0:T(8,128)}) fusion(bf16[4608,512]{1,0:T(8,128)(2,1)S(1)} %copy-done, bf16[512,128]{1,0:T(8,128)(2,1)S(1)} %get-tuple-element.33, ...), kind=kLoop, calls=%fused_computation.21 | loop fusion | flops 2359296 | bytes 7340032 | tf_op jit(solution)/shard_map/slice | solution.py:771
  158.8 2.6 %slice_convert_fusion = f32[2048,512]{1,0:T(8,128)} fusion(bf16[4608,512]{1,0:T(8,128)(2,1)S(1)} %copy-done), kind=kLoop, calls=%fused_computation.1 | loop fusion | flops 1048576 | bytes 6291456 | tf_op jit(solution)/shard_map/convert_element_type | solution.py:771
  161.4 0.0 copy-start.2
  161.4 0.0 copy-start.1
  161.4 2.6 %maximum_convert_fusion = f32[512,2048]{1,0:T(8,128)} fusion(bf16[512,512]{1,0:T(8,128)(2,1)S(1)} %get-tuple-element.28, bf16[512,512]{1,0:T(8,128)(2,1)S(1)} %get-tuple-element.29, bf16[512,512]{1,0:T(8,128)(2,1)S(1)} %get-tuple-element.30, bf16[512,512]{1,0:T(8,128)(2,1)S(1)} %get-tuple-element.27), kind=kLoop, calls=%fused_computation | loop fusion | flops 8388608 | bytes 6291456 | tf_op jit(solution)/shard_map/concatenate | solution.py:773
  163.9 0.0 copy-done.2
  163.9 0.7 copy.49
  164.7 0.0 copy-done.1
  164.7 0.7 copy.50
  (2 shorter events, 0.0 us)
Async XLA Ops:
  151.0 6.1 %copy-start = (bf16[4608,512]{1,0:T(8,128)(2,1)S(1)}, bf16[4608,512]{1,0:T(8,128)(2,1)}, u32[]{:S(2)}) copy-start(bf16[4608,512]{1,0:T(8,128)(2,1)} %get-tuple-element.26) | copy-start | bytes 14155780
  161.4 2.6 %copy-start.2 = (bf16[3,128,512]{2,1,0:T(8,128)(2,1)S(1)}, bf16[3,128,512]{2,1,0:T(8,128)(2,1)}, u32[]{:S(2)}) copy-start(bf16[3,128,512]{2,1,0:T(8,128)(2,1)} %get-tuple-element.72) | copy-start | bytes 1179652
  161.4 3.3 %copy-start.1 = (bf16[3,128,512]{2,1,0:T(8,128)(2,1)S(1)}, bf16[3,128,512]{2,1,0:T(8,128)(2,1)}, u32[]{:S(2)}) copy-start(bf16[3,128,512]{2,1,0:T(8,128)(2,1)} %get-tuple-element.73) | copy-start | bytes 1179652

commit v3 on v2

v3 whole, which is shorter than its diff:
```python
import functools
import types

import jax
import jax.numpy as jnp
from jax import lax
from jax.experimental import pallas as pl
from jax.experimental.pallas import tpu as pltpu
from jax.sharding import PartitionSpec as P

HEAD = 64
EPSILON = 1e-06
MESH = pl.DeviceIdType.MESH
ROWS = 16
LOW = jnp.bfloat16
WIDE = jnp.float32
VECTORS = 16

UNIT_ORDERS = ("cxyz", "cyxz", "cxyz", "cyxz", "cxyz", "cxyz", "cyxz", "cxyz", "cyxz")
OWN_ORDERS = ("zx", "xz", "zx")
SUM_ORDER = "cxyz"
POLLS = (
    (),
    (),
    (),
    (),
    (0, 1,),
    (2, 3,),
    (),
    (),
    (),
    (0,),
    (1,),
    (),
    (2, 3,),
    (),
    (8, 0,),
    (4, 5,),
    (1, 6, 7, 3,),
    (2, 0,),
    (4,),
    (8, 1,),
    (3, 5, 6, 2,),
    (4, 0, 7,),
    (8,),
    (9, 5, 6, 1,),
    (3, 0,),
    (2, 7,),
    (9, 4,),
    (8, 1, 5, 3,),
    (2, 6,),
    (9, 7, 0, 4,),
    (8, 1, 12,),
    (10, 11, 5, 2, 0, 6, 1, 3, 8, 12,),
    (9, 2,),
    (3, 7, 11, 4, 10, 6, 5, 11, 8, 12, 4, 8, 10, 4, 9, 5, 9, 7, 11, 5, 10, 12, 6, 6, 7, 11, 12, 7, 11, 10, 10,),
)


def stages_of(sizes):
    rest, step, far = sizes["dp"] // 2, 2, []
    while rest > 1:
        radix = 4 if rest % 4 == 0 else 2
        far.append(("dp", step, radix))
        step *= radix
        rest //= radix
    return {"c": [("blk", 1, 2)], "y": [("blk", 2, 2)], "x": [("dp", 1, 2)], "z": far}


def bits_of(sizes, letters):
    bits = []
    for letter in letters:
        for axis, step, radix in stages_of(sizes)[letter]:
            bits += [(axis, step, 2)] if radix == 2 else [(axis, step, 2), (axis, 2 * step, 2)]
    return bits


def digit_of(stage):
    axis, step, radix = stage
    index = lax.axis_index(axis)
    digit = lax.rem(lax.div(index, step), radix)
    others = []
    for offset in range(1, radix):
        other = lax.rem(digit + offset, radix)
        others.append((other, {axis: index + (other - digit) * step}))
    return digit, others


def flip(index, step):
    return index + step - 2 * step * lax.rem(lax.div(index, step), 2)


def aligned(start, unit):
    return start if isinstance(start, int) else pl.multiple_of(start, unit)


def span(start, count, unit=ROWS):
    return pl.ds(aligned(start, unit), count)


def send(src, dst, sems, at, peer, land_at=None):
    sends, receives = sems
    copy = pltpu.make_async_remote_copy(
        src_ref=src,
        dst_ref=dst,
        send_sem=sends.at[at],
        recv_sem=receives.at[at if land_at is None else land_at],
        device_id=peer,
        device_id_type=MESH,
    )
    copy.start()
    return copy


def plan_of(sizes, rows, letters):
    plan = []
    size = rows
    for letter in letters:
        for axis, step, radix in stages_of(sizes)[letter]:
            if size % (radix * ROWS) == 0:
                size //= radix
                plan.append(((axis, step, radix), True, size))
                continue
            bit = step
            while bit < step * radix:
                split = size % (2 * ROWS) == 0
                size = size // 2 if split else size
                plan.append(((axis, bit, 2), split, size))
                bit *= 2
    return plan


def landing_rows(sizes, rows, letters):
    return sum(size * (stage[2] - 1) for stage, _, size in plan_of(sizes, rows, letters))


def semaphores_of(sizes, rows, letters):
    return 2 * sum(stage[2] - 1 for stage, _, _ in plan_of(sizes, rows, letters))


def add_rows(first, first_at, land, land_at, terms, out, out_at, count):
    chunk = 64 if count % 64 == 0 else (32 if count % 32 == 0 else 16)

    def body(step, carry):
        shift = step * chunk
        total = first[span(first_at + shift, chunk)].astype(WIDE)
        for term in range(terms):
            total = total + land[span(land_at + term * count + shift, chunk)].astype(WIDE)
        out[span(out_at + shift, chunk)] = total.astype(out.dtype)
        return carry

    if count == chunk:
        body(0, 0)
    else:
        lax.fori_loop(0, count // chunk, body, 0)


def reduce_rows(sizes, work, land, out, sems, base, rows, land_at, sem_at, letters, pending):
    plan = plan_of(sizes, rows, letters)
    start = base
    trail = []
    for level, (stage, split, count) in enumerate(plan):
        digit, others = digit_of(stage)
        keep = start + digit * count if split else start
        copies = []
        for offset, (other, peer) in enumerate(others):
            give = start + other * count if split else start
            slot = len(others) - 1 - offset
            copies.append(
                send(
                    work.at[span(give, count)],
                    land.at[span(land_at + slot * count, count)],
                    sems,
                    sem_at + offset,
                    peer,
                    sem_at + slot,
                )
            )
        yield
        for copy in copies:
            copy.wait_recv()
        if split:
            pending.extend(copies)
            trail.append((others, keep, count))
        else:
            for copy in copies:
                copy.wait_send()
        target = out if level == len(plan) - 1 else work
        add_rows(work, keep, land, land_at, len(others), target, keep, count)
        land_at += count * len(others)
        sem_at += len(others)
        start = keep
    for others, mine, count in reversed(trail):
        part = out.at[span(mine, count)]
        copies = [
            send(part, part, sems, sem_at + offset, peer, sem_at + len(others) - 1 - offset)
            for offset, (_, peer) in enumerate(others)
        ]
        yield
        for copy in copies:
            copy.wait_recv()
        pending.extend(copies)
        sem_at += len(others)


def reduce_whole(steps, land, sems, sem_at, bits):
    for level, bit in enumerate(bits):
        copy = send(steps.at[level], land.at[level], sems, sem_at + level, digit_of(bit)[1][0][1])
        yield
        copy.wait()
        steps[level + 1] = steps[level] + land[level]


def share_blocks(slots, sems, sem_at, me, pending):
    near, far = flip(me, 1), flip(me, 2)
    across = send(slots.at[me], slots.at[me], sems, sem_at, {"blk": far})
    beside = send(slots.at[me], slots.at[me], sems, sem_at + 1, {"blk": near})
    yield
    across.wait_recv()
    onward = send(slots.at[far], slots.at[far], sems, sem_at + 2, {"blk": near})
    yield
    beside.wait_recv()
    onward.wait_recv()
    pending.extend([across, beside, onward])


def by_rows(total, chunk, body, carry=0):
    def step(index, held):
        return body(pl.multiple_of(index * chunk, chunk), held)

    return lax.fori_loop(0, total // chunk, step, carry)


def dot(left, right):
    return jnp.dot(left, right, preferred_element_type=WIDE)


def dot_right_t(left, right):
    return lax.dot_general(left, right, (((1,), (1,)), ((), ())), preferred_element_type=WIDE)


def dot_left_t(left, right):
    return lax.dot_general(left, right, (((0,), (0,)), ((), ())), preferred_element_type=WIDE)


def fold(values):
    rows, width = values.shape
    return jnp.sum(values.reshape(rows // 8, 8, width), axis=0)


def mean_of(values):
    return jnp.mean(values, axis=-1, keepdims=True)


def norm_back(upstream, scaled, inverse, gain):
    inner = upstream * gain
    return inverse * (inner - mean_of(inner) - scaled * mean_of(inner * scaled))


def layout_of(sizes, seqs, rows, width, hidden):
    tokens = seqs * rows
    blocks = sizes["blk"]
    length = rows * blocks
    own = width // blocks
    heads = own // HEAD
    levels = len(bits_of(sizes, SUM_ORDER))
    units = 2 * (hidden // width) + 1
    land_total = sum(landing_rows(sizes, width, UNIT_ORDERS[at]) for at in range(units))
    own_land = max(landing_rows(sizes, width, order) for order in OWN_ORDERS)
    return dict(
        x_all=((seqs, length, width), LOW),
        x_own=((seqs, rows, width), LOW),
        cot=((seqs, rows, width), LOW),
        w_qkv=((width, 3 * own), LOW),
        w_o=((width, width), LOW),
        w_up=((width, hidden), LOW),
        w_down=((hidden, width), LOW),
        vec_low=((VECTORS * width,), LOW),
        vec=((VECTORS, width), WIDE),
        flags=((blocks, 8, rows), WIDE),
        qkv=((seqs, length, 3 * own), LOW),
        probs=((seqs * heads, length, length), LOW),
        o_wide=((seqs, length, own), WIDE),
        o_send=((seqs, length, own), LOW),
        o_all=((seqs, rows, width), LOW),
        total=((tokens, width), WIDE),
        scaled=((tokens, width), WIDE),
        inverse=((tokens, 128), WIDE),
        normed=((tokens, width), WIDE),
        normed_low=((tokens, width), LOW),
        active=((tokens, hidden), LOW),
        slope=((tokens, hidden), WIDE),
        hid=((seqs, rows, width), LOW),
        grad_b=((tokens, width), WIDE),
        grad_y=((tokens, width), LOW),
        grad_z=((tokens, hidden), LOW),
        grad_t=((tokens, width), LOW),
        do_send=((seqs, rows, width), LOW),
        do_all=((seqs, length, own), LOW),
        grad_s=((heads, length, length), LOW),
        d_qkv=((seqs, length, 3 * own), LOW),
        dx_part=((seqs, length, width), LOW),
        dx_near=((seqs, 2, rows, width), LOW),
        dx_chip=((seqs, rows, width), LOW),
        dx_far=((seqs, rows, width), LOW),
        dx=((seqs, rows, width), LOW),
        work=((units * width, width), LOW),
        land=((land_total, width), LOW),
        out=((units * width, width), LOW),
        own_work=((3, width, own), LOW),
        own_land=((3, own_land, own), LOW),
        own_out=((3, blocks, width, own), LOW),
        steps=((levels + 1, VECTORS, width), WIDE),
        vec_land=((levels, VECTORS, width), WIDE),
    )


def layer_kernel(sizes, names, *refs):
    x, lengths, mask, wq, wk, wv, wo, wu, wd, cotangent = refs[:10]
    vectors_in = refs[10:19]
    hid_out, dx_out, sums_out, own_sums_out, vec_out = refs[19:24]
    r = types.SimpleNamespace(**dict(zip(names, refs[24:-3], strict=True)))
    sems = refs[-3:-1]
    local = refs[-1]
    x_all, qkv, vec, steps = r.x_all, r.qkv, r.vec, r.steps
    seqs, rows, width = r.x_own.shape
    tokens = seqs * rows
    length = x_all.shape[1]
    blocks = sizes["blk"]
    own = width // blocks
    heads = own // HEAD
    hidden = r.w_up.shape[1]
    tiles = hidden // width
    scale = HEAD ** (-0.5)
    me = lax.axis_index("blk")
    near, far = flip(me, 1), flip(me, 2)
    cross = flip(far, 1)
    peers = (near, far, cross)
    place = lambda index: span(index * rows, rows, rows)
    lanes = lambda index: span(index * own, own, own)

    used = {"sem": 0, "local": 0}
    pending, stores = [], []

    def slot(count=1):
        at = used["sem"]
        used["sem"] += count
        return at

    def fetch(src, dst):
        copy = pltpu.make_async_copy(src, dst, local.at[used["local"]])
        used["local"] += 1
        copy.start()
        return copy

    loads_x = [
        fetch(x, x_all.at[:, place(me), :]),
        fetch(x, r.x_own),
    ]
    loads_w = [
        fetch(weight.at[:, lanes(me)], r.w_qkv.at[:, pl.ds(at * own, own)])
        for at, weight in enumerate((wq, wk, wv))
    ]
    load_vectors = []
    at = 0
    for vector in vectors_in:
        count = vector.shape[0]
        load_vectors.append(fetch(vector, r.vec_low.at[pl.ds(at, count)]))
        at += count
    load_o = fetch(wo, r.w_o)
    load_up = fetch(wu, r.w_up)
    load_down = fetch(wd, r.w_down)
    load_cot = fetch(cotangent, r.cot)

    positions = me * rows + lax.broadcasted_iota(jnp.int32, (1, rows), 1)
    flag_rows = []
    for seq in range(seqs):
        good = (mask[seq : seq + 1, :] == 1) & (positions < lengths[seq])
        flag_rows.append(jnp.where(good, 0.0, -1000000000.0).astype(WIDE))
    flag_rows.append(jnp.zeros((8 - seqs, rows), WIDE))
    r.flags[me] = jnp.concatenate(flag_rows, axis=0)

    barrier = pltpu.get_barrier_semaphore()
    greeted = [{"blk": peer} for peer in peers] + [
        peer for letter in "xz" for stage in stages_of(sizes)[letter] for _, peer in digit_of(stage)[1]
    ]
    for peer in greeted:
        pl.semaphore_signal(barrier, inc=1, device_id=peer, device_id_type=MESH)
    pl.semaphore_wait(barrier, len(greeted))

    at_far, at_near, at_on, at_flag = slot(seqs), slot(seqs), slot(seqs), slot(len(peers))
    flag_copies = [
        send(r.flags.at[me], r.flags.at[me], sems, at_flag + index, {"blk": peer})
        for index, peer in enumerate(peers)
    ]
    x_far, x_near, x_on = [], [], []
    for seq in range(seqs):
        target = x_all.at[seq, place(me), :]
        x_far.append(send(x.at[seq], target, sems, at_far + seq, {"blk": far}))
        x_near.append(send(x.at[seq], target, sems, at_near + seq, {"blk": near}))
    pending += flag_copies + x_far + x_near

    def forward_x(seq):
        x_far[seq].wait_recv()
        block = x_all.at[seq, place(far), :]
        x_on.append(send(block, block, sems, at_on + seq, {"blk": near}))

    lane = lax.broadcasted_iota(jnp.int32, (1, own), 1)
    of_head = [(lane >= head * HEAD) & (lane < (head + 1) * HEAD) for head in range(heads)]
    only = lambda values, head: jnp.where(of_head[head], values.astype(WIDE), 0.0)
    for copy in load_vectors:
        copy.wait()
    for at in range(8 + tiles):
        vec[at : at + 1, :] = r.vec_low[at * width : (at + 1) * width].astype(WIDE).reshape(1, width)
    bias_q = vec[0:1, lanes(me)]
    bias_v = vec[1:2, lanes(me)]
    bias_qkv = jnp.concatenate([bias_q, jnp.zeros_like(bias_q), bias_v], axis=1)
    o_all, o_send = r.o_all, r.o_send
    at_o = slot(seqs * len(peers))
    o_copies = []

    def project(seq):
        def body(at, carry):
            made = dot(x_all[seq, pl.ds(at, 256), :], r.w_qkv[...]) + bias_qkv
            qkv[seq, pl.ds(at, 256), :] = made.astype(LOW)
            return carry

        by_rows(length, 256, body)

    def attend(seq):
        keys = qkv[seq, :, own : 2 * own]
        values = qkv[seq, :, 2 * own :]
        key_bias = jnp.concatenate([r.flags[block, seq : seq + 1, :] for block in range(blocks)], axis=1)
        column = lax.broadcasted_iota(jnp.int32, (128, length), 1)
        row = lax.broadcasted_iota(jnp.int32, (128, length), 0)

        def body(at, carry):
            query = qkv[seq, pl.ds(at, 128), 0:own].astype(WIDE) * scale
            bias = jnp.where(column == row + at, 0.0, key_bias)
            joined = None
            for head in range(heads):
                scores = dot_right_t(only(query, head).astype(LOW), keys) + bias
                raised = jnp.exp(scores - jnp.max(scores, axis=-1, keepdims=True))
                probs = (raised / jnp.sum(raised, axis=-1, keepdims=True)).astype(LOW)
                r.probs[seq * heads + head, pl.ds(at, 128), :] = probs
                result = dot(probs, values)
                joined = result if joined is None else jnp.where(of_head[head], result, joined)
            r.o_wide[seq, pl.ds(at, 128), :] = joined
            o_send[seq, pl.ds(at, 128), :] = joined.astype(LOW)
            return carry

        by_rows(length, 128, body)
        for index, peer in enumerate(peers):
            o_copies.append(
                send(
                    o_send.at[seq, place(peer), :],
                    o_all.at[seq, :, lanes(me)],
                    sems,
                    at_o + seq * len(peers) + index,
                    {"blk": peer},
                )
            )
        o_all[seq, :, lanes(me)] = o_send[seq, place(me), :]

    for copy in loads_w:
        copy.wait()
    for copy in loads_x:
        copy.wait()
    for copy in flag_copies:
        copy.wait_recv()
    forward_x(0)
    for seq in range(seqs):
        x_near[seq].wait_recv()
        x_on[seq].wait_recv()
        project(seq)
        if seq + 1 < seqs:
            forward_x(seq + 1)
        attend(seq)
    pending += x_on + o_copies

    total, scaled, inverse = r.total, r.scaled, r.inverse
    normed, normed_low = r.normed, r.normed_low
    wide_row = lambda at: vec[at : at + 1, :]
    load_o.wait()
    for copy in o_copies:
        copy.wait_recv()
    flat = lambda ref, at, count: ref[lax.div(at, rows), span(lax.rem(at, rows), count), :]

    total[...] = dot(o_all[...].reshape(tokens, width), r.w_o[...])

    def first_norm(at, carry):
        part = pl.ds(at, 32)
        values = flat(r.x_own, at, 32).astype(WIDE) + total[part, :] + wide_row(2)
        center = values - mean_of(values)
        inv = lax.rsqrt(mean_of(center * center) + EPSILON)
        made = center * inv
        scaled[part, :] = made
        inverse[part, :] = jnp.broadcast_to(inv, (32, 128))
        result = made * wide_row(3) + wide_row(4)
        normed[part, :] = result
        normed_low[part, :] = result.astype(LOW)
        return carry

    by_rows(tokens, 32, first_norm)

    load_up.wait()
    active, slope = r.active, r.slope

    def up(tile, carry):
        columns = span(tile * width, width, width)
        total[...] = dot(normed_low[...], r.w_up[:, columns])
        offset = vec[pl.ds(8 + tile, 1), :]

        def bend(at, held):
            part = pl.ds(at, 32)
            z = total[part, :] + offset
            below = 0.5 * (1.0 + lax.erf(z * 0.7071067811865476))
            active[part, columns] = (z * below).astype(LOW)
            slope[part, columns] = below + z * (0.3989422804014327 * jnp.exp(-0.5 * z * z))
            return held

        by_rows(tokens, 32, bend)
        return carry

    lax.fori_loop(0, tiles, up, 0)
    load_down.wait()
    load_cot.wait()
    total[...] = dot(active[...], r.w_down[...])

    grad_b, grad_y = r.grad_b, r.grad_y
    zero = jnp.zeros((8, width), WIDE)

    def second_norm(at, sums):
        shift_sum, gain_sum, down_sum = sums
        part = pl.ds(at, 32)
        values = normed[part, :] + total[part, :] + wide_row(5)
        center = values - mean_of(values)
        inv = lax.rsqrt(mean_of(center * center) + EPSILON)
        made = center * inv
        r.hid[lax.div(at, rows), span(lax.rem(at, rows), 32), :] = (made * wide_row(6) + wide_row(7)).astype(LOW)
        upstream = flat(r.cot, at, 32).astype(WIDE)
        back = norm_back(upstream, made, inv, wide_row(6))
        grad_b[part, :] = back
        rounded = back.astype(LOW)
        grad_y[part, :] = rounded
        return shift_sum + fold(upstream), gain_sum + fold(upstream * made), down_sum + fold(rounded.astype(WIDE))

    shift_sum, gain_sum, down_sum = by_rows(tokens, 32, second_norm, (zero, zero, zero))
    stores.append(fetch(r.hid, hid_out))
    total_row = lambda values: jnp.sum(values, axis=0, keepdims=True)
    steps[0] = jnp.zeros((VECTORS, width), WIDE)
    steps[0, 7:8, :] = total_row(shift_sum)
    steps[0, 6:7, :] = total_row(gain_sum)
    steps[0, 5:6, :] = total_row(down_sum)

    work = r.work
    running = {}
    place_of = {"land": 0, "poll": 0}

    def launch(name, item):
        running[name] = item
        advance(name)

    def advance(name):
        if name in running and next(running[name], True) is not None:
            del running[name]

    def launch_unit(unit):
        letters = UNIT_ORDERS[unit]
        at = slot(semaphores_of(sizes, width, letters))
        land_at = place_of["land"]
        place_of["land"] += landing_rows(sizes, width, letters)
        launch(
            unit,
            reduce_rows(sizes, work, r.land, r.out, sems, unit * width, width, land_at, at, letters, pending),
        )

    def launch_own(kind):
        letters = OWN_ORDERS[kind]
        at = slot(semaphores_of(sizes, width, letters))
        blocks_at = slot(3)
        slots = r.own_out.at[kind]

        def item():
            parts = r.own_work.at[kind], r.own_land.at[kind], slots.at[me]
            yield from reduce_rows(sizes, *parts, sems, 0, width, 0, at, letters, pending)
            yield from share_blocks(slots, sems, blocks_at, me, pending)

        launch(2 * tiles + 1 + kind, item())

    def poll():
        at = place_of["poll"]
        place_of["poll"] += 1
        for name in POLLS[at] if at < len(POLLS) else ():
            advance(name)

    cut = lambda tile: slice(tile * width, (tile + 1) * width)
    for tile in range(tiles):
        work[cut(tile), :] = dot_left_t(active[:, cut(tile)], grad_y[...]).astype(LOW)
        launch_unit(tile)
        poll()

    grad_z = r.grad_z

    for tile in range(tiles):
        total[...] = dot_right_t(grad_y[...], r.w_down[cut(tile), :])

        def bend(at, held):
            part = pl.ds(at, 32)
            made = (total[part, :] * slope[part, cut(tile)]).astype(LOW)
            grad_z[part, cut(tile)] = made
            return held + fold(made.astype(WIDE))

        steps[0, 8 + tile : 9 + tile, :] = total_row(by_rows(tokens, 32, bend, zero))
        poll()
    total[...] = dot_right_t(grad_z[...], r.w_up[...])
    poll()

    grad_t = r.grad_t

    def first_back(at, sums):
        shift_part, gain_part, out_part = sums
        part = pl.ds(at, 32)
        upstream = grad_b[part, :] + total[part, :]
        made = scaled[part, :]
        back = norm_back(upstream, made, inverse[part, 0:1], wide_row(3))
        grad_b[part, :] = back
        rounded = back.astype(LOW)
        grad_t[part, :] = rounded
        return shift_part + fold(upstream), gain_part + fold(upstream * made), out_part + fold(rounded.astype(WIDE))

    shift_part, gain_part, out_part = by_rows(tokens, 32, first_back, (zero, zero, zero))
    steps[0, 4:5, :] = total_row(shift_part)
    steps[0, 3:4, :] = total_row(gain_part)
    steps[0, 2:3, :] = total_row(out_part)
    poll()

    do_send, do_all = r.do_send, r.do_all
    at_do = slot(seqs * len(peers))
    do_copies = []
    made = dot_right_t(grad_t[...], r.w_o[...]).astype(LOW)
    do_send[...] = made.reshape(seqs, rows, width)
    for seq in range(seqs):
        do_copies.append(
            [
                send(
                    do_send.at[seq, :, lanes(peer)],
                    do_all.at[seq, place(me), :],
                    sems,
                    at_do + seq * len(peers) + index,
                    {"blk": peer},
                )
                for index, peer in enumerate(peers)
            ]
        )
        do_all[seq, place(me), :] = do_send[seq, :, lanes(me)]
        pending += do_copies[-1]

    poll()
    work[2 * hidden :, :] = dot_left_t(o_all[...].reshape(tokens, width), grad_t[...]).astype(LOW)
    launch_unit(2 * tiles)
    poll()
    for tile in range(tiles):
        work[cut(tiles + tile), :] = dot_left_t(normed_low[...], grad_z[:, cut(tile)]).astype(LOW)
        launch_unit(tiles + tile)
        poll()

    d_qkv, grad_s, dx_part = r.d_qkv, r.grad_s, r.dx_part
    at_dx_near, at_dx_far = slot(2 * seqs), slot(seqs)
    dx_near, dx_far = [], []

    def value_back(seq):
        upstream = do_all[seq].astype(WIDE)
        grads = [
            dot_left_t(r.probs[seq * heads + head], only(upstream, head).astype(LOW)) for head in range(heads)
        ]
        d_qkv[seq, :, 2 * own :] = functools.reduce(jnp.add, grads).astype(LOW)

    def score_back(seq):
        values = qkv[seq, :, 2 * own :]

        def body(at, carry):
            upstream = do_all[seq, pl.ds(at, 128), :].astype(WIDE)
            inner = upstream * r.o_wide[seq, pl.ds(at, 128), :]
            for head in range(heads):
                delta = jnp.sum(jnp.where(of_head[head], inner, 0.0), axis=-1, keepdims=True)
                prob_grad = dot_right_t(only(upstream, head).astype(LOW), values)
                probs = r.probs[seq * heads + head, pl.ds(at, 128), :].astype(WIDE)
                grad_s[head, pl.ds(at, 128), :] = (probs * (prob_grad - delta)).astype(LOW)
            return carry

        by_rows(length, 128, body)

    def query_key_back(seq):
        queries_wide = qkv[seq, :, 0:own].astype(WIDE) * scale
        keys_wide = qkv[seq, :, own : 2 * own].astype(WIDE) * scale
        query_grads, key_grads = [], []
        for head in range(heads):
            query_grads.append(dot(grad_s[head], only(keys_wide, head).astype(LOW)))
            key_grads.append(dot_left_t(grad_s[head], only(queries_wide, head).astype(LOW)))
        d_qkv[seq, :, 0:own] = functools.reduce(jnp.add, query_grads).astype(LOW)
        d_qkv[seq, :, own : 2 * own] = functools.reduce(jnp.add, key_grads).astype(LOW)

    def input_back(seq):
        def partial(at, carry):
            dx_part[seq, pl.ds(at, 128), :] = dot_right_t(d_qkv[seq, pl.ds(at, 128), :], r.w_qkv[...]).astype(LOW)
            return carry

        by_rows(length, 128, partial)
        dx_near.append(
            [
                send(dx_part.at[seq, place(block), :], r.dx_near.at[seq, at], sems, at_dx_near + 2 * seq + at, {"blk": near})
                for at, block in enumerate((near, cross))
            ]
        )
        pending.extend(dx_near[-1])

    def own_grad(columns):
        tokens_in = x_all[...].reshape(seqs * length, width)
        return dot_left_t(tokens_in, d_qkv[:, :, columns].reshape(seqs * length, -1)).astype(LOW)

    def hand_on(seq):
        dx_near[seq][1].wait_recv()

        def body(at, carry):
            part = pl.ds(at, 32)
            summed = dx_part[seq, span(far * rows + at, 32), :].astype(WIDE) + r.dx_near[seq, 1, part, :].astype(WIDE)
            r.dx_chip[seq, part, :] = summed.astype(LOW)
            return carry

        by_rows(rows, 32, body)
        dx_far.append(send(r.dx_chip.at[seq], r.dx_far.at[seq], sems, at_dx_far + seq, {"blk": far}))
        pending.append(dx_far[-1])

    for seq in range(seqs):
        for copy in do_copies[seq]:
            copy.wait_recv()
        value_back(seq)
        poll()
    r.own_work[0] = own_grad(slice(2 * own, None))
    launch_own(0)
    poll()
    for seq in range(seqs):
        score_back(seq)
        poll()
        query_key_back(seq)
        poll()
        input_back(seq)
        poll()
        if seq > 0:
            hand_on(seq - 1)
    made = own_grad(slice(0, 2 * own))
    r.own_work[1] = made[:, :own]
    launch_own(1)
    r.own_work[2] = made[:, own:]
    launch_own(2)
    hand_on(seqs - 1)

    def offsets(at, sums):
        part = d_qkv[lax.div(at, length), span(lax.rem(at, length), 128), :]
        return sums + fold(part.astype(WIDE))

    sums = total_row(by_rows(seqs * length, 128, offsets, jnp.zeros((8, 3 * own), WIDE)))
    steps[0, 0:1, lanes(me)] = sums[:, 0:own]
    steps[0, 1:2, lanes(me)] = sums[:, 2 * own :]
    sum_bits = bits_of(sizes, SUM_ORDER)
    launch(2 * tiles + 4, reduce_whole(steps, r.vec_land, sems, slot(len(sum_bits)), sum_bits))
    poll()

    for seq in range(seqs):
        dx_near[seq][0].wait_recv()
        dx_far[seq].wait_recv()

        def finish(at, carry):
            part = pl.ds(at, 32)
            summed = grad_b[span(seq * rows + at, 32), :] + dx_part[seq, span(me * rows + at, 32), :].astype(WIDE)
            summed = summed + r.dx_near[seq, 0, part, :].astype(WIDE) + r.dx_far[seq, part, :].astype(WIDE)
            r.dx[seq, part, :] = summed.astype(LOW)
            return carry

        by_rows(rows, 32, finish)
        poll()
    stores.append(fetch(r.dx, dx_out))

    for name in sum(POLLS[place_of["poll"] :], ()):
        advance(name)
    while running:
        for name in list(running):
            advance(name)
    vec_out[...] = steps[len(sum_bits)]
    stores.append(fetch(r.out, sums_out))
    stores.append(fetch(r.own_out, own_sums_out))
    for copy in pending:
        copy.wait_send()
    for copy in stores:
        copy.wait()


def widen_kernel(blocks, hid, dx, sums, shared, vec, *refs):
    hid_out, dx_out, wq, wk, wv, wo, wu, wd = refs[:8]
    rows_out, bu = refs[8:16], refs[16]
    low, shared_low, wide, shared_wide, hid_low, dx_low, sems = refs[17:]
    width = wq.shape[0]
    own = width // blocks
    units = low.shape[0] // width
    tiles = (units - 1) // 2
    used = [0]

    def copy(src, dst):
        made = pltpu.make_async_copy(src, dst, sems.at[used[0]])
        used[0] += 1
        made.start()
        return made

    unit = lambda ref, at: ref.at[pl.ds(at * width, width)]
    loads = [copy(unit(sums, at), unit(low, at)) for at in range(units)]
    load_shared = copy(shared, shared_low)
    token_loads = [copy(hid, hid_low), copy(dx, dx_low)]
    stores = []
    targets = (
        [unit(wd, at) for at in range(tiles)] + [wu.at[:, pl.ds(at * width, width)] for at in range(tiles)] + [wo]
    )
    for at, row in enumerate(rows_out):
        row[...] = vec[at, :]
    for at in range(tiles):
        bu[at * width : (at + 1) * width] = vec[len(rows_out) + at, :]
    for at in range(units):
        loads[at].wait()

        def body(step, carry):
            part = span(at * width + step * 64, 64)
            wide[part, :] = low[part, :].astype(WIDE)
            return carry

        lax.fori_loop(0, width // 64, body, 0)
        stores.append(copy(unit(wide, at), targets[at]))
    for load in token_loads:
        load.wait()
    stores += [copy(hid_low, hid_out), copy(dx_low, dx_out)]
    load_shared.wait()
    for kind, target in enumerate((wv, wq, wk)):

        def body(step, carry):
            part = span(step * 64, 64)
            for block in range(blocks):
                shared_wide[kind, part, block * own : (block + 1) * own] = shared_low[kind, block, part, :].astype(WIDE)
            return carry

        lax.fori_loop(0, width // 64, body, 0)
        stores.append(copy(shared_wide.at[kind], target))
    for made in stores:
        made.wait()


def on_device(
    sizes,
    hidden_input,
    lengths,
    key_mask,
    query_weight,
    query_offset,
    key_weight,
    value_weight,
    value_offset,
    output_weight,
    output_offset,
    mixer_gain,
    mixer_shift,
    up_weight,
    up_offset,
    down_weight,
    down_offset,
    final_gain,
    final_shift,
    cotangent,
):
    seqs, rows, width = hidden_input.shape
    hidden = up_weight.shape[1]
    blocks = sizes["blk"]
    own = width // blocks
    scratch = layout_of(sizes, seqs, rows, width, hidden)
    anywhere = pl.BlockSpec(memory_space=pl.ANY)
    inside = pl.BlockSpec(memory_space=pltpu.VMEM)
    scalars = pl.BlockSpec(memory_space=pltpu.SMEM)
    scratch_shape = types.SimpleNamespace(**{name: shape for name, (shape, _) in scratch.items()})
    units = scratch_shape.work
    shared = scratch_shape.own_out
    hid, dx, sums, own_sums, vec_sums = pl.pallas_call(
        functools.partial(layer_kernel, sizes, tuple(scratch)),
        out_shape=(
            jax.ShapeDtypeStruct(hidden_input.shape, LOW),
            jax.ShapeDtypeStruct(hidden_input.shape, LOW),
            jax.ShapeDtypeStruct(units, LOW),
            jax.ShapeDtypeStruct(shared, LOW),
            jax.ShapeDtypeStruct((VECTORS, width), WIDE),
        ),
        in_specs=[anywhere, scalars, inside] + [anywhere] * 16,
        out_specs=(anywhere, anywhere, anywhere, anywhere, inside),
        scratch_shapes=[pltpu.VMEM(shape, kind) for shape, kind in scratch.values()]
        + [
            pltpu.SemaphoreType.DMA((256,)),
            pltpu.SemaphoreType.DMA((256,)),
            pltpu.SemaphoreType.DMA((32,)),
        ],
        compiler_params=pltpu.CompilerParams(
            collective_id=0, has_side_effects=True, vmem_limit_bytes=60 * 1024 * 1024
        ),
    )(
        hidden_input,
        lengths,
        key_mask,
        query_weight,
        key_weight,
        value_weight,
        output_weight,
        up_weight,
        down_weight,
        cotangent,
        query_offset,
        value_offset,
        output_offset,
        mixer_gain,
        mixer_shift,
        down_offset,
        final_gain,
        final_shift,
        up_offset,
    )
    full = jax.ShapeDtypeStruct((width, width), WIDE)
    row = jax.ShapeDtypeStruct((width,), WIDE)
    flat = jax.ShapeDtypeStruct(hidden_input.shape, LOW)
    final = pl.pallas_call(
        functools.partial(widen_kernel, blocks),
        out_shape=(
            flat,
            flat,
            full,
            full,
            full,
            full,
            jax.ShapeDtypeStruct((width, hidden), WIDE),
            jax.ShapeDtypeStruct((hidden, width), WIDE),
        )
        + (row,) * 8
        + (jax.ShapeDtypeStruct((hidden,), WIDE),),
        in_specs=[anywhere] * 4 + [inside],
        out_specs=(anywhere,) * 8 + (inside,) * 9,
        scratch_shapes=[
            pltpu.VMEM(units, LOW),
            pltpu.VMEM(shared, LOW),
            pltpu.VMEM(units, WIDE),
            pltpu.VMEM((3, width, width), WIDE),
            pltpu.VMEM(hidden_input.shape, LOW),
            pltpu.VMEM(hidden_input.shape, LOW),
            pltpu.SemaphoreType.DMA((2 * units[0] // width + 12,)),
        ],
        compiler_params=pltpu.CompilerParams(vmem_limit_bytes=60 * 1024 * 1024),
    )(hid, dx, sums, own_sums, vec_sums)
    hid, dx, wq, wk, wv, wo, wu, wd, bq, bv, bo, g1, s1, bd, g2, s2, bu = final
    return hid, dx, wq, bq, wk, wv, bv, wo, bo, g1, s1, wu, bu, wd, bd, g2, s2


def solution(mesh):
    split = P("dp", "blk", None)
    in_specs = (split, P("dp"), P("dp", "blk")) + (P(),) * 15 + (split,)
    out_specs = (split, split) + (P(),) * 15
    return jax.shard_map(
        functools.partial(on_device, dict(mesh.shape)),
        mesh=mesh,
        in_specs=in_specs,
        out_specs=out_specs,
        check_vma=False,
    )
```

time: 166 us -> 125 us (0.75)
  Pallas kernels: 142 us -> 122 us
  local copies, waits for them, and re-layouts: 14.4 us -> 0 us
  other arithmetic: 8.27 us -> 0 us
    pallas_call x1, Pallas kernels: 142 us -> 113 us  [on_device(): pl.pallas_call(functools.partial(layer_kernel, sizes, tuple(scratch)), ou...]
    unnamed x19 -> x0, local copies, waits for them, and re-layouts: 10.5 us -> none
    pallas_call x0 -> x1, Pallas kernels: none -> 8.88 us  [on_device(): pl.pallas_call(functools.partial(widen_kernel, blocks), out_shape=(flat,...]
    convert_element_type x2 -> x0, other arithmetic: 4.05 us -> none  [the longest x1 2.6 us: on_device(): wide = lambda at, count: sums[at:at + count].astype(WIDE)]
    concatenate x1 -> x0, other arithmetic: 2.55 us -> none  [on_device(): jnp.concatenate([wide(hidden + at, width) for at in range(0, hidden, widt...]
    slice x1 -> x0, other arithmetic: 1.66 us -> none  [on_device(): wide = lambda at, count: sums[at:at + count].astype(WIDE)]
where the time goes in v3:
time: 125 us; the launch traced here: 123 us
  Pallas kernels  122 us (98%)
    pallas_call x1, Pallas kernels, on_device(): pl.pallas_call(functools.partial(layer_kernel, sizes, tuple(scratch)), ou...  113 us
    pallas_call x1, Pallas kernels, on_device(): pl.pallas_call(functools.partial(widen_kernel, blocks), out_shape=(flat,...  8.88 us

profile of v3, /device:TPU:5, one launch (start us, length us, event | category | flops | bytes accessed | tf_op | source)
XLA Modules:
  0.0 122.9 jit_solution(2193187612450351843)
XLA Ops:
  0.7 113.2 %shard_map.314 = (bf16[3,128,512]{2,1,0:T(8,128)(2,1)}, bf16[3,128,512]{2,1,0:T(8,128)(2,1)}, bf16[4608,512]{1,0:T(8,128)(2,1)}, bf16[3,4,512,128]{3,2,1,0:T(8,128)(2,1)}, f32[16,512]{1,0:T(8,128)}) custom-call(bf16[3,128,512]{2,1,0:T(8,128)(2,1)} %refs_0_.1, s32[3]{0:T(128)} %refs_1_.1, s32[3,128]{1,0:T(4,128)} %refs_2_.1, bf16[512,512]{1,0:T(8,128)(2,1)} %refs_3_.1, ...), custom_call_target="tpu_custom_call" | custom-call | tf_op jit(solution)/shard_map/pallas_call | solution.py:888
  113.8 8.9 %shard_map.315 = (bf16[3,128,512]{2,1,0:T(8,128)(2,1)}, bf16[3,128,512]{2,1,0:T(8,128)(2,1)}, f32[512,512]{1,0:T(8,128)}, f32[512,512]{1,0:T(8,128)}, f32[512,51...) custom-call(bf16[3,128,512]{2,1,0:T(8,128)(2,1)} %get-tuple-element., ...), custom_call_target="tpu_custom_call" | custom-call | tf_op jit(solution)/shard_map/pallas_call | solution.py:932

commit v4 on v3

v4 whole, which is shorter than its diff:
```python
import functools
import types

import jax
import jax.numpy as jnp
from jax import lax
from jax.experimental import pallas as pl
from jax.experimental.pallas import tpu as pltpu
from jax.sharding import PartitionSpec as P

HEAD = 64
EPSILON = 1e-06
MESH = pl.DeviceIdType.MESH
ROWS = 16
LOW = jnp.bfloat16
WIDE = jnp.float32
VECTORS = 16
LOCALS = 32

UNIT_ORDERS = ("cyxz", "cxyz", "cyxz", "cayxb", "caxby", "cxyab", "caxyb", "czxy", "cxyab")
OWN_ORDERS = ("xab", "xz", "xz")
SUM_ORDER = "cxyab"
POLLS = (
    (),
    (),
    (),
    (),
    (),
    (0,),
    (1, 2,),
    (3,),
    (),
    (),
    (),
    (),
    (),
    (0,),
    (1, 8,),
    (4, 3, 5,),
    (6, 2, 7,),
    (0,),
    (),
    (8, 4,),
    (1,),
    (3, 5,),
    (6,),
    (2,),
    (9, 8,),
    (4,),
    (5, 3,),
    (7, 6, 0,),
    (1,),
    (9, 2, 8, 7,),
    (4, 5, 6, 12,),
    (10, 3, 0, 1,),
    (9, 11, 2, 12, 8,),
    (7, 5, 4, 6, 0, 1, 10, 3, 9, 12, 7, 2, 4, 11, 8, 5, 9, 6, 1, 0, 12, 3, 10, 7, 1, 0, 4, 8, 2, 5, 6, 9, 11, 2, 3, 10, 12, 4, 8, 6, 5, 11, 7, 9, 3, 8, 7, 9, 3, 10, 8, 4, 5, 10, 4, 11, 5, 6, 11, 6,),
)


def stages_of(sizes):
    def split(step, rest):
        found = []
        while rest > 1:
            radix = 4 if rest % 4 == 0 else 2
            found.append(("dp", step, radix))
            step *= radix
            rest //= radix
        return found

    dp = sizes["dp"]
    return dict(
        c=[("blk", 1, 2)], y=[("blk", 2, 2)], x=[("dp", 1, 2)], a=[("dp", 2, 2)], b=split(4, dp // 4), z=split(2, dp // 2)
    )


def bits_of(sizes, letters):
    bits = []
    for letter in letters:
        for axis, step, radix in stages_of(sizes)[letter]:
            bits += [(axis, step, 2)] if radix == 2 else [(axis, step, 2), (axis, 2 * step, 2)]
    return bits


def digit_of(stage):
    axis, step, radix = stage
    index = lax.axis_index(axis)
    digit = lax.rem(lax.div(index, step), radix)
    others = []
    for offset in range(1, radix):
        other = lax.rem(digit + offset, radix)
        others.append((other, {axis: index + (other - digit) * step}))
    return digit, others


def flip(index, step):
    return index + step - 2 * step * lax.rem(lax.div(index, step), 2)


def aligned(start, unit):
    return start if isinstance(start, int) else pl.multiple_of(start, unit)


def span(start, count, unit=ROWS):
    return pl.ds(aligned(start, unit), count)


def send(src, dst, sems, at, peer, land_at=None):
    sends, receives = sems
    copy = pltpu.make_async_remote_copy(
        src_ref=src,
        dst_ref=dst,
        send_sem=sends.at[at],
        recv_sem=receives.at[at if land_at is None else land_at],
        device_id=peer,
        device_id_type=MESH,
    )
    copy.start()
    return copy


def plan_of(sizes, rows, letters):
    plan = []
    size = rows
    for letter in letters:
        for axis, step, radix in stages_of(sizes)[letter]:
            if size % (radix * ROWS) == 0:
                size //= radix
                plan.append(((axis, step, radix), True, size))
                continue
            bit = step
            while bit < step * radix:
                split = size % (2 * ROWS) == 0
                size = size // 2 if split else size
                plan.append(((axis, bit, 2), split, size))
                bit *= 2
    return plan


def landing_rows(sizes, rows, letters):
    return sum(size * (stage[2] - 1) for stage, _, size in plan_of(sizes, rows, letters))


def semaphores_of(sizes, rows, letters):
    peers = [stage[2] - 1 for stage, _, _ in plan_of(sizes, rows, letters)]
    return max(peers), 2 * sum(peers)


def semaphore_counts(sizes, seqs, width):
    sends, receives = 3 + 6 * seqs + 1, 3 + 12 * seqs + len(bits_of(sizes, SUM_ORDER))
    for letters in UNIT_ORDERS:
        sending, receiving = semaphores_of(sizes, width, letters)
        sends, receives = sends + sending, receives + receiving
    for letters in OWN_ORDERS:
        sending, receiving = semaphores_of(sizes, width, letters)
        sends, receives = sends + max(sending, 3), receives + receiving + 3
    return sends, receives


def add_rows(first, first_at, land, land_at, terms, out, out_at, count):
    total = first[span(first_at, count)].astype(WIDE)
    for term in range(terms):
        total = total + land[span(land_at + term * count, count)].astype(WIDE)
    out[span(out_at, count)] = total.astype(out.dtype)


def reduce_rows(sizes, work, land, out, sems, base, rows, land_at, send_at, receive_at, letters, sent):
    plan = plan_of(sizes, rows, letters)
    start = base
    trail = []
    for level, (stage, split, count) in enumerate(plan):
        digit, others = digit_of(stage)
        keep = start + digit * count if split else start
        for copy in sent:
            copy.wait_send()
        sent.clear()
        for offset, (other, peer) in enumerate(others):
            give = start + other * count if split else start
            slot = len(others) - 1 - offset
            sent.append(
                send(
                    work.at[span(give, count)],
                    land.at[span(land_at + slot * count, count)],
                    sems,
                    send_at + offset,
                    peer,
                    receive_at + slot,
                )
            )
        yield
        for copy in sent:
            copy.wait_recv()
        if split:
            trail.append((others, keep, count))
        else:
            for copy in sent:
                copy.wait_send()
            sent.clear()
        target = out if level == len(plan) - 1 else work
        add_rows(work, keep, land, land_at, len(others), target, keep, count)
        land_at += count * len(others)
        receive_at += len(others)
        start = keep
    for others, mine, count in reversed(trail):
        part = out.at[span(mine, count)]
        for copy in sent:
            copy.wait_send()
        sent.clear()
        for offset, (_, peer) in enumerate(others):
            sent.append(send(part, part, sems, send_at + offset, peer, receive_at + len(others) - 1 - offset))
        yield
        for copy in sent:
            copy.wait_recv()
        receive_at += len(others)


def reduce_whole(steps, land, sems, send_at, receive_at, bits):
    for level, bit in enumerate(bits):
        copy = send(steps.at[level], land.at[level], sems, send_at, digit_of(bit)[1][0][1], receive_at + level)
        yield
        copy.wait()
        steps[level + 1] = steps[level] + land[level]


def share_blocks(slots, sems, send_at, receive_at, me, sent):
    near, far = flip(me, 1), flip(me, 2)
    for copy in sent:
        copy.wait_send()
    across = send(slots.at[me], slots.at[me], sems, send_at, {"blk": far}, receive_at)
    beside = send(slots.at[me], slots.at[me], sems, send_at + 1, {"blk": near}, receive_at + 1)
    yield
    across.wait_recv()
    onward = send(slots.at[far], slots.at[far], sems, send_at + 2, {"blk": near}, receive_at + 2)
    yield
    beside.wait_recv()
    onward.wait_recv()
    sent[:] = [across, beside, onward]


def dot(left, right):
    return jnp.dot(left, right, preferred_element_type=WIDE)


def dot_right_t(left, right):
    return lax.dot_general(left, right, (((1,), (1,)), ((), ())), preferred_element_type=WIDE)


def dot_left_t(left, right):
    return lax.dot_general(left, right, (((0,), (0,)), ((), ())), preferred_element_type=WIDE)


def fold(values):
    rows, width = values.shape
    return jnp.sum(values.reshape(rows // 8, 8, width), axis=0)


def mean_of(values):
    return jnp.mean(values, axis=-1, keepdims=True)


def norm_back(upstream, scaled, inverse, gain):
    inner = upstream * gain
    return inverse * (inner - mean_of(inner) - scaled * mean_of(inner * scaled))


def layout_of(sizes, seqs, rows, width, hidden):
    tokens = seqs * rows
    blocks = sizes["blk"]
    length = rows * blocks
    own = width // blocks
    heads = own // HEAD
    levels = len(bits_of(sizes, SUM_ORDER))
    units = 2 * (hidden // width) + 1
    land_total = sum(landing_rows(sizes, width, UNIT_ORDERS[at]) for at in range(units))
    own_land = max(landing_rows(sizes, width, order) for order in OWN_ORDERS)
    return dict(
        x_all=((seqs, length, width), LOW),
        x_own=((seqs, rows, width), LOW),
        cot=((seqs, rows, width), LOW),
        w_qkv=((width, 3 * own), LOW),
        w_o=((width, width), LOW),
        w_up=((width, hidden), LOW),
        w_down=((hidden, width), LOW),
        vec_low=((VECTORS * width,), LOW),
        vec=((VECTORS, width), WIDE),
        flags=((blocks, 8, rows), WIDE),
        qkv=((seqs, length, 3 * own), LOW),
        probs=((seqs * heads, length, length), LOW),
        o_wide=((seqs, length, own), WIDE),
        o_send=((seqs, length, own), LOW),
        o_all=((seqs, rows, width), LOW),
        total=((tokens, width), WIDE),
        scaled=((tokens, width), WIDE),
        inverse=((tokens, 128), WIDE),
        normed=((tokens, width), WIDE),
        normed_low=((tokens, width), LOW),
        active=((tokens, hidden), LOW),
        slope=((tokens, hidden), WIDE),
        grad_b=((tokens, width), WIDE),
        grad_y=((tokens, width), LOW),
        grad_z=((tokens, hidden), LOW),
        grad_t=((tokens, width), LOW),
        do_send=((seqs, rows, width), LOW),
        do_all=((seqs, length, own), LOW),
        grad_s=((heads, length, length), LOW),
        d_qkv=((seqs, length, 3 * own), LOW),
        dx_part=((seqs, length, width), LOW),
        dx_near=((seqs, 2, rows, width), LOW),
        dx_chip=((seqs, rows, width), LOW),
        hid=((seqs, rows, width), LOW),
        dx=((seqs, rows, width), LOW),
        out=((units * width, width), LOW),
        own_out=((3, blocks, width, own), LOW),
        dx_far=((seqs, rows, width), LOW),
        work=((units * width, width), LOW),
        land=((land_total, width), LOW),
        own_work=((3, width, own), LOW),
        own_land=((3, own_land, own), LOW),
        steps=((levels + 1, VECTORS, width), WIDE),
        vec_land=((levels, VECTORS, width), WIDE),
    )


def layer_kernel(sizes, names, *refs):
    x, lengths, mask, wq, wk, wv, wo, wu, wd, cotangent = refs[:10]
    vectors_in = refs[10:19]
    hid_out, dx_out, sums_out, own_sums_out, vec_out = refs[19:24]
    r = types.SimpleNamespace(**dict(zip(names, refs[24:-3], strict=True)))
    sems = refs[-3:-1]
    local = refs[-1]
    x_all, qkv, vec, steps = r.x_all, r.qkv, r.vec, r.steps
    seqs, rows, width = r.x_own.shape
    tokens = seqs * rows
    length = x_all.shape[1]
    blocks = sizes["blk"]
    own = width // blocks
    heads = own // HEAD
    hidden = r.w_up.shape[1]
    tiles = hidden // width
    scale = HEAD ** (-0.5)
    me = lax.axis_index("blk")
    near, far = flip(me, 1), flip(me, 2)
    cross = flip(far, 1)
    peers = (near, far, cross)
    place = lambda index: span(index * rows, rows, rows)
    lanes = lambda index: span(index * own, own, own)

    used = {"send": 0, "receive": 0, "local": 0}
    pending, stores = [], []

    def take(which, count):
        at = used[which]
        used[which] += count
        return at

    def slot(count):
        return take("send", count), take("receive", count)

    def send_in(pair, offset, src, dst, peer):
        return send(src, dst, sems, pair[0] + offset, {"blk": peer}, pair[1] + offset)

    def fetch(src, dst):
        copy = pltpu.make_async_copy(src, dst, local.at[used["local"]])
        used["local"] += 1
        copy.start()
        return copy

    loads_x = [
        fetch(x, x_all.at[:, place(me), :]),
        fetch(x, r.x_own),
    ]
    loads_w = [
        fetch(weight.at[:, lanes(me)], r.w_qkv.at[:, pl.ds(at * own, own)])
        for at, weight in enumerate((wq, wk, wv))
    ]
    load_vectors = []
    at = 0
    for vector in vectors_in:
        count = vector.shape[0]
        load_vectors.append(fetch(vector, r.vec_low.at[pl.ds(at, count)]))
        at += count
    load_o = fetch(wo, r.w_o)
    load_up = fetch(wu, r.w_up)
    load_down = fetch(wd, r.w_down)
    load_cot = fetch(cotangent, r.cot)

    positions = me * rows + lax.broadcasted_iota(jnp.int32, (1, rows), 1)
    flag_rows = []
    for seq in range(seqs):
        good = (mask[seq : seq + 1, :] == 1) & (positions < lengths[seq])
        flag_rows.append(jnp.where(good, 0.0, -1000000000.0).astype(WIDE))
    flag_rows.append(jnp.zeros((8 - seqs, rows), WIDE))
    r.flags[me] = jnp.concatenate(flag_rows, axis=0)

    barrier = pltpu.get_barrier_semaphore()
    greeted = [{"blk": peer} for peer in peers] + [
        peer for letter in "xz" for stage in stages_of(sizes)[letter] for _, peer in digit_of(stage)[1]
    ]
    for peer in greeted:
        pl.semaphore_signal(barrier, inc=1, device_id=peer, device_id_type=MESH)
    pl.semaphore_wait(barrier, len(greeted))

    at_far, at_near, at_on, at_flag = slot(seqs), slot(seqs), slot(seqs), slot(len(peers))
    flag_copies = [
        send_in(at_flag, index, r.flags.at[me], r.flags.at[me], peer)
        for index, peer in enumerate(peers)
    ]
    x_far, x_near, x_on = [], [], []
    for seq in range(seqs):
        target = x_all.at[seq, place(me), :]
        x_far.append(send_in(at_far, seq, x.at[seq], target, far))
        x_near.append(send_in(at_near, seq, x.at[seq], target, near))
    pending += flag_copies

    def forward_x(seq):
        x_far[seq].wait_recv()
        block = x_all.at[seq, place(far), :]
        x_on.append(send_in(at_on, seq, block, block, near))

    lane = lax.broadcasted_iota(jnp.int32, (1, own), 1)
    of_head = [(lane >= head * HEAD) & (lane < (head + 1) * HEAD) for head in range(heads)]
    only = lambda values, head: jnp.where(of_head[head], values.astype(WIDE), 0.0)
    for copy in load_vectors:
        copy.wait()
    for at in range(8 + tiles):
        vec[at : at + 1, :] = r.vec_low[at * width : (at + 1) * width].astype(WIDE).reshape(1, width)
    bias_q = vec[0:1, lanes(me)]
    bias_v = vec[1:2, lanes(me)]
    bias_qkv = jnp.concatenate([bias_q, jnp.zeros_like(bias_q), bias_v], axis=1)
    o_all, o_send = r.o_all, r.o_send
    at_o = slot(seqs * len(peers))
    o_copies = []

    def project(seq):
        qkv[seq] = (dot(x_all[seq], r.w_qkv[...]) + bias_qkv).astype(LOW)

    column = lax.broadcasted_iota(jnp.int32, (length, length), 1)
    row = lax.broadcasted_iota(jnp.int32, (length, length), 0)

    def attend(seq):
        keys = qkv[seq, :, own : 2 * own]
        values = qkv[seq, :, 2 * own :]
        key_bias = jnp.concatenate([r.flags[block, seq : seq + 1, :] for block in range(blocks)], axis=1)
        bias = jnp.where(column == row, 0.0, key_bias)
        query = qkv[seq, :, 0:own].astype(WIDE) * scale
        joined = None
        for head in range(heads):
            scores = dot_right_t(only(query, head).astype(LOW), keys) + bias
            raised = jnp.exp(scores - jnp.max(scores, axis=-1, keepdims=True))
            probs = (raised / jnp.sum(raised, axis=-1, keepdims=True)).astype(LOW)
            r.probs[seq * heads + head] = probs
            result = dot(probs, values)
            joined = result if joined is None else jnp.where(of_head[head], result, joined)
        r.o_wide[seq] = joined
        o_send[seq] = joined.astype(LOW)
        for index, peer in enumerate(peers):
            part = o_send.at[seq, place(peer), :]
            o_copies.append(send_in(at_o, seq * len(peers) + index, part, o_all.at[seq, :, lanes(me)], peer))
        o_all[seq, :, lanes(me)] = o_send[seq, place(me), :]

    for copy in loads_w:
        copy.wait()
    for copy in loads_x:
        copy.wait()
    for copy in flag_copies:
        copy.wait_recv()
    forward_x(0)
    for seq in range(seqs):
        x_near[seq].wait_recv()
        x_on[seq].wait_recv()
        project(seq)
        if seq + 1 < seqs:
            forward_x(seq + 1)
        attend(seq)

    total, scaled, inverse = r.total, r.scaled, r.inverse
    normed, normed_low = r.normed, r.normed_low
    wide_row = lambda at: vec[at : at + 1, :]
    load_o.wait()
    for copy in o_copies:
        copy.wait_recv()
    flat = lambda ref: ref[...].reshape(tokens, width)
    values = flat(r.x_own).astype(WIDE) + dot(flat(o_all), r.w_o[...]) + wide_row(2)
    center = values - mean_of(values)
    inv = lax.rsqrt(mean_of(center * center) + EPSILON)
    made = center * inv
    scaled[...] = made
    inverse[...] = jnp.broadcast_to(inv, inverse.shape)
    result = made * wide_row(3) + wide_row(4)
    normed[...] = result
    normed_low[...] = result.astype(LOW)

    load_up.wait()
    active, slope = r.active, r.slope

    def up(tile, carry):
        columns = span(tile * width, width, width)
        z = dot(normed_low[...], r.w_up[:, columns]) + vec[pl.ds(8 + tile, 1), :]
        below = 0.5 * (1.0 + lax.erf(z * 0.7071067811865476))
        active[:, columns] = (z * below).astype(LOW)
        slope[:, columns] = below + z * (0.3989422804014327 * jnp.exp(-0.5 * z * z))
        return carry

    lax.fori_loop(0, tiles, up, 0)
    load_down.wait()
    load_cot.wait()
    values = normed[...] + dot(active[...], r.w_down[...]) + wide_row(5)

    grad_b, grad_y = r.grad_b, r.grad_y
    center = values - mean_of(values)
    inv = lax.rsqrt(mean_of(center * center) + EPSILON)
    made = center * inv
    r.hid[...] = (made * wide_row(6) + wide_row(7)).astype(LOW).reshape(seqs, rows, width)
    upstream = flat(r.cot).astype(WIDE)
    back = norm_back(upstream, made, inv, wide_row(6))
    grad_b[...] = back
    rounded = back.astype(LOW)
    grad_y[...] = rounded
    total_row = lambda values: jnp.sum(fold(values), axis=0, keepdims=True)
    steps[0] = jnp.zeros((VECTORS, width), WIDE)
    steps[0, 7:8, :] = total_row(upstream)
    steps[0, 6:7, :] = total_row(upstream * made)
    steps[0, 5:6, :] = total_row(rounded.astype(WIDE))

    stores.append(fetch(r.hid, hid_out))

    work = r.work
    running = {}
    last = []
    place_of = {"land": 0, "poll": 0}

    def launch(name, item):
        running[name] = item
        advance(name)

    def advance(name):
        if name in running and next(running[name], True) is not None:
            del running[name]

    def launch_unit(unit):
        letters = UNIT_ORDERS[unit]
        sending, receiving = semaphores_of(sizes, width, letters)
        ats = take("send", sending), take("receive", receiving)
        land_at = place_of["land"]
        place_of["land"] += landing_rows(sizes, width, letters)
        sent = []
        last.append(sent)
        def item():
            yield from reduce_rows(sizes, work, r.land, r.out, sems, unit * width, width, land_at, *ats, letters, sent)
            stores.append(fetch(r.out.at[cut(unit)], sums_out.at[cut(unit)]))

        launch(unit, item())

    def launch_own(kind):
        letters = OWN_ORDERS[kind]
        sending, receiving = semaphores_of(sizes, width, letters)
        ats = take("send", max(sending, 3)), take("receive", receiving)
        blocks_at = take("receive", 3)
        slots = r.own_out.at[kind]
        sent = []
        last.append(sent)

        def item():
            parts = r.own_work.at[kind], r.own_land.at[kind], slots.at[me]
            yield from reduce_rows(sizes, *parts, sems, 0, width, 0, *ats, letters, sent)
            yield from share_blocks(slots, sems, ats[0], blocks_at, me, sent)
            stores.append(fetch(slots, own_sums_out.at[kind]))

        launch(2 * tiles + 1 + kind, item())

    def poll():
        at = place_of["poll"]
        place_of["poll"] += 1
        for name in POLLS[at] if at < len(POLLS) else ():
            advance(name)

    cut = lambda tile: slice(tile * width, (tile + 1) * width)
    for tile in range(tiles):
        work[cut(tile), :] = dot_left_t(active[:, cut(tile)], grad_y[...]).astype(LOW)
        launch_unit(tile)
        poll()

    grad_z = r.grad_z

    for tile in range(tiles):
        made = (dot_right_t(grad_y[...], r.w_down[cut(tile), :]) * slope[:, cut(tile)]).astype(LOW)
        grad_z[:, cut(tile)] = made
        steps[0, 8 + tile : 9 + tile, :] = total_row(made.astype(WIDE))
        poll()
    upstream = grad_b[...] + dot_right_t(grad_z[...], r.w_up[...])
    total[...] = upstream
    poll()
    upstream = total[...]

    grad_t = r.grad_t
    made = scaled[...]
    back = norm_back(upstream, made, inverse[:, 0:1], wide_row(3))
    grad_b[...] = back
    rounded = back.astype(LOW)
    grad_t[...] = rounded
    steps[0, 4:5, :] = total_row(upstream)
    steps[0, 3:4, :] = total_row(upstream * made)
    steps[0, 2:3, :] = total_row(rounded.astype(WIDE))
    poll()

    do_send, do_all = r.do_send, r.do_all
    for copy in x_far + x_near + x_on:
        copy.wait_send()
    at_do = at_far[0], take("receive", seqs * len(peers))
    do_copies = []
    made = dot_right_t(grad_t[...], r.w_o[...]).astype(LOW)
    do_send[...] = made.reshape(seqs, rows, width)
    for seq in range(seqs):
        do_copies.append(
            [
                send_in(
                    at_do,
                    seq * len(peers) + index,
                    do_send.at[seq, :, lanes(peer)],
                    do_all.at[seq, place(me), :],
                    peer,
                )
                for index, peer in enumerate(peers)
            ]
        )
        do_all[seq, place(me), :] = do_send[seq, :, lanes(me)]
        pending += do_copies[-1]

    poll()
    work[2 * hidden :, :] = dot_left_t(o_all[...].reshape(tokens, width), grad_t[...]).astype(LOW)
    launch_unit(2 * tiles)
    poll()
    for tile in range(tiles):
        work[cut(tiles + tile), :] = dot_left_t(normed_low[...], grad_z[:, cut(tile)]).astype(LOW)
        launch_unit(tiles + tile)
        poll()

    d_qkv, grad_s, dx_part = r.d_qkv, r.grad_s, r.dx_part
    for copy in o_copies:
        copy.wait_send()
    at_dx_near = at_o[0], take("receive", 2 * seqs)
    at_dx_far = at_o[0] + 2 * seqs, take("receive", seqs)
    dx_near, dx_far = [], []

    def value_back(seq):
        upstream = do_all[seq].astype(WIDE)
        grads = [
            dot_left_t(r.probs[seq * heads + head], only(upstream, head).astype(LOW)) for head in range(heads)
        ]
        d_qkv[seq, :, 2 * own :] = functools.reduce(jnp.add, grads).astype(LOW)

    def score_back(seq):
        values = qkv[seq, :, 2 * own :]
        upstream = do_all[seq].astype(WIDE)
        inner = upstream * r.o_wide[seq]
        for head in range(heads):
            delta = jnp.sum(only(inner, head), axis=-1, keepdims=True)
            prob_grad = dot_right_t(only(upstream, head).astype(LOW), values)
            probs = r.probs[seq * heads + head].astype(WIDE)
            grad_s[head] = (probs * (prob_grad - delta)).astype(LOW)

    def query_key_back(seq):
        queries_wide = qkv[seq, :, 0:own].astype(WIDE) * scale
        keys_wide = qkv[seq, :, own : 2 * own].astype(WIDE) * scale
        query_grads, key_grads = [], []
        for head in range(heads):
            query_grads.append(dot(grad_s[head], only(keys_wide, head).astype(LOW)))
            key_grads.append(dot_left_t(grad_s[head], only(queries_wide, head).astype(LOW)))
        d_qkv[seq, :, 0:own] = functools.reduce(jnp.add, query_grads).astype(LOW)
        d_qkv[seq, :, own : 2 * own] = functools.reduce(jnp.add, key_grads).astype(LOW)

    def input_back(seq):
        dx_part[seq] = dot_right_t(d_qkv[seq], r.w_qkv[...]).astype(LOW)
        dx_near.append(
            [
                send_in(at_dx_near, 2 * seq + at, dx_part.at[seq, place(block), :], r.dx_near.at[seq, at], near)
                for at, block in enumerate((near, cross))
            ]
        )
        pending.extend(dx_near[-1])

    def own_grad(columns):
        tokens_in = x_all[...].reshape(seqs * length, width)
        return dot_left_t(tokens_in, d_qkv[:, :, columns].reshape(seqs * length, -1)).astype(LOW)

    def hand_on(seq):
        dx_near[seq][1].wait_recv()
        summed = dx_part[seq, place(far), :].astype(WIDE) + r.dx_near[seq, 1].astype(WIDE)
        r.dx_chip[seq] = summed.astype(LOW)
        dx_far.append(send_in(at_dx_far, seq, r.dx_chip.at[seq], r.dx_far.at[seq], far))
        pending.append(dx_far[-1])

    for seq in range(seqs):
        for copy in do_copies[seq]:
            copy.wait_recv()
        value_back(seq)
        poll()
    r.own_work[0] = own_grad(slice(2 * own, None))
    launch_own(0)
    poll()
    for seq in range(seqs):
        score_back(seq)
        poll()
        query_key_back(seq)
        poll()
        input_back(seq)
        poll()
        if seq > 0:
            hand_on(seq - 1)
    made = own_grad(slice(0, 2 * own))
    r.own_work[1] = made[:, :own]
    launch_own(1)
    r.own_work[2] = made[:, own:]
    launch_own(2)
    hand_on(seqs - 1)

    sums = total_row(d_qkv[...].reshape(seqs * length, 3 * own).astype(WIDE))
    steps[0, 0:1, lanes(me)] = sums[:, 0:own]
    steps[0, 1:2, lanes(me)] = sums[:, 2 * own :]
    sum_bits = bits_of(sizes, SUM_ORDER)
    launch(2 * tiles + 4, reduce_whole(steps, r.vec_land, sems, take("send", 1), take("receive", len(sum_bits)), sum_bits))
    poll()

    for seq in range(seqs):
        dx_near[seq][0].wait_recv()
        dx_far[seq].wait_recv()

        summed = grad_b[seq * rows : (seq + 1) * rows, :] + dx_part[seq, place(me), :].astype(WIDE)
        summed = summed + r.dx_near[seq, 0].astype(WIDE) + r.dx_far[seq].astype(WIDE)
        r.dx[seq] = summed.astype(LOW)
        poll()
    stores.append(fetch(r.dx, dx_out))

    for name in sum(POLLS[place_of["poll"] :], ()):
        advance(name)
    while running:
        for name in list(running):
            advance(name)
    vec_out[...] = steps[len(sum_bits)]
    for copy in sum(last, pending):
        copy.wait_send()
    for copy in stores:
        copy.wait()
    assert (used["send"], used["receive"]) == semaphore_counts(sizes, seqs, width) and used["local"] == LOCALS


def widen_kernel(blocks, hid, dx, sums, shared, vec, *refs):
    hid_out, dx_out, wq, wk, wv, wo, wu, wd = refs[:8]
    rows_out, bu = refs[8:16], refs[16]
    low, shared_low, wide, shared_wide, hid_low, dx_low, sems = refs[17:]
    width = wq.shape[0]
    own = width // blocks
    units = sums.shape[0] // width
    tiles = (units - 1) // 2
    used = [0]

    def copy(src, dst):
        made = pltpu.make_async_copy(src, dst, sems.at[used[0]])
        used[0] += 1
        made.start()
        return made

    unit = lambda ref, at: ref.at[pl.ds(at * width, width)]
    loads = [copy(unit(sums, at), unit(low, at)) for at in range(units)]
    shared_loads = [copy(shared.at[kind], shared_low.at[kind]) for kind in range(3)]
    token_loads = [copy(hid, hid_low), copy(dx, dx_low)]
    stores = []
    targets = (
        [unit(wd, at) for at in range(tiles)] + [wu.at[:, pl.ds(at * width, width)] for at in range(tiles)] + [wo]
    )
    for at in range(units):
        loads[at].wait()

        def body(step, carry):
            part = span(at * width + step * 256, 256)
            wide[part, :] = low[part, :].astype(WIDE)
            return carry

        lax.fori_loop(0, width // 256, body, 0)
        stores.append(copy(unit(wide, at), targets[at]))
    for load in token_loads:
        load.wait()
    stores += [copy(hid_low, hid_out), copy(dx_low, dx_out)]
    for kind, target in enumerate((wv, wq, wk)):
        shared_loads[kind].wait()
        for block in range(blocks):
            shared_wide[kind, :, block * own : (block + 1) * own] = shared_low[kind, block].astype(WIDE)
        stores.append(copy(shared_wide.at[kind], target))
    for at, row in enumerate(rows_out):
        row[...] = vec[at, :]
    for at in range(tiles):
        bu[at * width : (at + 1) * width] = vec[len(rows_out) + at, :]
    for made in stores:
        made.wait()


def on_device(
    sizes,
    hidden_input,
    lengths,
    key_mask,
    query_weight,
    query_offset,
    key_weight,
    value_weight,
    value_offset,
    output_weight,
    output_offset,
    mixer_gain,
    mixer_shift,
    up_weight,
    up_offset,
    down_weight,
    down_offset,
    final_gain,
    final_shift,
    cotangent,
):
    seqs, rows, width = hidden_input.shape
    hidden = up_weight.shape[1]
    blocks = sizes["blk"]
    own = width // blocks
    scratch = layout_of(sizes, seqs, rows, width, hidden)
    anywhere = pl.BlockSpec(memory_space=pl.ANY)
    inside = pl.BlockSpec(memory_space=pltpu.VMEM)
    scalars = pl.BlockSpec(memory_space=pltpu.SMEM)
    scratch_shape = types.SimpleNamespace(**{name: shape for name, (shape, _) in scratch.items()})
    units = scratch_shape.work
    shared = (3, blocks, width, own)
    hid, dx, sums, own_sums, vec_sums = pl.pallas_call(
        functools.partial(layer_kernel, sizes, tuple(scratch)),
        out_shape=(
            jax.ShapeDtypeStruct(hidden_input.shape, LOW),
            jax.ShapeDtypeStruct(hidden_input.shape, LOW),
            jax.ShapeDtypeStruct(units, LOW),
            jax.ShapeDtypeStruct(shared, LOW),
            jax.ShapeDtypeStruct((VECTORS, width), WIDE),
        ),
        in_specs=[anywhere, scalars, inside] + [anywhere] * 16,
        out_specs=(anywhere,) * 4 + (inside,),
        scratch_shapes=[pltpu.VMEM(shape, kind) for shape, kind in scratch.values()]
        + [
            *(pltpu.SemaphoreType.DMA((count,)) for count in semaphore_counts(sizes, seqs, width)),
            pltpu.SemaphoreType.DMA((LOCALS,)),
        ],
        compiler_params=pltpu.CompilerParams(
            collective_id=0, has_side_effects=True, vmem_limit_bytes=60 * 1024 * 1024
        ),
    )(
        hidden_input,
        lengths,
        key_mask,
        query_weight,
        key_weight,
        value_weight,
        output_weight,
        up_weight,
        down_weight,
        cotangent,
        query_offset,
        value_offset,
        output_offset,
        mixer_gain,
        mixer_shift,
        down_offset,
        final_gain,
        final_shift,
        up_offset,
    )
    full = jax.ShapeDtypeStruct((width, width), WIDE)
    row = jax.ShapeDtypeStruct((width,), WIDE)
    flat = jax.ShapeDtypeStruct(hidden_input.shape, LOW)
    final = pl.pallas_call(
        functools.partial(widen_kernel, blocks),
        out_shape=(
            flat,
            flat,
            full,
            full,
            full,
            full,
            jax.ShapeDtypeStruct((width, hidden), WIDE),
            jax.ShapeDtypeStruct((hidden, width), WIDE),
        )
        + (row,) * 8
        + (jax.ShapeDtypeStruct((hidden,), WIDE),),
        in_specs=[anywhere] * 4 + [inside],
        out_specs=(anywhere,) * 8 + (inside,) * 9,
        scratch_shapes=[
            pltpu.VMEM(units, LOW),
            pltpu.VMEM(shared, LOW),
            pltpu.VMEM(units, WIDE),
            pltpu.VMEM((3, width, width), WIDE),
            pltpu.VMEM(hidden_input.shape, LOW),
            pltpu.VMEM(hidden_input.shape, LOW),
            pltpu.SemaphoreType.DMA((2 * units[0] // width + 10,)),
        ],
        compiler_params=pltpu.CompilerParams(vmem_limit_bytes=60 * 1024 * 1024),
    )(hid, dx, sums, own_sums, vec_sums)
    hid, dx, wq, wk, wv, wo, wu, wd, bq, bv, bo, g1, s1, bd, g2, s2, bu = final
    return hid, dx, wq, bq, wk, wv, bv, wo, bo, g1, s1, wu, bu, wd, bd, g2, s2


def solution(mesh):
    split = P("dp", "blk", None)
    in_specs = (split, P("dp"), P("dp", "blk")) + (P(),) * 15 + (split,)
    out_specs = (split, split) + (P(),) * 15
    return jax.shard_map(
        functools.partial(on_device, dict(mesh.shape)),
        mesh=mesh,
        in_specs=in_specs,
        out_specs=out_specs,
        check_vma=False,
    )
```

time: 125 us -> 102 us (0.82)
  Pallas kernels: 122 us -> 99.8 us
    pallas_call x1, Pallas kernels: 113 us -> 90.9 us  [on_device(): pl.pallas_call(functools.partial(layer_kernel, sizes, tuple(scratch)), ou...]
where the time goes in v4:
time: 102 us; the launch traced here: 101 us
  Pallas kernels  99.8 us (98%)
    pallas_call x1, Pallas kernels, on_device(): pl.pallas_call(functools.partial(layer_kernel, sizes, tuple(scratch)), ou...  90.9 us
    pallas_call x1, Pallas kernels, on_device(): pl.pallas_call(functools.partial(widen_kernel, blocks), out_shape=(flat,...  8.93 us

profile of v4, /device:TPU:5, one launch (start us, length us, event | category | flops | bytes accessed | tf_op | source)
XLA Modules:
  0.0 100.7 jit_solution(10967958201532879863)
XLA Ops:
  0.7 90.9 %shard_map.314 = (bf16[3,128,512]{2,1,0:T(8,128)(2,1)}, bf16[3,128,512]{2,1,0:T(8,128)(2,1)}, bf16[4608,512]{1,0:T(8,128)(2,1)}, bf16[3,4,512,128]{3,2,1,0:T(8,128)(2,1)}, f32[16,512]{1,0:T(8,128)}) custom-call(bf16[3,128,512]{2,1,0:T(8,128)(2,1)} %refs_0_.1, s32[3]{0:T(128)} %refs_1_.1, s32[3,128]{1,0:T(4,128)} %refs_2_.1, bf16[512,512]{1,0:T(8,128)(2,1)} %refs_3_.1, ...), custom_call_target="tpu_custom_call" | custom-call | tf_op jit(solution)/shard_map/pallas_call | solution.py:830
  91.5 8.9 %shard_map.315 = (bf16[3,128,512]{2,1,0:T(8,128)(2,1)}, bf16[3,128,512]{2,1,0:T(8,128)(2,1)}, f32[512,512]{1,0:T(8,128)}, f32[512,512]{1,0:T(8,128)}, f32[512,51...) custom-call(bf16[3,128,512]{2,1,0:T(8,128)(2,1)} %get-tuple-element., ...), custom_call_target="tpu_custom_call" | custom-call | tf_op jit(solution)/shard_map/pallas_call | solution.py:873

commit v5 on v4

--- a/solution.py
+++ b/solution.py
@@ -17,8 +17,8 @@
 VECTORS = 16
 LOCALS = 32
 
-UNIT_ORDERS = ("cyxz", "cxyz", "cyxz", "cayxb", "caxby", "cxyab", "caxyb", "czxy", "cxyab")
-OWN_ORDERS = ("xab", "xz", "xz")
+UNIT_ORDERS = ("cxaby", "caxby", "cabxy", "cxyab", "cabxy", "cxyab", "cyxab", "cyxz", "cxyz")
+OWN_ORDERS = ("axb", "xz", "axb")
 SUM_ORDER = "cxyab"
 POLLS = (
     (),
@@ -26,35 +26,36 @@
     (),
     (),
     (),
+    (),
+    (),
+    (),
+    (0, 1,),
+    (2,),
+    (3,),
+    (),
+    (),
+    (),
+    (),
+    (),
+    (8, 4, 5, 6, 7,),
+    (0, 1,),
+    (),
+    (3, 2,),
+    (),
+    (),
+    (),
+    (),
+    (8,),
+    (4, 6,),
     (0,),
-    (1, 2,),
-    (3,),
-    (),
-    (),
-    (),
-    (),
-    (),
-    (0,),
-    (1, 8,),
-    (4, 3, 5,),
-    (6, 2, 7,),
-    (0,),
-    (),
-    (8, 4,),
-    (1,),
-    (3, 5,),
-    (6,),
-    (2,),
-    (9, 8,),
-    (4,),
-    (5, 3,),
-    (7, 6, 0,),
-    (1,),
-    (9, 2, 8, 7,),
-    (4, 5, 6, 12,),
-    (10, 3, 0, 1,),
-    (9, 11, 2, 12, 8,),
-    (7, 5, 4, 6, 0, 1, 10, 3, 9, 12, 7, 2, 4, 11, 8, 5, 9, 6, 1, 0, 12, 3, 10, 7, 1, 0, 4, 8, 2, 5, 6, 9, 11, 2, 3, 10, 12, 4, 8, 6, 5, 11, 7, 9, 3, 8, 7, 9, 3, 10, 8, 4, 5, 10, 4, 11, 5, 6, 11, 6,),
+    (),
+    (5,),
+    (9, 7, 1, 3, 2,),
+    (10, 11, 6, 8,),
+    (9, 4, 5, 0, 12, 3, 1, 7,),
+    (11, 10, 2, 6,),
+    (9, 8, 4, 5, 12, 3,),
+    (0, 1, 7, 2, 11, 10, 6, 4, 9, 12, 0, 1, 2, 8, 5, 4, 3, 10, 9, 12, 7, 2, 11, 6, 8, 4, 3, 0, 9, 1, 7, 10, 5, 11, 10, 12, 6, 3, 8, 2, 1, 0, 9, 8, 5, 6, 9, 11, 4, 7, 3, 7, 5, 2, 3, 0, 2, 6, 1, 0, 6, 1, 11, 5, 4, 11, 5, 4,),
 )
 
 
@@ -475,53 +476,58 @@
 
     total, scaled, inverse = r.total, r.scaled, r.inverse
     normed, normed_low = r.normed, r.normed_low
+    active, slope = r.active, r.slope
+    grad_b, grad_y = r.grad_b, r.grad_y
     wide_row = lambda at: vec[at : at + 1, :]
-    load_o.wait()
-    for copy in o_copies:
-        copy.wait_recv()
+    total_row = lambda values: jnp.sum(fold(values), axis=0, keepdims=True)
     flat = lambda ref: ref[...].reshape(tokens, width)
-    values = flat(r.x_own).astype(WIDE) + dot(flat(o_all), r.w_o[...]) + wide_row(2)
-    center = values - mean_of(values)
-    inv = lax.rsqrt(mean_of(center * center) + EPSILON)
-    made = center * inv
-    scaled[...] = made
-    inverse[...] = jnp.broadcast_to(inv, inverse.shape)
-    result = made * wide_row(3) + wide_row(4)
-    normed[...] = result
-    normed_low[...] = result.astype(LOW)
-
-    load_up.wait()
-    active, slope = r.active, r.slope
-
-    def up(tile, carry):
-        columns = span(tile * width, width, width)
-        z = dot(normed_low[...], r.w_up[:, columns]) + vec[pl.ds(8 + tile, 1), :]
-        below = 0.5 * (1.0 + lax.erf(z * 0.7071067811865476))
-        active[:, columns] = (z * below).astype(LOW)
-        slope[:, columns] = below + z * (0.3989422804014327 * jnp.exp(-0.5 * z * z))
-        return carry
-
-    lax.fori_loop(0, tiles, up, 0)
-    load_down.wait()
-    load_cot.wait()
-    values = normed[...] + dot(active[...], r.w_down[...]) + wide_row(5)
-
-    grad_b, grad_y = r.grad_b, r.grad_y
-    center = values - mean_of(values)
-    inv = lax.rsqrt(mean_of(center * center) + EPSILON)
-    made = center * inv
-    r.hid[...] = (made * wide_row(6) + wide_row(7)).astype(LOW).reshape(seqs, rows, width)
-    upstream = flat(r.cot).astype(WIDE)
-    back = norm_back(upstream, made, inv, wide_row(6))
-    grad_b[...] = back
-    rounded = back.astype(LOW)
-    grad_y[...] = rounded
-    total_row = lambda values: jnp.sum(fold(values), axis=0, keepdims=True)
     steps[0] = jnp.zeros((VECTORS, width), WIDE)
-    steps[0, 7:8, :] = total_row(upstream)
-    steps[0, 6:7, :] = total_row(upstream * made)
-    steps[0, 5:6, :] = total_row(rounded.astype(WIDE))
-
+
+    def normalize(values):
+        center = values - mean_of(values)
+        inv = lax.rsqrt(mean_of(center * center) + EPSILON)
+        return center * inv, inv
+
+    def feed_forward(first, count):
+        some = slice(first, first + count)
+        size = count * rows
+        part = pl.ds(first * rows, size)
+        mixed = o_all[some].reshape(size, width)
+        made, inv = normalize(
+            r.x_own[some].reshape(size, width).astype(WIDE) + dot(mixed, r.w_o[...]) + wide_row(2)
+        )
+        scaled[part, :] = made
+        inverse[part, :] = jnp.broadcast_to(inv, (size, 128))
+        result = made * wide_row(3) + wide_row(4)
+        normed[part, :] = result
+        normed_low[part, :] = result.astype(LOW)
+        step = min(hidden, 2 * width * (2 * rows) // size)
+        for at in range(0, hidden, step):
+            columns = slice(at, at + step)
+            offset = jnp.concatenate([wide_row(8 + tile) for tile in range(at // width, (at + step) // width)], axis=1)
+            z = dot(normed_low[part, :], r.w_up[:, columns]) + offset
+            below = 0.5 * (1.0 + lax.erf(z * 0.7071067811865476))
+            active[part, columns] = (z * below).astype(LOW)
+            slope[part, columns] = below + z * (0.3989422804014327 * jnp.exp(-0.5 * z * z))
+        made, inv = normalize(normed[part, :] + dot(active[part, :], r.w_down[...]) + wide_row(5))
+        r.hid[some] = (made * wide_row(6) + wide_row(7)).astype(LOW).reshape(count, rows, width)
+        upstream = r.cot[some].reshape(size, width).astype(WIDE)
+        back = norm_back(upstream, made, inv, wide_row(6))
+        grad_b[part, :] = back
+        rounded = back.astype(LOW)
+        grad_y[part, :] = rounded
+        steps[0, 7:8, :] += total_row(upstream)
+        steps[0, 6:7, :] += total_row(upstream * made)
+        steps[0, 5:6, :] += total_row(rounded.astype(WIDE))
+
+    for copy in (load_o, load_up, load_down, load_cot):
+        copy.wait()
+    arrived = 0
+    for first, count in ((0, seqs - 1), (seqs - 1, 1)) if seqs > 1 else ((0, 1),):
+        for copy in o_copies[arrived : (first + count) * len(peers)]:
+            copy.wait_recv()
+        arrived = (first + count) * len(peers)
+        feed_forward(first, count)
     stores.append(fetch(r.hid, hid_out))
 
     work = r.work
@@ -703,15 +709,17 @@
         poll()
         query_key_back(seq)
         poll()
-        input_back(seq)
-        poll()
-        if seq > 0:
-            hand_on(seq - 1)
     made = own_grad(slice(0, 2 * own))
     r.own_work[1] = made[:, :own]
     launch_own(1)
     r.own_work[2] = made[:, own:]
     launch_own(2)
+    poll()
+    for seq in range(seqs):
+        input_back(seq)
+        poll()
+        if seq > 0:
+            hand_on(seq - 1)
     hand_on(seqs - 1)
 
     sums = total_row(d_qkv[...].reshape(seqs * length, 3 * own).astype(WIDE))
@@ -747,7 +755,7 @@
 def widen_kernel(blocks, hid, dx, sums, shared, vec, *refs):
     hid_out, dx_out, wq, wk, wv, wo, wu, wd = refs[:8]
     rows_out, bu = refs[8:16], refs[16]
-    low, shared_low, wide, shared_wide, hid_low, dx_low, sems = refs[17:]
+    low, shared_low, wide, shared_wide, hid_low, dx_low, flat_vec, sems = refs[17:]
     width = wq.shape[0]
     own = width // blocks
     units = sums.shape[0] // width
@@ -765,6 +773,12 @@
     shared_loads = [copy(shared.at[kind], shared_low.at[kind]) for kind in range(3)]
     token_loads = [copy(hid, hid_low), copy(dx, dx_low)]
     stores = []
+    count = len(rows_out)
+    for at in range(count + tiles):
+        flat_vec[at * width : (at + 1) * width] = vec[at, :]
+    for at, row in enumerate(rows_out):
+        stores.append(copy(flat_vec.at[pl.ds(at * width, width)], row))
+    stores.append(copy(flat_vec.at[pl.ds(count * width, tiles * width)], bu))
     targets = (
         [unit(wd, at) for at in range(tiles)] + [wu.at[:, pl.ds(at * width, width)] for at in range(tiles)] + [wo]
     )
@@ -786,10 +800,6 @@
         for block in range(blocks):
             shared_wide[kind, :, block * own : (block + 1) * own] = shared_low[kind, block].astype(WIDE)
         stores.append(copy(shared_wide.at[kind], target))
-    for at, row in enumerate(rows_out):
-        row[...] = vec[at, :]
-    for at in range(tiles):
-        bu[at * width : (at + 1) * width] = vec[len(rows_out) + at, :]
     for made in stores:
         made.wait()
 
@@ -885,7 +895,7 @@
         + (row,) * 8
         + (jax.ShapeDtypeStruct((hidden,), WIDE),),
         in_specs=[anywhere] * 4 + [inside],
-        out_specs=(anywhere,) * 8 + (inside,) * 9,
+        out_specs=(anywhere,) * 17,
         scratch_shapes=[
             pltpu.VMEM(units, LOW),
             pltpu.VMEM(shared, LOW),
@@ -893,7 +903,8 @@
             pltpu.VMEM((3, width, width), WIDE),
             pltpu.VMEM(hidden_input.shape, LOW),
             pltpu.VMEM(hidden_input.shape, LOW),
-            pltpu.SemaphoreType.DMA((2 * units[0] // width + 10,)),
+            pltpu.VMEM((VECTORS * width,), WIDE),
+            pltpu.SemaphoreType.DMA((2 * units[0] // width + 19,)),
         ],
         compiler_params=pltpu.CompilerParams(vmem_limit_bytes=60 * 1024 * 1024),
     )(hid, dx, sums, own_sums, vec_sums)

time: 102 us -> 96.9 us (0.950)
  Pallas kernels: 99.8 us -> 94.8 us
    pallas_call x1, Pallas kernels: 90.9 us -> 86.4 us  [on_device(): pl.pallas_call(functools.partial(layer_kernel, sizes, tuple(scratch)), ou...]
where the time goes in v5:
time: 96.9 us; the launch traced here: 95.7 us
  Pallas kernels  94.8 us (98%)
    pallas_call x1, Pallas kernels, on_device(): pl.pallas_call(functools.partial(layer_kernel, sizes, tuple(scratch)), ou...  86.4 us
    pallas_call x1, Pallas kernels, on_device(): pl.pallas_call(functools.partial(widen_kernel, blocks), out_shape=(flat,...  8.4 us

profile of v5, /device:TPU:5, one launch (start us, length us, event | category | flops | bytes accessed | tf_op | source)
XLA Modules:
  0.0 95.7 jit_solution(410120634735861376)
XLA Ops:
  0.7 86.4 %shard_map.314 = (bf16[3,128,512]{2,1,0:T(8,128)(2,1)}, bf16[3,128,512]{2,1,0:T(8,128)(2,1)}, bf16[4608,512]{1,0:T(8,128)(2,1)}, bf16[3,4,512,128]{3,2,1,0:T(8,128)(2,1)}, f32[16,512]{1,0:T(8,128)}) custom-call(bf16[3,128,512]{2,1,0:T(8,128)(2,1)} %refs_0_.1, s32[3]{0:T(128)} %refs_1_.1, s32[3,128]{1,0:T(4,128)} %refs_2_.1, bf16[512,512]{1,0:T(8,128)(2,1)} %refs_3_.1, ...), custom_call_target="tpu_custom_call" | custom-call | tf_op jit(solution)/shard_map/pallas_call | solution.py:840
  87.1 8.4 %shard_map.315 = (bf16[3,128,512]{2,1,0:T(8,128)(2,1)}, bf16[3,128,512]{2,1,0:T(8,128)(2,1)}, f32[512,512]{1,0:T(8,128)}, f32[512,512]{1,0:T(8,128)}, f32[512,51...) custom-call(bf16[3,128,512]{2,1,0:T(8,128)(2,1)} %get-tuple-element., ...), custom_call_target="tpu_custom_call" | custom-call | tf_op jit(solution)/shard_map/pallas_call | solution.py:883

commit v6 on v5

--- a/solution.py
+++ b/solution.py
@@ -15,10 +15,10 @@
 LOW = jnp.bfloat16
 WIDE = jnp.float32
 VECTORS = 16
-LOCALS = 32
-
-UNIT_ORDERS = ("cxaby", "caxby", "cabxy", "cxyab", "cabxy", "cxyab", "cyxab", "cyxz", "cxyz")
-OWN_ORDERS = ("axb", "xz", "axb")
+HALVES = 2
+
+UNIT_ORDERS = ("cxzy", "caxby", "cyxab", "cabyx", "cayxb", "cxaby", "cxyab", "caxyb", "cyxab", "caxyb", "caxyb", "cyxab", "cxayb", "cyaxb", "cxayb", "cxyab", "cxyab", "caxyb")
+OWN_ORDERS = ("xab", "xab", "xab")
 SUM_ORDER = "cxyab"
 POLLS = (
     (),
@@ -26,36 +26,36 @@
     (),
     (),
     (),
-    (),
-    (),
-    (),
-    (0, 1,),
+    (0,),
+    (1,),
     (2,),
-    (3,),
-    (),
-    (),
-    (),
-    (),
-    (),
-    (8, 4, 5, 6, 7,),
-    (0, 1,),
-    (),
-    (3, 2,),
-    (),
-    (),
-    (),
-    (),
+    (3, 4, 5,),
+    (6, 7,),
+    (),
+    (),
+    (),
+    (),
+    (),
+    (),
+    (16, 0, 17, 1, 8, 9, 2, 10, 11, 12, 5, 13, 3, 14, 15,),
+    (),
+    (6, 4,),
+    (),
+    (16, 7,),
+    (1,),
+    (2,),
+    (0,),
     (8,),
-    (4, 6,),
-    (0,),
-    (),
-    (5,),
-    (9, 7, 1, 3, 2,),
-    (10, 11, 6, 8,),
-    (9, 4, 5, 0, 12, 3, 1, 7,),
-    (11, 10, 2, 6,),
-    (9, 8, 4, 5, 12, 3,),
-    (0, 1, 7, 2, 11, 10, 6, 4, 9, 12, 0, 1, 2, 8, 5, 4, 3, 10, 9, 12, 7, 2, 11, 6, 8, 4, 3, 0, 9, 1, 7, 10, 5, 11, 10, 12, 6, 3, 8, 2, 1, 0, 9, 8, 5, 6, 9, 11, 4, 7, 3, 7, 5, 2, 3, 0, 2, 6, 1, 0, 6, 1, 11, 5, 4, 11, 5, 4,),
+    (17, 12,),
+    (),
+    (11,),
+    (9, 14,),
+    (13,),
+    (10, 15, 6,),
+    (5, 7,),
+    (18, 4, 16, 0, 3, 2, 1,),
+    (12, 8, 14, 17, 15, 7, 13, 11,),
+    (6, 9, 5, 21, 18, 16, 19, 22, 0, 3, 20, 8, 2, 1, 15, 10, 4, 11, 7, 13, 6, 21, 18, 22, 19, 16, 0, 20, 3, 2, 8, 0, 1, 15, 22, 12, 4, 14, 6, 17, 11, 9, 18, 5, 13, 2, 10, 7, 16, 1, 21, 19, 3, 4, 8, 15, 6, 20, 11, 12, 18, 13, 2, 14, 7, 16, 17, 8, 2, 4, 9, 1, 15, 5, 12, 21, 6, 10, 1, 19, 11, 6, 3, 20, 16, 18, 13, 14, 17, 16, 15, 18, 7, 8, 15, 19, 9, 7, 10, 4, 8, 5, 20, 4, 11, 12, 17, 21, 11, 13, 9, 3, 10, 13, 14, 3, 5, 19, 17, 5, 12, 19, 9, 17, 12, 14, 9, 20, 10, 14, 20, 10,),
 )
 
 
@@ -121,21 +121,30 @@
 
 
 def plan_of(sizes, rows, letters):
+    stages = [stage for letter in letters for stage in stages_of(sizes)[letter]]
     plan = []
     size = rows
-    for letter in letters:
-        for axis, step, radix in stages_of(sizes)[letter]:
-            if size % (radix * ROWS) == 0:
-                size //= radix
-                plan.append(((axis, step, radix), True, size))
-                continue
-            bit = step
-            while bit < step * radix:
-                split = size % (2 * ROWS) == 0
-                size = size // 2 if split else size
-                plan.append(((axis, bit, 2), split, size))
-                bit *= 2
+    for axis, step, radix in stages[:-1]:
+        size = cut_stage(plan, axis, step, radix, size)
+    axis, step, radix = stages[-1]
+    if radix == 2:
+        plan.append((stages[-1], False, size))
+    else:
+        cut_stage(plan, axis, step, radix, size)
     return plan
+
+
+def cut_stage(plan, axis, step, radix, size):
+    if size % (radix * ROWS) == 0:
+        plan.append(((axis, step, radix), True, size // radix))
+        return size // radix
+    bit = step
+    while bit < step * radix:
+        split = size % (2 * ROWS) == 0
+        size = size // 2 if split else size
+        plan.append(((axis, bit, 2), split, size))
+        bit *= 2
+    return size
 
 
 def landing_rows(sizes, rows, letters):
@@ -143,14 +152,14 @@
 
 
 def semaphores_of(sizes, rows, letters):
-    peers = [stage[2] - 1 for stage, _, _ in plan_of(sizes, rows, letters)]
-    return max(peers), 2 * sum(peers)
+    plan = plan_of(sizes, rows, letters)
+    return max(stage[2] - 1 for stage, _, _ in plan), sum((stage[2] - 1) * (1 + split) for stage, split, _ in plan)
 
 
 def semaphore_counts(sizes, seqs, width):
     sends, receives = 3 + 6 * seqs + 1, 3 + 12 * seqs + len(bits_of(sizes, SUM_ORDER))
     for letters in UNIT_ORDERS:
-        sending, receiving = semaphores_of(sizes, width, letters)
+        sending, receiving = semaphores_of(sizes, width // HALVES, letters)
         sends, receives = sends + sending, receives + receiving
     for letters in OWN_ORDERS:
         sending, receiving = semaphores_of(sizes, width, letters)
@@ -272,7 +281,7 @@
     heads = own // HEAD
     levels = len(bits_of(sizes, SUM_ORDER))
     units = 2 * (hidden // width) + 1
-    land_total = sum(landing_rows(sizes, width, UNIT_ORDERS[at]) for at in range(units))
+    land_total = sum(landing_rows(sizes, width // HALVES, letters) for letters in UNIT_ORDERS)
     own_land = max(landing_rows(sizes, width, order) for order in OWN_ORDERS)
     return dict(
         x_all=((seqs, length, width), LOW),
@@ -360,11 +369,16 @@
     def send_in(pair, offset, src, dst, peer):
         return send(src, dst, sems, pair[0] + offset, {"blk": peer}, pair[1] + offset)
 
-    def fetch(src, dst):
-        copy = pltpu.make_async_copy(src, dst, local.at[used["local"]])
-        used["local"] += 1
+    def fetch(src, dst, at=None):
+        copy = pltpu.make_async_copy(src, dst, local.at[take("local", 1) if at is None else at])
         copy.start()
         return copy
+
+    unit_store, own_store = take("local", 1), take("local", 1)
+    whole_stores = [
+        pltpu.make_async_copy(r.out, sums_out, local.at[unit_store]),
+        pltpu.make_async_copy(r.own_out, own_sums_out, local.at[own_store]),
+    ]
 
     loads_x = [
         fetch(x, x_all.at[:, place(me), :]),
@@ -545,17 +559,24 @@
 
     def launch_unit(unit):
         letters = UNIT_ORDERS[unit]
-        sending, receiving = semaphores_of(sizes, width, letters)
+        count = width // HALVES
+        sending, receiving = semaphores_of(sizes, count, letters)
         ats = take("send", sending), take("receive", receiving)
         land_at = place_of["land"]
-        place_of["land"] += landing_rows(sizes, width, letters)
+        place_of["land"] += landing_rows(sizes, count, letters)
         sent = []
         last.append(sent)
+
         def item():
-            yield from reduce_rows(sizes, work, r.land, r.out, sems, unit * width, width, land_at, *ats, letters, sent)
-            stores.append(fetch(r.out.at[cut(unit)], sums_out.at[cut(unit)]))
+            yield from reduce_rows(sizes, work, r.land, r.out, sems, unit * count, count, land_at, *ats, letters, sent)
+            part = pl.ds(unit * count, count)
+            fetch(r.out.at[part], sums_out.at[part], unit_store)
 
         launch(unit, item())
+
+    def launch_units(tile):
+        for half in range(HALVES):
+            launch_unit(tile * HALVES + half)
 
     def launch_own(kind):
         letters = OWN_ORDERS[kind]
@@ -570,9 +591,9 @@
             parts = r.own_work.at[kind], r.own_land.at[kind], slots.at[me]
             yield from reduce_rows(sizes, *parts, sems, 0, width, 0, *ats, letters, sent)
             yield from share_blocks(slots, sems, ats[0], blocks_at, me, sent)
-            stores.append(fetch(slots, own_sums_out.at[kind]))
-
-        launch(2 * tiles + 1 + kind, item())
+            fetch(slots, own_sums_out.at[kind], own_store)
+
+        launch(len(UNIT_ORDERS) + kind, item())
 
     def poll():
         at = place_of["poll"]
@@ -583,7 +604,7 @@
     cut = lambda tile: slice(tile * width, (tile + 1) * width)
     for tile in range(tiles):
         work[cut(tile), :] = dot_left_t(active[:, cut(tile)], grad_y[...]).astype(LOW)
-        launch_unit(tile)
+        launch_units(tile)
         poll()
 
     grad_z = r.grad_z
@@ -634,11 +655,11 @@
 
     poll()
     work[2 * hidden :, :] = dot_left_t(o_all[...].reshape(tokens, width), grad_t[...]).astype(LOW)
-    launch_unit(2 * tiles)
+    launch_units(2 * tiles)
     poll()
     for tile in range(tiles):
         work[cut(tiles + tile), :] = dot_left_t(normed_low[...], grad_z[:, cut(tile)]).astype(LOW)
-        launch_unit(tiles + tile)
+        launch_units(tiles + tile)
         poll()
 
     d_qkv, grad_s, dx_part = r.d_qkv, r.grad_s, r.dx_part
@@ -697,6 +718,7 @@
         pending.append(dx_far[-1])
 
     for seq in range(seqs):
+        poll()
         for copy in do_copies[seq]:
             copy.wait_recv()
         value_back(seq)
@@ -726,19 +748,20 @@
     steps[0, 0:1, lanes(me)] = sums[:, 0:own]
     steps[0, 1:2, lanes(me)] = sums[:, 2 * own :]
     sum_bits = bits_of(sizes, SUM_ORDER)
-    launch(2 * tiles + 4, reduce_whole(steps, r.vec_land, sems, take("send", 1), take("receive", len(sum_bits)), sum_bits))
+    launch(len(UNIT_ORDERS) + 3, reduce_whole(steps, r.vec_land, sems, take("send", 1), take("receive", len(sum_bits)), sum_bits))
     poll()
 
-    for seq in range(seqs):
-        dx_near[seq][0].wait_recv()
-        dx_far[seq].wait_recv()
-
-        summed = grad_b[seq * rows : (seq + 1) * rows, :] + dx_part[seq, place(me), :].astype(WIDE)
-        summed = summed + r.dx_near[seq, 0].astype(WIDE) + r.dx_far[seq].astype(WIDE)
-        r.dx[seq] = summed.astype(LOW)
-        poll()
-    stores.append(fetch(r.dx, dx_out))
-
+    def finish_input():
+        for seq in range(seqs):
+            yield
+            dx_near[seq][0].wait_recv()
+            dx_far[seq].wait_recv()
+            summed = grad_b[seq * rows : (seq + 1) * rows, :] + dx_part[seq, place(me), :].astype(WIDE)
+            summed = summed + r.dx_near[seq, 0].astype(WIDE) + r.dx_far[seq].astype(WIDE)
+            r.dx[seq] = summed.astype(LOW)
+        stores.append(fetch(r.dx, dx_out))
+
+    launch(len(UNIT_ORDERS) + 4, finish_input())
     for name in sum(POLLS[place_of["poll"] :], ()):
         advance(name)
     while running:
@@ -747,15 +770,15 @@
     vec_out[...] = steps[len(sum_bits)]
     for copy in sum(last, pending):
         copy.wait_send()
-    for copy in stores:
+    for copy in stores + whole_stores:
         copy.wait()
-    assert (used["send"], used["receive"]) == semaphore_counts(sizes, seqs, width) and used["local"] == LOCALS
+    assert (used["send"], used["receive"]) == semaphore_counts(sizes, seqs, width) and used["local"] == local.shape[0]
 
 
 def widen_kernel(blocks, hid, dx, sums, shared, vec, *refs):
     hid_out, dx_out, wq, wk, wv, wo, wu, wd = refs[:8]
     rows_out, bu = refs[8:16], refs[16]
-    low, shared_low, wide, shared_wide, hid_low, dx_low, flat_vec, sems = refs[17:]
+    low, shared_low, wide, shared_wide, hid_low, dx_low, vec_in, flat_vec, sems = refs[17:]
     width = wq.shape[0]
     own = width // blocks
     units = sums.shape[0] // width
@@ -769,37 +792,36 @@
         return made
 
     unit = lambda ref, at: ref.at[pl.ds(at * width, width)]
+    load_vec = copy(vec, vec_in)
+    shared_loads = [copy(shared.at[kind], shared_low.at[kind]) for kind in range(3)]
     loads = [copy(unit(sums, at), unit(low, at)) for at in range(units)]
-    shared_loads = [copy(shared.at[kind], shared_low.at[kind]) for kind in range(3)]
     token_loads = [copy(hid, hid_low), copy(dx, dx_low)]
     stores = []
-    count = len(rows_out)
-    for at in range(count + tiles):
-        flat_vec[at * width : (at + 1) * width] = vec[at, :]
-    for at, row in enumerate(rows_out):
-        stores.append(copy(flat_vec.at[pl.ds(at * width, width)], row))
-    stores.append(copy(flat_vec.at[pl.ds(count * width, tiles * width)], bu))
+    for kind, target in enumerate((wv, wq, wk)):
+        shared_loads[kind].wait()
+        for block in range(blocks):
+            shared_wide[kind, :, block * own : (block + 1) * own] = shared_low[kind, block].astype(WIDE)
+        stores.append(copy(shared_wide.at[kind], target))
     targets = (
         [unit(wd, at) for at in range(tiles)] + [wu.at[:, pl.ds(at * width, width)] for at in range(tiles)] + [wo]
     )
     for at in range(units):
         loads[at].wait()
-
-        def body(step, carry):
-            part = span(at * width + step * 256, 256)
-            wide[part, :] = low[part, :].astype(WIDE)
-            return carry
-
-        lax.fori_loop(0, width // 256, body, 0)
+        part = slice(at * width, (at + 1) * width)
+        wide[part, :] = low[part, :].astype(WIDE)
         stores.append(copy(unit(wide, at), targets[at]))
-    for load in token_loads:
-        load.wait()
-    stores += [copy(hid_low, hid_out), copy(dx_low, dx_out)]
-    for kind, target in enumerate((wv, wq, wk)):
-        shared_loads[kind].wait()
-        for block in range(blocks):
-            shared_wide[kind, :, block * own : (block + 1) * own] = shared_low[kind, block].astype(WIDE)
-        stores.append(copy(shared_wide.at[kind], target))
+        if at == 0:
+            load_vec.wait()
+            count = len(rows_out)
+            for index in range(count + tiles):
+                flat_vec[index * width : (index + 1) * width] = vec_in[index, :]
+            for index, row in enumerate(rows_out):
+                stores.append(copy(flat_vec.at[pl.ds(index * width, width)], row))
+            stores.append(copy(flat_vec.at[pl.ds(count * width, tiles * width)], bu))
+        if at == units // 2:
+            for load in token_loads:
+                load.wait()
+            stores += [copy(hid_low, hid_out), copy(dx_low, dx_out)]
     for made in stores:
         made.wait()
 
@@ -851,7 +873,7 @@
         scratch_shapes=[pltpu.VMEM(shape, kind) for shape, kind in scratch.values()]
         + [
             *(pltpu.SemaphoreType.DMA((count,)) for count in semaphore_counts(sizes, seqs, width)),
-            pltpu.SemaphoreType.DMA((LOCALS,)),
+            pltpu.SemaphoreType.DMA((22,)),
         ],
         compiler_params=pltpu.CompilerParams(
             collective_id=0, has_side_effects=True, vmem_limit_bytes=60 * 1024 * 1024
@@ -894,7 +916,7 @@
         )
         + (row,) * 8
         + (jax.ShapeDtypeStruct((hidden,), WIDE),),
-        in_specs=[anywhere] * 4 + [inside],
+        in_specs=[anywhere] * 5,
         out_specs=(anywhere,) * 17,
         scratch_shapes=[
             pltpu.VMEM(units, LOW),
@@ -903,8 +925,9 @@
             pltpu.VMEM((3, width, width), WIDE),
             pltpu.VMEM(hidden_input.shape, LOW),
             pltpu.VMEM(hidden_input.shape, LOW),
+            pltpu.VMEM((VECTORS, width), WIDE),
             pltpu.VMEM((VECTORS * width,), WIDE),
-            pltpu.SemaphoreType.DMA((2 * units[0] // width + 19,)),
+            pltpu.SemaphoreType.DMA((2 * units[0] // width + 20,)),
         ],
         compiler_params=pltpu.CompilerParams(vmem_limit_bytes=60 * 1024 * 1024),
     )(hid, dx, sums, own_sums, vec_sums)

time: 96.9 us -> 92.7 us (0.957)
  Pallas kernels: 94.8 us -> 90.6 us
    pallas_call x1, Pallas kernels: 86.4 us -> 82.8 us  [on_device(): pl.pallas_call(functools.partial(layer_kernel, sizes, tuple(scratch)), ou...]
where the time goes in v6:
time: 92.7 us; the launch traced here: 91.4 us
  Pallas kernels  90.6 us (98%)
    pallas_call x1, Pallas kernels, on_device(): pl.pallas_call(functools.partial(layer_kernel, sizes, tuple(scratch)), ou...  82.8 us
    pallas_call x1, Pallas kernels, on_device(): pl.pallas_call(functools.partial(widen_kernel, blocks), out_shape=(flat,...  7.84 us

profile of v6, /device:TPU:5, one launch (start us, length us, event | category | flops | bytes accessed | tf_op | source)
XLA Modules:
  0.0 91.4 jit_solution(2311674730017779886)
XLA Ops:
  0.7 82.8 %shard_map.314 = (bf16[3,128,512]{2,1,0:T(8,128)(2,1)}, bf16[3,128,512]{2,1,0:T(8,128)(2,1)}, bf16[4608,512]{1,0:T(8,128)(2,1)}, bf16[3,4,512,128]{3,2,1,0:T(8,128)(2,1)}, f32[16,512]{1,0:T(8,128)}) custom-call(bf16[3,128,512]{2,1,0:T(8,128)(2,1)} %refs_0_.1, s32[3]{0:T(128)} %refs_1_.1, s32[3,128]{1,0:T(4,128)} %refs_2_.1, bf16[512,512]{1,0:T(8,128)(2,1)} %refs_3_.1, ...), custom_call_target="tpu_custom_call" | custom-call | tf_op jit(solution)/shard_map/pallas_call | solution.py:862
  83.4 7.8 %shard_map.315 = (bf16[3,128,512]{2,1,0:T(8,128)(2,1)}, bf16[3,128,512]{2,1,0:T(8,128)(2,1)}, f32[512,512]{1,0:T(8,128)}, f32[512,512]{1,0:T(8,128)}, f32[512,51...) custom-call(bf16[3,128,512]{2,1,0:T(8,128)(2,1)} %get-tuple-element., ...), custom_call_target="tpu_custom_call" | custom-call | tf_op jit(solution)/shard_map/pallas_call | solution.py:905

commit v7 on v6

--- a/solution.py
+++ b/solution.py
@@ -17,7 +17,7 @@
 VECTORS = 16
 HALVES = 2
 
-UNIT_ORDERS = ("cxzy", "caxby", "cyxab", "cabyx", "cayxb", "cxaby", "cxyab", "caxyb", "cyxab", "caxyb", "caxyb", "cyxab", "cxayb", "cyaxb", "cxayb", "cxyab", "cxyab", "caxyb")
+UNIT_ORDERS = ("caxyb", "cxzy", "cyxab", "cyxab", "cxyab", "cayxb", "cabyx", "cxaby", "cxyab", "cabxy", "cxaby", "cabxy", "cxayb", "cxyab", "caxyb", "cyxab", "cxyab", "cyaxb")
 OWN_ORDERS = ("xab", "xab", "xab")
 SUM_ORDER = "cxyab"
 POLLS = (
@@ -25,37 +25,37 @@
     (),
     (),
     (),
-    (),
     (0,),
     (1,),
     (2,),
-    (3, 4, 5,),
-    (6, 7,),
-    (),
-    (),
-    (),
-    (),
-    (),
-    (),
-    (16, 0, 17, 1, 8, 9, 2, 10, 11, 12, 5, 13, 3, 14, 15,),
-    (),
-    (6, 4,),
-    (),
-    (16, 7,),
-    (1,),
+    (3, 4,),
+    (5, 6, 7,),
+    (),
+    (),
+    (),
+    (),
+    (),
+    (),
+    (0, 16,),
+    (1, 17, 8, 2, 9, 10, 11, 12, 5, 4, 13, 14, 3, 15, 6, 7,),
+    (0,),
+    (),
+    (1, 16,),
+    (9,),
+    (8,),
+    (11,),
     (2,),
-    (0,),
-    (8,),
-    (17, 12,),
-    (),
-    (11,),
-    (9, 14,),
-    (13,),
-    (10, 15, 6,),
-    (5, 7,),
-    (18, 4, 16, 0, 3, 2, 1,),
-    (12, 8, 14, 17, 15, 7, 13, 11,),
-    (6, 9, 5, 21, 18, 16, 19, 22, 0, 3, 20, 8, 2, 1, 15, 10, 4, 11, 7, 13, 6, 21, 18, 22, 19, 16, 0, 20, 3, 2, 8, 0, 1, 15, 22, 12, 4, 14, 6, 17, 11, 9, 18, 5, 13, 2, 10, 7, 16, 1, 21, 19, 3, 4, 8, 15, 6, 20, 11, 12, 18, 13, 2, 14, 7, 16, 17, 8, 2, 4, 9, 1, 15, 5, 12, 21, 6, 10, 1, 19, 11, 6, 3, 20, 16, 18, 13, 14, 17, 16, 15, 18, 7, 8, 15, 19, 9, 7, 10, 4, 8, 5, 20, 4, 11, 12, 17, 21, 11, 13, 9, 3, 10, 13, 14, 3, 5, 19, 17, 5, 12, 19, 9, 17, 12, 14, 9, 20, 10, 14, 20, 10,),
+    (17,),
+    (5, 14,),
+    (10, 4,),
+    (6,),
+    (7, 12,),
+    (15, 0, 9, 1,),
+    (13, 2, 11, 16,),
+    (3, 17, 8,),
+    (18, 6, 10, 4, 5,),
+    (19, 7, 12, 14, 0, 13,),
+    (16, 1, 3, 8, 2, 21, 20, 18, 15, 9, 10, 11, 22, 4, 17, 5, 6, 19, 13, 16, 1, 3, 2, 21, 8, 22, 20, 1, 5, 15, 18, 4, 17, 22, 2, 7, 16, 19, 12, 3, 14, 8, 13, 0, 9, 10, 11, 17, 20, 6, 18, 15, 21, 19, 5, 7, 3, 4, 12, 0, 13, 9, 14, 11, 17, 2, 10, 20, 16, 18, 2, 8, 15, 6, 19, 21, 3, 12, 4, 5, 13, 3, 14, 7, 4, 20, 5, 17, 0, 16, 17, 9, 0, 16, 11, 8, 10, 18, 15, 8, 6, 18, 13, 21, 14, 6, 12, 19, 13, 7, 9, 19, 7, 10, 11, 9, 20, 10, 12, 14, 11, 20, 15, 12, 14, 15,),
 )
 
 
@@ -294,6 +294,7 @@
         vec_low=((VECTORS * width,), LOW),
         vec=((VECTORS, width), WIDE),
         flags=((blocks, 8, rows), WIDE),
+        mask=((seqs, rows), jnp.int32),
         qkv=((seqs, length, 3 * own), LOW),
         probs=((seqs * heads, length, length), LOW),
         o_wide=((seqs, length, own), WIDE),
@@ -335,7 +336,7 @@
     x, lengths, mask, wq, wk, wv, wo, wu, wd, cotangent = refs[:10]
     vectors_in = refs[10:19]
     hid_out, dx_out, sums_out, own_sums_out, vec_out = refs[19:24]
-    r = types.SimpleNamespace(**dict(zip(names, refs[24:-3], strict=True)))
+    r = types.SimpleNamespace(**dict(zip(names, refs[24:-4], strict=True)), lengths=refs[-4])
     sems = refs[-3:-1]
     local = refs[-1]
     x_all, qkv, vec, steps = r.x_all, r.qkv, r.vec, r.steps
@@ -380,6 +381,14 @@
         pltpu.make_async_copy(r.own_out, own_sums_out, local.at[own_store]),
     ]
 
+    barrier = pltpu.get_barrier_semaphore()
+    greeted = [peer for letter in "zx" for stage in stages_of(sizes)[letter] for _, peer in digit_of(stage)[1]]
+    greeted += [{"blk": peer} for peer in peers]
+    for peer in greeted:
+        pl.semaphore_signal(barrier, inc=1, device_id=peer, device_id_type=MESH)
+
+    load_mask = fetch(mask, r.mask)
+    load_lengths = fetch(lengths, r.lengths)
     loads_x = [
         fetch(x, x_all.at[:, place(me), :]),
         fetch(x, r.x_own),
@@ -399,20 +408,16 @@
     load_down = fetch(wd, r.w_down)
     load_cot = fetch(cotangent, r.cot)
 
+    load_mask.wait()
+    load_lengths.wait()
     positions = me * rows + lax.broadcasted_iota(jnp.int32, (1, rows), 1)
     flag_rows = []
     for seq in range(seqs):
-        good = (mask[seq : seq + 1, :] == 1) & (positions < lengths[seq])
+        good = (r.mask[seq : seq + 1, :] == 1) & (positions < r.lengths[seq])
         flag_rows.append(jnp.where(good, 0.0, -1000000000.0).astype(WIDE))
     flag_rows.append(jnp.zeros((8 - seqs, rows), WIDE))
     r.flags[me] = jnp.concatenate(flag_rows, axis=0)
 
-    barrier = pltpu.get_barrier_semaphore()
-    greeted = [{"blk": peer} for peer in peers] + [
-        peer for letter in "xz" for stage in stages_of(sizes)[letter] for _, peer in digit_of(stage)[1]
-    ]
-    for peer in greeted:
-        pl.semaphore_signal(barrier, inc=1, device_id=peer, device_id_type=MESH)
     pl.semaphore_wait(barrier, len(greeted))
 
     at_far, at_near, at_on, at_flag = slot(seqs), slot(seqs), slot(seqs), slot(len(peers))
@@ -420,11 +425,13 @@
         send_in(at_flag, index, r.flags.at[me], r.flags.at[me], peer)
         for index, peer in enumerate(peers)
     ]
+    for copy in loads_x:
+        copy.wait()
     x_far, x_near, x_on = [], [], []
     for seq in range(seqs):
         target = x_all.at[seq, place(me), :]
-        x_far.append(send_in(at_far, seq, x.at[seq], target, far))
-        x_near.append(send_in(at_near, seq, x.at[seq], target, near))
+        x_far.append(send_in(at_far, seq, r.x_own.at[seq], target, far))
+        x_near.append(send_in(at_near, seq, r.x_own.at[seq], target, near))
     pending += flag_copies
 
     def forward_x(seq):
@@ -474,8 +481,6 @@
         o_all[seq, :, lanes(me)] = o_send[seq, place(me), :]
 
     for copy in loads_w:
-        copy.wait()
-    for copy in loads_x:
         copy.wait()
     for copy in flag_copies:
         copy.wait_recv()
@@ -767,7 +772,7 @@
     while running:
         for name in list(running):
             advance(name)
-    vec_out[...] = steps[len(sum_bits)]
+    stores.append(fetch(steps.at[len(sum_bits)], vec_out))
     for copy in sum(last, pending):
         copy.wait_send()
     for copy in stores + whole_stores:
@@ -854,8 +859,6 @@
     own = width // blocks
     scratch = layout_of(sizes, seqs, rows, width, hidden)
     anywhere = pl.BlockSpec(memory_space=pl.ANY)
-    inside = pl.BlockSpec(memory_space=pltpu.VMEM)
-    scalars = pl.BlockSpec(memory_space=pltpu.SMEM)
     scratch_shape = types.SimpleNamespace(**{name: shape for name, (shape, _) in scratch.items()})
     units = scratch_shape.work
     shared = (3, blocks, width, own)
@@ -868,12 +871,13 @@
             jax.ShapeDtypeStruct(shared, LOW),
             jax.ShapeDtypeStruct((VECTORS, width), WIDE),
         ),
-        in_specs=[anywhere, scalars, inside] + [anywhere] * 16,
-        out_specs=(anywhere,) * 4 + (inside,),
+        in_specs=[anywhere, anywhere] + [anywhere] * 17,
+        out_specs=(anywhere,) * 5,
         scratch_shapes=[pltpu.VMEM(shape, kind) for shape, kind in scratch.values()]
         + [
+            pltpu.SMEM((seqs,), jnp.int32),
             *(pltpu.SemaphoreType.DMA((count,)) for count in semaphore_counts(sizes, seqs, width)),
-            pltpu.SemaphoreType.DMA((22,)),
+            pltpu.SemaphoreType.DMA((25,)),
         ],
         compiler_params=pltpu.CompilerParams(
             collective_id=0, has_side_effects=True, vmem_limit_bytes=60 * 1024 * 1024

time: 92.7 us -> 90.5 us (0.976)
  Pallas kernels: 90.6 us -> 87.9 us
    pallas_call x1, Pallas kernels: 82.8 us -> 80.1 us  [on_device(): pl.pallas_call(functools.partial(layer_kernel, sizes, tuple(scratch)), ou...]
where the time goes in v7:
time: 90.5 us; the launch traced here: 88.8 us
  Pallas kernels  87.9 us (97%)
    pallas_call x1, Pallas kernels, on_device(): pl.pallas_call(functools.partial(layer_kernel, sizes, tuple(scratch)), ou...  80.1 us
    pallas_call x1, Pallas kernels, on_device(): pl.pallas_call(functools.partial(widen_kernel, blocks), out_shape=(flat,...  7.84 us

profile of v7, /device:TPU:5, one launch (start us, length us, event | category | flops | bytes accessed | tf_op | source)
XLA Modules:
  0.0 88.8 jit_solution(10942407843409991490)
XLA Ops:
  0.7 80.1 %shard_map.314 = (bf16[3,128,512]{2,1,0:T(8,128)(2,1)}, bf16[3,128,512]{2,1,0:T(8,128)(2,1)}, bf16[4608,512]{1,0:T(8,128)(2,1)}, bf16[3,4,512,128]{3,2,1,0:T(8,128)(2,1)}, f32[16,512]{1,0:T(8,128)}) custom-call(bf16[3,128,512]{2,1,0:T(8,128)(2,1)} %refs_0_.1, s32[3]{0:T(128)} %refs_1_.1, s32[3,128]{1,0:T(4,128)} %refs_2_.1, bf16[512,512]{1,0:T(8,128)(2,1)} %refs_3_.1, ...), custom_call_target="tpu_custom_call" | custom-call | tf_op jit(solution)/shard_map/pallas_call | solution.py:865
  80.8 7.8 %shard_map.315 = (bf16[3,128,512]{2,1,0:T(8,128)(2,1)}, bf16[3,128,512]{2,1,0:T(8,128)(2,1)}, f32[512,512]{1,0:T(8,128)}, f32[512,512]{1,0:T(8,128)}, f32[512,51...) custom-call(bf16[3,128,512]{2,1,0:T(8,128)(2,1)} %get-tuple-element., ...), custom_call_target="tpu_custom_call" | custom-call | tf_op jit(solution)/shard_map/pallas_call | solution.py:909

commit v8 on v7

--- a/solution.py
+++ b/solution.py
@@ -17,7 +17,7 @@
 VECTORS = 16
 HALVES = 2
 
-UNIT_ORDERS = ("caxyb", "cxzy", "cyxab", "cyxab", "cxyab", "cayxb", "cabyx", "cxaby", "cxyab", "cabxy", "cxaby", "cabxy", "cxayb", "cxyab", "caxyb", "cyxab", "cxyab", "cyaxb")
+UNIT_ORDERS = ("cyaxb", "cxyab", "caxyb", "cyxab", "caxyb", "cxyab", "cxaby", "cayxb", "cyaxb", "cxaby", "caxby", "cabxy", "cyxab", "cxyab", "cxayb", "cabxy", "cxyab", "cyaxb")
 OWN_ORDERS = ("xab", "xab", "xab")
 SUM_ORDER = "cxyab"
 POLLS = (
@@ -29,33 +29,33 @@
     (1,),
     (2,),
     (3, 4,),
-    (5, 6, 7,),
-    (),
+    (5, 6,),
+    (7,),
     (),
     (),
     (),
     (),
     (),
     (0, 16,),
-    (1, 17, 8, 2, 9, 10, 11, 12, 5, 4, 13, 14, 3, 15, 6, 7,),
-    (0,),
+    (1, 17, 8, 2, 9, 10, 11, 3, 12, 5, 13, 14, 4, 15,),
+    (6,),
+    (7, 0,),
+    (16,),
+    (2, 10,),
     (),
-    (1, 16,),
-    (9,),
-    (8,),
+    (1, 9,),
     (11,),
-    (2,),
+    (3,),
     (17,),
-    (5, 14,),
-    (10, 4,),
-    (6,),
-    (7, 12,),
-    (15, 0, 9, 1,),
-    (13, 2, 11, 16,),
-    (3, 17, 8,),
-    (18, 6, 10, 4, 5,),
-    (19, 7, 12, 14, 0, 13,),
-    (16, 1, 3, 8, 2, 21, 20, 18, 15, 9, 10, 11, 22, 4, 17, 5, 6, 19, 13, 16, 1, 3, 2, 21, 8, 22, 20, 1, 5, 15, 18, 4, 17, 22, 2, 7, 16, 19, 12, 3, 14, 8, 13, 0, 9, 10, 11, 17, 20, 6, 18, 15, 21, 19, 5, 7, 3, 4, 12, 0, 13, 9, 14, 11, 17, 2, 10, 20, 16, 18, 2, 8, 15, 6, 19, 21, 3, 12, 4, 5, 13, 3, 14, 7, 4, 20, 5, 17, 0, 16, 17, 9, 0, 16, 11, 8, 10, 18, 15, 8, 6, 18, 13, 21, 14, 6, 12, 19, 13, 7, 9, 19, 7, 10, 11, 9, 20, 10, 12, 14, 11, 20, 15, 12, 14, 15,),
+    (15,),
+    (13,),
+    (6, 8,),
+    (1, 14, 9,),
+    (12, 4,),
+    (0, 5, 11, 3,),
+    (18, 10, 7, 17, 16, 15, 2,),
+    (19, 6, 13, 8, 4, 1, 14, 9,),
+    (0, 5, 20, 3, 21, 12, 18, 11, 7, 10, 16, 17, 15, 2, 22, 8, 19, 0, 13, 4, 1, 21, 5, 20, 22, 3, 12, 18, 7, 16, 17, 22, 8, 6, 14, 3, 9, 0, 11, 19, 10, 5, 15, 7, 13, 2, 4, 17, 8, 1, 18, 20, 16, 21, 12, 11, 6, 15, 3, 19, 14, 2, 13, 9, 4, 0, 3, 17, 10, 5, 8, 1, 7, 0, 20, 16, 21, 14, 18, 1, 12, 13, 11, 19, 6, 17, 10, 15, 8, 5, 17, 2, 9, 20, 8, 5, 2, 4, 18, 16, 12, 7, 4, 18, 16, 21, 13, 14, 7, 19, 6, 13, 11, 19, 9, 6, 10, 11, 20, 9, 14, 15, 10, 12, 20, 14, 15, 12,),
 )
 
 
@@ -382,7 +382,10 @@
     ]
 
     barrier = pltpu.get_barrier_semaphore()
-    greeted = [peer for letter in "zx" for stage in stages_of(sizes)[letter] for _, peer in digit_of(stage)[1]]
+    far_letters = "z" if "z" in set("".join(UNIT_ORDERS + OWN_ORDERS)) else "ba"
+    greeted = [
+        peer for letter in far_letters + "x" for stage in stages_of(sizes)[letter] for _, peer in digit_of(stage)[1]
+    ]
     greeted += [{"blk": peer} for peer in peers]
     for peer in greeted:
         pl.semaphore_signal(barrier, inc=1, device_id=peer, device_id_type=MESH)
@@ -456,29 +459,29 @@
     def project(seq):
         qkv[seq] = (dot(x_all[seq], r.w_qkv[...]) + bias_qkv).astype(LOW)
 
-    column = lax.broadcasted_iota(jnp.int32, (length, length), 1)
-    row = lax.broadcasted_iota(jnp.int32, (length, length), 0)
-
-    def attend(seq):
+    def attend(seq, start, count, receivers):
+        part = span(start, count, count)
         keys = qkv[seq, :, own : 2 * own]
         values = qkv[seq, :, 2 * own :]
         key_bias = jnp.concatenate([r.flags[block, seq : seq + 1, :] for block in range(blocks)], axis=1)
+        column = lax.broadcasted_iota(jnp.int32, (count, length), 1)
+        row = lax.broadcasted_iota(jnp.int32, (count, length), 0) + start
         bias = jnp.where(column == row, 0.0, key_bias)
-        query = qkv[seq, :, 0:own].astype(WIDE) * scale
+        query = qkv[seq, part, 0:own].astype(WIDE) * scale
         joined = None
         for head in range(heads):
             scores = dot_right_t(only(query, head).astype(LOW), keys) + bias
             raised = jnp.exp(scores - jnp.max(scores, axis=-1, keepdims=True))
             probs = (raised / jnp.sum(raised, axis=-1, keepdims=True)).astype(LOW)
-            r.probs[seq * heads + head] = probs
+            r.probs[seq * heads + head, part, :] = probs
             result = dot(probs, values)
             joined = result if joined is None else jnp.where(of_head[head], result, joined)
-        r.o_wide[seq] = joined
-        o_send[seq] = joined.astype(LOW)
-        for index, peer in enumerate(peers):
-            part = o_send.at[seq, place(peer), :]
-            o_copies.append(send_in(at_o, seq * len(peers) + index, part, o_all.at[seq, :, lanes(me)], peer))
-        o_all[seq, :, lanes(me)] = o_send[seq, place(me), :]
+        r.o_wide[seq, part, :] = joined
+        o_send[seq, part, :] = joined.astype(LOW)
+        for index in receivers:
+            peer = peers[index]
+            given = o_send.at[seq, place(peer), :]
+            o_copies.append(send_in(at_o, seq * len(peers) + index, given, o_all.at[seq, :, lanes(me)], peer))
 
     for copy in loads_w:
         copy.wait()
@@ -491,7 +494,13 @@
         project(seq)
         if seq + 1 < seqs:
             forward_x(seq + 1)
-        attend(seq)
+        if seq + 1 < seqs:
+            attend(seq, 0, length, (0, 1, 2))
+        else:
+            half = 2 * rows
+            attend(seq, lax.div(far, 2) * half, half, (1, 2))
+            attend(seq, lax.div(me, 2) * half, half, (0,))
+        o_all[seq, :, lanes(me)] = o_send[seq, place(me), :]
 
     total, scaled, inverse = r.total, r.scaled, r.inverse
     normed, normed_low = r.normed, r.normed_low

time: 90.5 us -> 90.1 us (level)
  no operation moved by 1% of the time
where the time goes in v8:
time: 90.1 us; the launch traced here: 89.2 us
  Pallas kernels  88.4 us (98%)
    pallas_call x1, Pallas kernels, on_device(): pl.pallas_call(functools.partial(layer_kernel, sizes, tuple(scratch)), ou...  80.5 us
    pallas_call x1, Pallas kernels, on_device(): pl.pallas_call(functools.partial(widen_kernel, blocks), out_shape=(flat,...  7.84 us

profile of v8, /device:TPU:5, one launch (start us, length us, event | category | flops | bytes accessed | tf_op | source)
XLA Modules:
  0.0 89.2 jit_solution(5061459546844907118)
XLA Ops:
  0.7 80.5 %shard_map.314 = (bf16[3,128,512]{2,1,0:T(8,128)(2,1)}, bf16[3,128,512]{2,1,0:T(8,128)(2,1)}, bf16[4608,512]{1,0:T(8,128)(2,1)}, bf16[3,4,512,128]{3,2,1,0:T(8,128)(2,1)}, f32[16,512]{1,0:T(8,128)}) custom-call(bf16[3,128,512]{2,1,0:T(8,128)(2,1)} %refs_0_.1, s32[3]{0:T(128)} %refs_1_.1, s32[3,128]{1,0:T(4,128)} %refs_2_.1, bf16[512,512]{1,0:T(8,128)(2,1)} %refs_3_.1, ...), custom_call_target="tpu_custom_call" | custom-call | tf_op jit(solution)/shard_map/pallas_call | solution.py:874
  81.2 7.8 %shard_map.315 = (bf16[3,128,512]{2,1,0:T(8,128)(2,1)}, bf16[3,128,512]{2,1,0:T(8,128)(2,1)}, f32[512,512]{1,0:T(8,128)}, f32[512,512]{1,0:T(8,128)}, f32[512,51...) custom-call(bf16[3,128,512]{2,1,0:T(8,128)(2,1)} %get-tuple-element., ...), custom_call_target="tpu_custom_call" | custom-call | tf_op jit(solution)/shard_map/pallas_call | solution.py:918

commit v9 on v7

--- a/solution.py
+++ b/solution.py
@@ -456,29 +456,29 @@
     def project(seq):
         qkv[seq] = (dot(x_all[seq], r.w_qkv[...]) + bias_qkv).astype(LOW)
 
-    column = lax.broadcasted_iota(jnp.int32, (length, length), 1)
-    row = lax.broadcasted_iota(jnp.int32, (length, length), 0)
-
-    def attend(seq):
+    def attend(seq, start, count, receivers):
+        part = span(start, count, count)
         keys = qkv[seq, :, own : 2 * own]
         values = qkv[seq, :, 2 * own :]
         key_bias = jnp.concatenate([r.flags[block, seq : seq + 1, :] for block in range(blocks)], axis=1)
+        column = lax.broadcasted_iota(jnp.int32, (count, length), 1)
+        row = lax.broadcasted_iota(jnp.int32, (count, length), 0) + start
         bias = jnp.where(column == row, 0.0, key_bias)
-        query = qkv[seq, :, 0:own].astype(WIDE) * scale
+        query = qkv[seq, part, 0:own].astype(WIDE) * scale
         joined = None
         for head in range(heads):
             scores = dot_right_t(only(query, head).astype(LOW), keys) + bias
             raised = jnp.exp(scores - jnp.max(scores, axis=-1, keepdims=True))
             probs = (raised / jnp.sum(raised, axis=-1, keepdims=True)).astype(LOW)
-            r.probs[seq * heads + head] = probs
+            r.probs[seq * heads + head, part, :] = probs
             result = dot(probs, values)
             joined = result if joined is None else jnp.where(of_head[head], result, joined)
-        r.o_wide[seq] = joined
-        o_send[seq] = joined.astype(LOW)
-        for index, peer in enumerate(peers):
-            part = o_send.at[seq, place(peer), :]
-            o_copies.append(send_in(at_o, seq * len(peers) + index, part, o_all.at[seq, :, lanes(me)], peer))
-        o_all[seq, :, lanes(me)] = o_send[seq, place(me), :]
+        r.o_wide[seq, part, :] = joined
+        o_send[seq, part, :] = joined.astype(LOW)
+        for index in receivers:
+            peer = peers[index]
+            given = o_send.at[seq, place(peer), :]
+            o_copies.append(send_in(at_o, seq * len(peers) + index, given, o_all.at[seq, :, lanes(me)], peer))
 
     for copy in loads_w:
         copy.wait()
@@ -491,7 +491,13 @@
         project(seq)
         if seq + 1 < seqs:
             forward_x(seq + 1)
-        attend(seq)
+        if seq + 1 < seqs:
+            attend(seq, 0, length, (0, 1, 2))
+        else:
+            half = 2 * rows
+            attend(seq, lax.div(far, 2) * half, half, (1, 2))
+            attend(seq, lax.div(me, 2) * half, half, (0,))
+        o_all[seq, :, lanes(me)] = o_send[seq, place(me), :]
 
     total, scaled, inverse = r.total, r.scaled, r.inverse
     normed, normed_low = r.normed, r.normed_low

time: 90.5 us -> 90.4 us (level)
  no operation moved by 1% of the time
where the time goes in v9:
time: 90.4 us; the launch traced here: 88.6 us
  Pallas kernels  87.8 us (97%)
    pallas_call x1, Pallas kernels, on_device(): pl.pallas_call(functools.partial(layer_kernel, sizes, tuple(scratch)), ou...  79.9 us
    pallas_call x1, Pallas kernels, on_device(): pl.pallas_call(functools.partial(widen_kernel, blocks), out_shape=(flat,...  7.84 us

profile of v9, /device:TPU:5, one launch (start us, length us, event | category | flops | bytes accessed | tf_op | source)
XLA Modules:
  0.0 88.6 jit_solution(7168413931503199651)
XLA Ops:
  0.7 79.9 %shard_map.314 = (bf16[3,128,512]{2,1,0:T(8,128)(2,1)}, bf16[3,128,512]{2,1,0:T(8,128)(2,1)}, bf16[4608,512]{1,0:T(8,128)(2,1)}, bf16[3,4,512,128]{3,2,1,0:T(8,128)(2,1)}, f32[16,512]{1,0:T(8,128)}) custom-call(bf16[3,128,512]{2,1,0:T(8,128)(2,1)} %refs_0_.1, s32[3]{0:T(128)} %refs_1_.1, s32[3,128]{1,0:T(4,128)} %refs_2_.1, bf16[512,512]{1,0:T(8,128)(2,1)} %refs_3_.1, ...), custom_call_target="tpu_custom_call" | custom-call | tf_op jit(solution)/shard_map/pallas_call | solution.py:871
  80.6 7.8 %shard_map.315 = (bf16[3,128,512]{2,1,0:T(8,128)(2,1)}, bf16[3,128,512]{2,1,0:T(8,128)(2,1)}, f32[512,512]{1,0:T(8,128)}, f32[512,512]{1,0:T(8,128)}, f32[512,51...) custom-call(bf16[3,128,512]{2,1,0:T(8,128)(2,1)} %get-tuple-element., ...), custom_call_target="tpu_custom_call" | custom-call | tf_op jit(solution)/shard_map/pallas_call | solution.py:915
